TPU v7x, 128 devices: a whole 4x4x4 slice. The times are simulated.
128 devices in a mesh: dp: 2 (over core), gx: 8 (over y, z_lo), gy: 8 (over x, z_hi).
Axes of the slice: x: 4, y: 4, z: 4 (z_hi: 2, z_lo: 2; z = z_hi * 2 + z_lo), core: 2. Of those that a mesh axis runs over, the one named last changes fastest.
Arguments:
- state_now: bfloat16 [2, 8, 32, 192, 128], P('dp', None, 'gx', 'gy'), may hold values from -6 to 6
- enc_pre: bfloat16 [2, 32, 32, 192, 128], P('dp', None, 'gx', 'gy'), may hold values from -8 to 8
- mid_pre: bfloat16 [2, 64, 16, 96, 64], P('dp', None, 'gx', 'gy'), may hold values from -8 to 8
- dec_pre: bfloat16 [2, 32, 32, 192, 128], P('dp', None, 'gx', 'gy'), may hold values from -8 to 8
- cotangent: bfloat16 [2, 8, 32, 192, 128], P('dp', None, 'gx', 'gy'), may hold values from -6 to 6
- enc_kernel: bfloat16 [32, 8, 3, 3, 3], replicated, may hold values from -0.4375 to 0.4375
- mid_kernel: bfloat16 [64, 32, 3, 3, 3], replicated, may hold values from -0.21875 to 0.21875
- dec_kernel: bfloat16 [32, 96, 3, 3, 3], replicated, may hold values from -0.125 to 0.125
- out_kernel: bfloat16 [8, 32], replicated, may hold values from -1 to 1
Outputs:
- state_grad: bfloat16 [2, 8, 32, 192, 128], P('dp', None, 'gx', 'gy')
- enc_grad: float32 [32, 8, 3, 3, 3], replicated
- mid_grad: float32 [64, 32, 3, 3, 3], replicated
- dec_grad: float32 [32, 96, 3, 3, 3], replicated
- out_grad: float32 [8, 32], replicated
All inputs are finite; a program needn't handle non-finite values.
Results may differ from a plain program's by a relative error of at most 0.0069.
Values may be sent and summed in bfloat16 or wider, within the bound.
No kernel may reach another device: no remote copies, remote signals or barrier semaphores. Data moves between devices by JAX's collectives and lax.ppermute only.
A program may use at most 128 MiB of HBM per device.

v0:
```python
import math

import jax
import jax.numpy as jnp
from jax import lax
from jax.sharding import PartitionSpec as P


def padded(cells, sides, width):
    for axis, dim in sides:
        count = lax.axis_size(axis)
        ends = count - 1
        head = lax.slice_in_dim(cells, 0, width, axis=dim)
        tail = lax.slice_in_dim(cells, cells.shape[dim] - width, cells.shape[dim], axis=dim)
        cells = jnp.concatenate(
            [
                lax.ppermute(tail, axis, [(i, (i + 1) % count) for i in range(ends)]),
                cells,
                lax.ppermute(head, axis, [((i + 1) % count, i) for i in range(ends)]),
            ],
            axis=dim,
        )
    return cells


def apply_conv(values, kernel, pads):
    return lax.conv_general_dilated(
        values,
        kernel,
        (1, 1, 1),
        pads,
        dimension_numbers=("NCDHW", "OIDHW", "NCDHW"),
        preferred_element_type=jnp.float32,
    )


def flip_kernel(kernel):
    return jnp.transpose(jnp.flip(kernel, (2, 3, 4)), (1, 0, 2, 3, 4))


def silu_slope(values):
    sig = jax.nn.sigmoid(values)
    return sig * (1.0 + values * (1.0 - sig))


def block_sum(values):
    shape = values.shape
    split = values.reshape(shape[0], shape[1], shape[2] // 2, 2, shape[3] // 2, 2, shape[4] // 2, 2)
    return jnp.sum(split, axis=(3, 5, 7))


def upsample(values):
    return jnp.repeat(jnp.repeat(jnp.repeat(values, 2, axis=2), 2, axis=3), 2, axis=4)


def depth_padded(values):
    return jnp.pad(values, ((0, 0), (0, 0), (0, 0), (0, 0), (1, 1)))


def values_rim_grad(values_ext, delta):
    wide = depth_padded(values_ext)
    size_x, size_y, size_z = (delta.shape[2], delta.shape[3], delta.shape[4])
    terms = []
    for off_a in range(3):
        for off_b in range(3):
            for off_c in range(3):
                piece = wide[
                    :, :, off_a : off_a + size_x, off_b : off_b + size_y, off_c : off_c + size_z
                ]
                terms.append(
                    jnp.einsum("bixyz,boxyz->oi", piece, delta, preferred_element_type=jnp.float32)
                )
    stacked = jnp.stack(terms, axis=-1)
    return stacked.reshape(stacked.shape[0], stacked.shape[1], 3, 3, 3)


def fine_rim(values):
    return padded(values, (("gx", 2), ("gy", 3)), 1)


def coarse_rim(values):
    return padded(values, (("gx", 2), ("gy", 3)), 1)


def on_device(
    state_now, enc_pre, mid_pre, dec_pre, cotangent, enc_kernel, mid_kernel, dec_kernel, out_kernel
):
    depth_pad = ((0, 0), (0, 0), (1, 1))
    enc_wide = enc_pre.astype(jnp.float32)
    mid_wide = mid_pre.astype(jnp.float32)
    dec_wide = dec_pre.astype(jnp.float32)
    hidden_enc = jax.nn.silu(enc_wide).astype(jnp.bfloat16)
    pooled = (block_sum(hidden_enc.astype(jnp.float32)) * 0.125).astype(jnp.bfloat16)
    hidden_mid = jax.nn.silu(mid_wide).astype(jnp.bfloat16)
    decoded = jax.nn.silu(dec_wide).astype(jnp.bfloat16)
    shape = state_now.shape
    cell_count = (
        shape[0]
        * lax.axis_size("dp")
        * shape[2]
        * lax.axis_size("gx")
        * shape[3]
        * lax.axis_size("gy")
        * shape[4]
    )
    grad_scale = 1.0 / math.sqrt(cell_count)
    out_term = jnp.einsum("boxyz,bcxyz->oc", cotangent, decoded, preferred_element_type=jnp.float32)
    dec_back = jnp.einsum(
        "oc,boxyz->bcxyz", out_kernel, cotangent, preferred_element_type=jnp.float32
    )
    dec_delta = (dec_back * silu_slope(dec_wide)).astype(jnp.bfloat16)
    dec_ext = fine_rim(dec_delta)
    joined = jnp.concatenate([upsample(hidden_mid), hidden_enc], axis=1)
    dec_term = values_rim_grad(fine_rim(joined), dec_delta)
    joined_back = apply_conv(dec_ext, flip_kernel(dec_kernel), depth_pad)
    wide_mid = joined_back.shape[1] - enc_pre.shape[1]
    mid_delta = (block_sum(joined_back[:, :wide_mid]) * silu_slope(mid_wide)).astype(jnp.bfloat16)
    mid_ext = coarse_rim(mid_delta)
    mid_term = values_rim_grad(coarse_rim(pooled), mid_delta)
    pool_back = apply_conv(mid_ext, flip_kernel(mid_kernel), depth_pad)
    enc_delta = (
        (joined_back[:, wide_mid:] + upsample(pool_back) * 0.125) * silu_slope(enc_wide)
    ).astype(jnp.bfloat16)
    enc_ext = fine_rim(enc_delta)
    enc_term = values_rim_grad(fine_rim(state_now), enc_delta)
    state_grad = (
        cotangent.astype(jnp.float32) + apply_conv(enc_ext, flip_kernel(enc_kernel), depth_pad)
    ).astype(jnp.bfloat16)
    totals = lax.psum((enc_term, mid_term, dec_term, out_term), ("dp", "gx", "gy"))
    return (
        state_grad,
        totals[0] * grad_scale,
        totals[1] * grad_scale,
        totals[2] * grad_scale,
        totals[3] * grad_scale,
    )


def solution(mesh):
    return jax.shard_map(
        on_device,
        mesh=mesh,
        in_specs=(
            P("dp", None, "gx", "gy", None),
            P("dp", None, "gx", "gy", None),
            P("dp", None, "gx", "gy", None),
            P("dp", None, "gx", "gy", None),
            P("dp", None, "gx", "gy", None),
            P(),
            P(),
            P(),
            P(),
        ),
        out_specs=(P("dp", None, "gx", "gy", None), P(), P(), P(), P()),
        check_vma=False,
    )
```

profile of v0, /device:TPU:1, one launch (start us, length us, event | category | flops | bytes accessed | tf_op | source)
XLA Modules:
  0.0 548.1 jit_solution(8730675966384088067)
XLA Ops:
  11.6 5.0 collective-permute-start
  27.7 5.8 %collective-permute-start.2 = (bf16[1,32,6,1,128]{4,1,3,2,0:T(8,128)(2,1)S(1)}, bf16[1,32,6,1,128]{4,1,3,2,0:T(8,128)(2,1)S(1)}, u32[]{:S(2)}, u32[]{:S(2)}) collective-permute-start(bf16[1,32,6,1,128]{4,1,3,2,0:T(8,128)(2,1)S(1)} %get-tuple-element.27), channel_id=1, source_target_pairs={{0,1},{1,2},{2,3},{3,4},{4,5},{5,6},{6,7},{8,9},{9,10},{10,11},{11... | collective-permute-start | bytes 147464 | tf_op jit(solution)/shard_map/ppermute | solution.py:17
  38.7 12.5 %reshape.520 = bf16[32,6,26,1,8,17]{5,4,0,2,1,3:T(8,128)(2,1)} reshape(bf16[32,6,26,1,136]{4,0,2,1,3:T(8,128)(2,1)} %pad.15) | data formatting | bytes 2715648 | tf_op jit(solution)/shard_map/conv_general_dilated | solution.py:27
  51.2 14.1 %copy.117 = bf16[32,6,26,1,8,17]{0,4,5,2,1,3:T(8,128)(2,1)} copy(bf16[32,6,26,1,8,17]{5,4,0,2,1,3:T(8,128)(2,1)} %reshape.520) | data formatting | bytes 2715648 | tf_op jit(solution)/shard_map/conv_general_dilated | solution.py:27
  66.7 13.7 %broadcast_select_fusion.1 = f32[4,24,8,17,96]{4,2,3,1,0:T(8,128)S(1)} fusion(pred[8,17]{0,1:T(8,128)(4,1)S(1)} %copy-done.34, bf16[32,96,3,3,3]{1,0,4,3,2:T(8,128)(2,1)S(1)} %copy-done, bf16[32,6,26,1,7,2]{0,4,5,2,1,3:T(8,128)(2,1)S(1)} %slice.490, bf16[32,6,26,1,8,17]{0,4,5,2,1,3:T(8,128)(2,1)} %copy.117), kind=kOutput, calls=%fused_computation.33 | convolution fusion | flops 2171639808 | bytes 6677128 | tf_op jit(solution)/shard_map/conv_general_dilated | solution.py:27
  86.2 6.8 %reduce_sum.20 = f32[64,2,12,64]{0,2,3,1:T(8,128)S(1)} reduce(f32[64,2,2,12,2,64,2]{0,4,3,6,5,2,1:T(2,128)} %bitcast.1227, f32[]{:T(128)} %constant.6.clone.1), dimensions={2,4,6}, to_apply=%region_0.1 | reduce | flops 688128 | bytes 3538948 | tf_op jit(solution)/shard_map/reduce_sum | solution.py:49
  100.3 6.7 %collective-permute-start.14 = (bf16[1,8,6,1,128]{4,1,3,2,0:T(8,128)(2,1)S(1)}, bf16[1,8,6,1,128]{4,1,3,2,0:T(8,128)(2,1)S(1)}, u32[]{:S(2)}, u32[]{:S(2)}) collective-permute-start(bf16[1,8,6,1,128]{4,1,3,2,0:T(8,128)(2,1)S(1)} %get-tuple-element.45), channel_id=1, source_target_pairs={{0,1},{1,2},{2,3},{3,4},{4,5},{5,6},{6,7},{8,9},{9,10},{10,11},{11... | collective-permute-start | bytes 36872 | tf_op jit(solution)/shard_map/ppermute | solution.py:17
  111.3 6.6 %collective-permute-start.6 = (bf16[1,64,4,1,64]{1,3,4,2,0:T(2,128)(2,1)S(1)}, bf16[1,64,4,1,64]{1,3,4,2,0:T(2,128)(2,1)S(1)}, u32[]{:S(2)}, u32[]{:S(2)}) collective-permute-start(bf16[1,64,4,1,64]{1,3,4,2,0:T(2,128)(2,1)S(1)} %get-tuple-element.29), channel_id=1, source_target_pairs={{0,1},{1,2},{2,3},{3,4},{4,5},{5,6},{6,7},{8,9},{9,10},{10,11},{11... | collective-permute-start | bytes 98312 | tf_op jit(solution)/shard_map/ppermute | solution.py:17
  119.1 4.7 slice.491
  128.0 5.9 %copy.253 = f32[4,24,1,128,32]{3,4,1,0,2:T(8,128)} copy(f32[4,24,1,128,32]{4,1,3,0,2:T(8,128)} %slice.492) | data formatting | bytes 3145728
  152.4 5.7 %copy.127 = f32[1,32,4,24,128]{4,1,3,2,0:T(8,128)} copy(f32[1,32,4,24,128]{1,3,4,2,0:T(8,128)} %bitcast.1228) | data formatting | bytes 3145728 | tf_op jit(solution)/shard_map/mul | solution.py:122
  163.2 4.8 collective-permute-start.8
  178.0 70.2 %all-reduce.3 = (f32[32,8,3,3,3]{0,1,4,3,2:T(8,128)}, f32[8,32]{1,0:T(8,128)S(1)}) all-reduce(f32[32,8,3,3,3]{0,1,4,3,2:T(8,128)} %bitcast.1242, f32[8,32]{1,0:T(8,128)S(1)} %convolution_bitcast_fusion.27), channel_id=1, replica_groups=mesh['dp'=2,'gx'=8,'gy'=8] {'dp','gx','gy'}, use_global_device_ids=true, to_apply=%region_1.2 | all-reduce | flops 7168 | bytes 57344 | tf_op jit(solution)/shard_map/psum | solution.py:129
  253.2 7.6 %reduce_sum.22 = f32[32,2,12,64]{0,3,2,1:T(8,128)} reduce(f32[32,2,2,12,2,64,2]{0,6,5,4,3,2,1:T(2,128)} %bitcast.1226, f32[]{:T(128)} %constant.6.clone.1), dimensions={2,4,6}, to_apply=%region_2.3 | reduce | flops 344064 | bytes 1769476 | tf_op jit(solution)/shard_map/reduce_sum | solution.py:49
  273.9 5.7 %collective-permute-start.18 = (bf16[1,32,4,1,64]{4,1,3,2,0:T(8,128)(2,1)S(1)}, bf16[1,32,4,1,64]{4,1,3,2,0:T(8,128)(2,1)S(1)}, u32[]{:S(2)}, u32[]{:S(2)}) collective-permute-start(bf16[1,32,4,1,64]{4,1,3,2,0:T(8,128)(2,1)S(1)} %get-tuple-element.43), channel_id=1, source_target_pairs={{0,1},{1,2},{2,3},{3,4},{4,5},{5,6},{6,7},{8,9},{9,10},{10,11},{11... | collective-permute-start | bytes 49160 | tf_op jit(solution)/shard_map/ppermute | solution.py:17
  280.2 9.8 %collective-permute-done.19 = bf16[1,32,4,1,64]{4,1,3,2,0:T(8,128)(2,1)S(1)} collective-permute-done((bf16[1,32,4,1,64]{4,1,3,2,0:T(8,128)(2,1)S(1)}, bf16[1,32,4,1,64]{4,1,3,2,0:T(8,128)(2,1)S(1)}, u32[]{:S(2)}, u32[]{:S(2)}) %collective-permute-start.19) | collective-permute-done | bytes 16416 | tf_op jit(solution)/shard_map/ppermute | solution.py:19
  300.5 5.5 %collective-permute-start.10 = (bf16[1,32,6,1,128]{4,1,3,2,0:T(8,128)(2,1)S(1)}, bf16[1,32,6,1,128]{4,1,3,2,0:T(8,128)(2,1)S(1)}, u32[]{:S(2)}, u32[]{:S(2)}) collective-permute-start(bf16[1,32,6,1,128]{4,1,3,2,0:T(8,128)(2,1)S(1)} %get-tuple-element.25), channel_id=1, source_target_pairs={{0,1},{1,2},{2,3},{3,4},{4,5},{5,6},{6,7},{8,9},{9,10},{10,11},{11... | collective-permute-start | bytes 147464 | tf_op jit(solution)/shard_map/ppermute | solution.py:17
  308.1 6.1 %collective-permute-start.22 = (bf16[1,96,6,1,128]{4,1,3,2,0:T(8,128)(2,1)}, bf16[1,96,6,1,128]{4,1,3,2,0:T(8,128)(2,1)}, u32[]{:S(2)}, u32[]{:S(2)}) collective-permute-start(bf16[1,96,6,1,128]{4,1,3,2,0:T(8,128)(2,1)} %get-tuple-element.21), channel_id=1, source_target_pairs={{0,1},{1,2},{2,3},{3,4},{4,5},{5,6},{6,7},{8,9},{9,10},{10,11},{11... | collective-permute-start | bytes 442376 | tf_op jit(solution)/shard_map/ppermute | solution.py:17
  319.1 12.5 %reshape.534 = bf16[32,6,26,1,8,17]{5,4,0,2,1,3:T(8,128)(2,1)} reshape(bf16[32,6,26,1,136]{4,0,2,1,3:T(8,128)(2,1)} %pad.19) | data formatting | bytes 2715648 | tf_op jit(solution)/shard_map/conv_general_dilated | solution.py:27
  331.7 14.1 %copy.130 = bf16[32,6,26,1,8,17]{0,4,5,2,1,3:T(8,128)(2,1)} copy(bf16[32,6,26,1,8,17]{5,4,0,2,1,3:T(8,128)(2,1)} %reshape.534) | data formatting | bytes 2715648 | tf_op jit(solution)/shard_map/conv_general_dilated | solution.py:27
  347.9 11.7 %select_maximum_fusion = bf16[1,96,6,26,130]{4,1,3,2,0:T(8,128)(2,1)S(1)} fusion(bf16[1,96,6,1,128]{4,1,3,2,0:T(8,128)(2,1)} %collective-permute-done.23, bf16[1,96,6,1,128]{4,1,3,2,0:T(8,128)(2,1)} %collective-permute-done.22, bf16[1,96,1,24,128]{4,1,3,2,0:T(8,128)(2,1)S(1)} %copy-done.5, bf16[1,96,1,24,128]{4,1,3,2,0:T(8,128)(2,1)S(1)} %copy-done.7, ...), kind=kLoop, calls=%fused_computation.6 | loop fusion | flops 40884480 | bytes 7727616 | tf_op jit(solution)/shard_map/concatenate | solution.py:15
  391.6 15.1 %broadcast_select_fusion = f32[4,24,8,17,8]{4,2,3,1,0:T(8,128)} fusion(pred[8,17]{0,1:T(8,128)(4,1)S(1)} %copy-done.35, bf16[32,8,3,3,3]{0,1,4,3,2:T(8,128)(2,1)S(1)} %copy-done.33, bf16[32,6,26,1,7,2]{0,4,5,2,1,3:T(8,128)(2,1)S(1)} %copy-done.18, bf16[32,6,26,1,8,17]{0,4,5,2,1,3:T(8,128)(2,1)} %copy.130), kind=kOutput, calls=%fused_computation.32 | convolution fusion | flops 185143296 | bytes 1929352 | tf_op jit(solution)/shard_map/conv_general_dilated | solution.py:27
  406.6 7.8 %copy.131 = f32[4,24,8,17,8]{3,2,4,1,0:T(8,128)} copy(f32[4,24,8,17,8]{4,2,3,1,0:T(8,128)} %broadcast_select_fusion) | data formatting | bytes 835584 | tf_op jit(solution)/shard_map/conv_general_dilated | solution.py:27
  417.7 119.8 %all-reduce.7.cloned.1.call-done = (f32[64,32,3,3,3]{0,1,4,3,2:T(8,128)}, f32[32,96,3,3,3]{1,0,4,3,2:T(8,128)}) async-done(((f32[64,32,3,3,3]{0,1,4,3,2:T(8,128)}, f32[32,96,3,3,3]{1,0,4,3,2:T(8,128)}), (f32[64,32,3,3,3]{0,1,4,3,2:T(8,128)}, f32[32,96,3,3,3]{1,0,4,3,2:T(8,128)})) %all-reduce.7.cloned.1.call-update) | async-done | bytes 552976 | tf_op jit(solution)/shard_map/psum | solution.py:129
  (258 shorter events, 154.6 us)
Async XLA Ops:
  7.2 530.3 %all-reduce.7.cloned.1.call-start = ((), (), s32[]{:S(2)}) async-start(), calls=%async_computation | async-start | bytes 1769472 | tf_op jit(solution)/shard_map/psum | solution.py:129
  10.3 16.0 %collective-permute-start.1 = (bf16[1,32,1,24,128]{4,1,3,2,0:T(8,128)(2,1)}, bf16[1,32,1,24,128]{4,1,3,2,0:T(8,128)(2,1)S(1)}, u32[]{:S(2)}, u32[]{:S(2)}) collective-permute-start(bf16[1,32,1,24,128]{4,1,3,2,0:T(8,128)(2,1)} %get-tuple-element.36), channel_id=1, source_target_pairs={{8,0},{16,8},{24,16},{32,24},{40,32},{48,40},{56,48},{9,1},{17,9},... | collective-permute-start | bytes 589832 | tf_op jit(solution)/shard_map/ppermute | solution.py:19
  11.6 14.7 %collective-permute-start = (bf16[1,32,1,24,128]{4,1,3,2,0:T(8,128)(2,1)}, bf16[1,32,1,24,128]{4,1,3,2,0:T(8,128)(2,1)S(1)}, u32[]{:S(2)}, u32[]{:S(2)}) collective-permute-start(bf16[1,32,1,24,128]{4,1,3,2,0:T(8,128)(2,1)} %get-tuple-element.35), channel_id=1, source_target_pairs={{0,8},{8,16},{16,24},{24,32},{32,40},{40,48},{48,56},{1,9},{9,17},... | collective-permute-start | bytes 589832 | tf_op jit(solution)/shard_map/ppermute | solution.py:17
  16.8 9.4 %collective-permute-start.12 = (bf16[1,8,1,24,128]{4,1,3,2,0:T(8,128)(2,1)S(1)}, bf16[1,8,1,24,128]{4,1,3,2,0:T(8,128)(2,1)S(1)}, u32[]{:S(2)}, u32[]{:S(2)}) collective-permute-start(bf16[1,8,1,24,128]{4,1,3,2,0:T(8,128)(2,1)S(1)} %get-tuple-element.50), channel_id=1, source_target_pairs={{0,8},{8,16},{16,24},{24,32},{32,40},{40,48},{48,56},{1,9},{9,17},... | collective-permute-start | bytes 147464 | tf_op jit(solution)/shard_map/ppermute | solution.py:17
  21.0 12.5 %collective-permute-start.13 = (bf16[1,8,1,24,128]{4,1,3,2,0:T(8,128)(2,1)S(1)}, bf16[1,8,1,24,128]{4,1,3,2,0:T(8,128)(2,1)S(1)}, u32[]{:S(2)}, u32[]{:S(2)}) collective-permute-start(bf16[1,8,1,24,128]{4,1,3,2,0:T(8,128)(2,1)S(1)} %get-tuple-element.49), channel_id=1, source_target_pairs={{8,0},{16,8},{24,16},{32,24},{40,32},{48,40},{56,48},{9,1},{17,9},... | collective-permute-start | bytes 147464 | tf_op jit(solution)/shard_map/ppermute | solution.py:19
  26.4 7.2 %collective-permute-start.3 = (bf16[1,32,6,1,128]{4,1,3,2,0:T(8,128)(2,1)S(1)}, bf16[1,32,6,1,128]{4,1,3,2,0:T(8,128)(2,1)S(1)}, u32[]{:S(2)}, u32[]{:S(2)}) collective-permute-start(bf16[1,32,6,1,128]{4,1,3,2,0:T(8,128)(2,1)S(1)} %get-tuple-element.28), channel_id=1, source_target_pairs={{1,0},{2,1},{3,2},{4,3},{5,4},{6,5},{7,6},{9,8},{10,9},{11,10},{12... | collective-permute-start | bytes 147464 | tf_op jit(solution)/shard_map/ppermute | solution.py:19
  27.7 7.3 %collective-permute-start.2 = (bf16[1,32,6,1,128]{4,1,3,2,0:T(8,128)(2,1)S(1)}, bf16[1,32,6,1,128]{4,1,3,2,0:T(8,128)(2,1)S(1)}, u32[]{:S(2)}, u32[]{:S(2)}) collective-permute-start(bf16[1,32,6,1,128]{4,1,3,2,0:T(8,128)(2,1)S(1)} %get-tuple-element.27), channel_id=1, source_target_pairs={{0,1},{1,2},{2,3},{3,4},{4,5},{5,6},{6,7},{8,9},{9,10},{10,11},{11... | collective-permute-start | bytes 147464 | tf_op jit(solution)/shard_map/ppermute | solution.py:17
  93.5 13.5 %collective-permute-start.5 = (bf16[1,64,1,12,64]{1,3,4,2,0:T(8,128)(2,1)S(1)}, bf16[1,64,1,12,64]{1,3,4,2,0:T(8,128)(2,1)S(1)}, u32[]{:S(2)}, u32[]{:S(2)}) collective-permute-start(bf16[1,64,1,12,64]{1,3,4,2,0:T(8,128)(2,1)S(1)} %get-tuple-element.40), channel_id=1, source_target_pairs={{8,0},{16,8},{24,16},{32,24},{40,32},{48,40},{56,48},{9,1},{17,9},... | collective-permute-start | bytes 294920 | tf_op jit(solution)/shard_map/ppermute | solution.py:19
  94.8 14.9 %collective-permute-start.4 = (bf16[1,64,1,12,64]{1,3,4,2,0:T(8,128)(2,1)S(1)}, bf16[1,64,1,12,64]{1,3,4,2,0:T(8,128)(2,1)S(1)}, u32[]{:S(2)}, u32[]{:S(2)}) collective-permute-start(bf16[1,64,1,12,64]{1,3,4,2,0:T(8,128)(2,1)S(1)} %get-tuple-element.39), channel_id=1, source_target_pairs={{0,8},{8,16},{16,24},{24,32},{32,40},{40,48},{48,56},{1,9},{9,17},... | collective-permute-start | bytes 294920 | tf_op jit(solution)/shard_map/ppermute | solution.py:17
  99.0 18.9 %collective-permute-start.15 = (bf16[1,8,6,1,128]{4,1,3,2,0:T(8,128)(2,1)S(1)}, bf16[1,8,6,1,128]{4,1,3,2,0:T(8,128)(2,1)S(1)}, u32[]{:S(2)}, u32[]{:S(2)}) collective-permute-start(bf16[1,8,6,1,128]{4,1,3,2,0:T(8,128)(2,1)S(1)} %get-tuple-element.46), channel_id=1, source_target_pairs={{1,0},{2,1},{3,2},{4,3},{5,4},{6,5},{7,6},{9,8},{10,9},{11,10},{12... | collective-permute-start | bytes 36872 | tf_op jit(solution)/shard_map/ppermute | solution.py:19
  100.3 17.6 %collective-permute-start.14 = (bf16[1,8,6,1,128]{4,1,3,2,0:T(8,128)(2,1)S(1)}, bf16[1,8,6,1,128]{4,1,3,2,0:T(8,128)(2,1)S(1)}, u32[]{:S(2)}, u32[]{:S(2)}) collective-permute-start(bf16[1,8,6,1,128]{4,1,3,2,0:T(8,128)(2,1)S(1)} %get-tuple-element.45), channel_id=1, source_target_pairs={{0,1},{1,2},{2,3},{3,4},{4,5},{5,6},{6,7},{8,9},{9,10},{10,11},{11... | collective-permute-start | bytes 36872 | tf_op jit(solution)/shard_map/ppermute | solution.py:17
  110.0 31.1 %collective-permute-start.7 = (bf16[1,64,4,1,64]{1,3,4,2,0:T(2,128)(2,1)S(1)}, bf16[1,64,4,1,64]{1,3,4,2,0:T(2,128)(2,1)S(1)}, u32[]{:S(2)}, u32[]{:S(2)}) collective-permute-start(bf16[1,64,4,1,64]{1,3,4,2,0:T(2,128)(2,1)S(1)} %get-tuple-element.30), channel_id=1, source_target_pairs={{1,0},{2,1},{3,2},{4,3},{5,4},{6,5},{7,6},{9,8},{10,9},{11,10},{12... | collective-permute-start | bytes 98312 | tf_op jit(solution)/shard_map/ppermute | solution.py:19
  111.3 29.8 %collective-permute-start.6 = (bf16[1,64,4,1,64]{1,3,4,2,0:T(2,128)(2,1)S(1)}, bf16[1,64,4,1,64]{1,3,4,2,0:T(2,128)(2,1)S(1)}, u32[]{:S(2)}, u32[]{:S(2)}) collective-permute-start(bf16[1,64,4,1,64]{1,3,4,2,0:T(2,128)(2,1)S(1)} %get-tuple-element.29), channel_id=1, source_target_pairs={{0,1},{1,2},{2,3},{3,4},{4,5},{5,6},{6,7},{8,9},{9,10},{10,11},{11... | collective-permute-start | bytes 98312 | tf_op jit(solution)/shard_map/ppermute | solution.py:17
  161.9 136.5 %collective-permute-start.9 = (bf16[1,32,1,24,128]{4,1,3,2,0:T(8,128)(2,1)}, bf16[1,32,1,24,128]{4,1,3,2,0:T(8,128)(2,1)}, u32[]{:S(2)}, u32[]{:S(2)}) collective-permute-start(bf16[1,32,1,24,128]{4,1,3,2,0:T(8,128)(2,1)} %get-tuple-element.34), channel_id=1, source_target_pairs={{8,0},{16,8},{24,16},{32,24},{40,32},{48,40},{56,48},{9,1},{17,9},... | collective-permute-start | bytes 589832 | tf_op jit(solution)/shard_map/ppermute | solution.py:19
  163.2 135.2 %collective-permute-start.8 = (bf16[1,32,1,24,128]{4,1,3,2,0:T(8,128)(2,1)}, bf16[1,32,1,24,128]{4,1,3,2,0:T(8,128)(2,1)}, u32[]{:S(2)}, u32[]{:S(2)}) collective-permute-start(bf16[1,32,1,24,128]{4,1,3,2,0:T(8,128)(2,1)} %get-tuple-element.33), channel_id=1, source_target_pairs={{0,8},{8,16},{16,24},{24,32},{32,40},{40,48},{48,56},{1,9},{9,17},... | collective-permute-start | bytes 589832 | tf_op jit(solution)/shard_map/ppermute | solution.py:17
  265.3 7.3 %collective-permute-start.16 = (bf16[1,32,1,12,64]{4,1,3,2,0:T(8,128)(2,1)S(1)}, bf16[1,32,1,12,64]{4,1,3,2,0:T(8,128)(2,1)S(1)}, u32[]{:S(2)}, u32[]{:S(2)}) collective-permute-start(bf16[1,32,1,12,64]{4,1,3,2,0:T(8,128)(2,1)S(1)} %get-tuple-element.47), channel_id=1, source_target_pairs={{0,8},{8,16},{16,24},{24,32},{32,40},{40,48},{48,56},{1,9},{9,17},... | collective-permute-start | bytes 147464 | tf_op jit(solution)/shard_map/ppermute | solution.py:17
  269.4 36.6 %collective-permute-start.21 = (bf16[1,96,1,24,128]{4,1,3,2,0:T(8,128)(2,1)S(1)}, bf16[1,96,1,24,128]{4,1,3,2,0:T(8,128)(2,1)S(1)}, u32[]{:S(2)}, u32[]{:S(2)}) collective-permute-start(bf16[1,96,1,24,128]{4,1,3,2,0:T(8,128)(2,1)S(1)} %get-tuple-element.24), channel_id=1, source_target_pairs={{8,0},{16,8},{24,16},{32,24},{40,32},{48,40},{56,48},{9,1},{17,9},... | collective-permute-start | bytes 1769480 | tf_op jit(solution)/shard_map/ppermute | solution.py:19
  272.6 17.4 %collective-permute-start.19 = (bf16[1,32,4,1,64]{4,1,3,2,0:T(8,128)(2,1)S(1)}, bf16[1,32,4,1,64]{4,1,3,2,0:T(8,128)(2,1)S(1)}, u32[]{:S(2)}, u32[]{:S(2)}) collective-permute-start(bf16[1,32,4,1,64]{4,1,3,2,0:T(8,128)(2,1)S(1)} %get-tuple-element.44), channel_id=1, source_target_pairs={{1,0},{2,1},{3,2},{4,3},{5,4},{6,5},{7,6},{9,8},{10,9},{11,10},{12... | collective-permute-start | bytes 49160 | tf_op jit(solution)/shard_map/ppermute | solution.py:19
  273.9 17.4 %collective-permute-start.18 = (bf16[1,32,4,1,64]{4,1,3,2,0:T(8,128)(2,1)S(1)}, bf16[1,32,4,1,64]{4,1,3,2,0:T(8,128)(2,1)S(1)}, u32[]{:S(2)}, u32[]{:S(2)}) collective-permute-start(bf16[1,32,4,1,64]{4,1,3,2,0:T(8,128)(2,1)S(1)} %get-tuple-element.43), channel_id=1, source_target_pairs={{0,1},{1,2},{2,3},{3,4},{4,5},{5,6},{6,7},{8,9},{9,10},{10,11},{11... | collective-permute-start | bytes 49160 | tf_op jit(solution)/shard_map/ppermute | solution.py:17
  290.0 16.0 %collective-permute-start.20 = (bf16[1,96,1,24,128]{4,1,3,2,0:T(8,128)(2,1)S(1)}, bf16[1,96,1,24,128]{4,1,3,2,0:T(8,128)(2,1)S(1)}, u32[]{:S(2)}, u32[]{:S(2)}) collective-permute-start(bf16[1,96,1,24,128]{4,1,3,2,0:T(8,128)(2,1)S(1)} %get-tuple-element.23), channel_id=1, source_target_pairs={{0,8},{8,16},{16,24},{24,32},{32,40},{40,48},{48,56},{1,9},{9,17},... | collective-permute-start | bytes 1769480 | tf_op jit(solution)/shard_map/ppermute | solution.py:17
  299.2 15.4 %collective-permute-start.11 = (bf16[1,32,6,1,128]{4,1,3,2,0:T(8,128)(2,1)S(1)}, bf16[1,32,6,1,128]{4,1,3,2,0:T(8,128)(2,1)S(1)}, u32[]{:S(2)}, u32[]{:S(2)}) collective-permute-start(bf16[1,32,6,1,128]{4,1,3,2,0:T(8,128)(2,1)S(1)} %get-tuple-element.26), channel_id=1, source_target_pairs={{1,0},{2,1},{3,2},{4,3},{5,4},{6,5},{7,6},{9,8},{10,9},{11,10},{12... | collective-permute-start | bytes 147464 | tf_op jit(solution)/shard_map/ppermute | solution.py:19
  300.5 14.9 %collective-permute-start.10 = (bf16[1,32,6,1,128]{4,1,3,2,0:T(8,128)(2,1)S(1)}, bf16[1,32,6,1,128]{4,1,3,2,0:T(8,128)(2,1)S(1)}, u32[]{:S(2)}, u32[]{:S(2)}) collective-permute-start(bf16[1,32,6,1,128]{4,1,3,2,0:T(8,128)(2,1)S(1)} %get-tuple-element.25), channel_id=1, source_target_pairs={{0,1},{1,2},{2,3},{3,4},{4,5},{5,6},{6,7},{8,9},{9,10},{10,11},{11... | collective-permute-start | bytes 147464 | tf_op jit(solution)/shard_map/ppermute | solution.py:17
  306.8 41.1 %collective-permute-start.23 = (bf16[1,96,6,1,128]{4,1,3,2,0:T(8,128)(2,1)}, bf16[1,96,6,1,128]{4,1,3,2,0:T(8,128)(2,1)}, u32[]{:S(2)}, u32[]{:S(2)}) collective-permute-start(bf16[1,96,6,1,128]{4,1,3,2,0:T(8,128)(2,1)} %get-tuple-element.22), channel_id=1, source_target_pairs={{1,0},{2,1},{3,2},{4,3},{5,4},{6,5},{7,6},{9,8},{10,9},{11,10},{12... | collective-permute-start | bytes 442376 | tf_op jit(solution)/shard_map/ppermute | solution.py:19
  308.1 39.8 %collective-permute-start.22 = (bf16[1,96,6,1,128]{4,1,3,2,0:T(8,128)(2,1)}, bf16[1,96,6,1,128]{4,1,3,2,0:T(8,128)(2,1)}, u32[]{:S(2)}, u32[]{:S(2)}) collective-permute-start(bf16[1,96,6,1,128]{4,1,3,2,0:T(8,128)(2,1)} %get-tuple-element.21), channel_id=1, source_target_pairs={{0,1},{1,2},{2,3},{3,4},{4,5},{5,6},{6,7},{8,9},{9,10},{10,11},{11... | collective-permute-start | bytes 442376 | tf_op jit(solution)/shard_map/ppermute | solution.py:17
  (38 other events, 533.7 us)
Sparse Core Ops, SparseCore 0:
  391.7 145.7 all-reduce.6
where the time goes:
time: 555 us; the launch traced here: 548 us
  waiting for transfers between devices  138 us (25%)
  local copies, waits for them, and re-layouts  124 us (22%)
  matrix products  78.3 us (14%)
  starting transfers between devices  75.6 us (14%)
  blocking collectives  70.2 us (13%)
  other arithmetic  47 us (8%)
  between operations  15.2 us (3%)
    psum x1, waiting for transfers between devices, on_device(): lax.psum((enc_term, mid_term, dec_term, out_term), ('dp', 'gx', 'gy'))  120 us
    conv_general_dilated x15, local copies, waits for them, and re-layouts, apply_conv(): lax.conv_general_dilated(values, kernel, (1, 1, 1), pads, dimension_numbe...  80.3 us
    psum x1, blocking collectives, on_device(): lax.psum((enc_term, mid_term, dec_term, out_term), ('dp', 'gx', 'gy'))  70.2 us
    ppermute x12, starting transfers between devices, padded(): lax.ppermute(tail, axis, [(i, (i + 1) % count) for i in range(ends)])  60 us
    dot_general x81, matrix products, values_rim_grad(): jnp.einsum('bixyz,boxyz->oi', piece, delta, preferred_element_type=jnp.fl...  43.3 us
    conv_general_dilated x3, matrix products, apply_conv(): lax.conv_general_dilated(values, kernel, (1, 1, 1), pads, dimension_numbe...  32.2 us
    concatenate x8, other arithmetic, padded(): jnp.concatenate([lax.ppermute(tail, axis, [(i, (i + 1) % count) for i in...  20.3 us
    ppermute x12, starting transfers between devices, padded(): lax.ppermute(head, axis, [((i + 1) % count, i) for i in range(ends)])  15.6 us
  transfers between devices with their start and end apart: 25, of which 6 were waited for; matrix products, arithmetic and copies ran while one was open for 22% of the time, Pallas kernels for 0%

commit v1 on v0

v1 whole, which is shorter than its diff:
```python
import functools
import math

import jax
import jax.numpy as jnp
import numpy as np
from jax import lax
from jax.experimental import pallas as pl
from jax.experimental.pallas import tpu as pltpu
from jax.sharding import PartitionSpec as P

F32 = jnp.float32
BF16 = jnp.bfloat16


VMEM = pl.BlockSpec(memory_space=pltpu.VMEM)
HBM = pl.BlockSpec(memory_space=pltpu.HBM)


def call(body, outs, scratch, args, flops, limit, far=0, far_outs=0):
    return pl.pallas_call(
        body,
        out_shape=outs,
        in_specs=[HBM] * far + [VMEM] * (len(args) - far),
        out_specs=[HBM] * far_outs + [VMEM] * (len(outs) - far_outs),
        scratch_shapes=scratch,
        compiler_params=pltpu.CompilerParams(vmem_limit_bytes=limit << 20),
        cost_estimate=pl.CostEstimate(flops=flops, bytes_accessed=4 << 20, transcendentals=0),
    )(*args)


def fetch(pairs, sems):
    copies = [pltpu.make_async_copy(src, dst, sems.at[i]) for i, (src, dst) in enumerate(pairs)]
    for copy in copies:
        copy.start()
    return [copy.wait for copy in copies]


def sds(shape, dtype):
    return jax.ShapeDtypeStruct(shape, dtype)


def dot(a, b):
    return lax.dot_general(a, b, (((1,), (0,)), ((), ())), preferred_element_type=F32)


def dot_tn(a, b):
    return lax.dot_general(a, b, (((0,), (0,)), ((), ())), preferred_element_type=F32)


def dot_nt(a, b):
    return lax.dot_general(a, b, (((1,), (1,)), ((), ())), preferred_element_type=F32)


def sigmoid(v):
    return 0.5 + 0.5 * jnp.tanh(0.5 * v)


def slope(v, s):
    return s * (1.0 + v * (1.0 - s))


def lane_ids(shape):
    return lax.broadcasted_iota(jnp.int32, shape, len(shape) - 1)


def shifts(v, period):
    lane = jnp.bitwise_and(lane_ids(v.shape), period - 1)
    axis = v.ndim - 1
    size = v.shape[-1]
    back = jnp.where(lane == period - 1, 0.0, pltpu.roll(v, size - 1, axis))
    ahead = jnp.where(lane == 0, 0.0, pltpu.roll(v, 1, axis))
    return back, v, ahead


def delta_plane(dec, cot, head):
    pre = jnp.swapaxes(dec.astype(F32), 0, 1)
    cot = jnp.swapaxes(cot.astype(F32), 0, 1)
    cot_lanes = jnp.concatenate([cot[y] for y in range(24)], axis=1).astype(BF16)
    back = dot_tn(head, cot_lanes)
    back = jnp.stack([back[:, y * 128 : y * 128 + 128] for y in range(24)], axis=0)
    s = sigmoid(pre)
    return (back * slope(pre, s)).astype(BF16), cot_lanes, pre * s


def face_body(dec_far, cot_far, head_far, low_far, high_far, dec_ref, cot_ref, head_ref, delta_ref, sems, out_sems):
    planes = (0, 3)
    pairs = [(head_far, head_ref)]
    for i, x in enumerate(planes):
        pairs += [(cot_far.at[:, x], cot_ref.at[i]), (dec_far.at[:, x], dec_ref.at[i])]
    waits = fetch(pairs, sems)
    waits[0]()
    writes = []
    for i, far in enumerate((low_far, high_far)):
        waits[2 * i + 1]()
        waits[2 * i + 2]()
        delta_ref[i] = delta_plane(dec_ref[i], cot_ref[i], head_ref[...])[0]
        writes += fetch([(delta_ref.at[i], far)], out_sems.at[i])
    for wait in writes:
        wait()


def forward_body(
    dec_ref, cot_ref, head_ref, enc_ref, state_ref, mid_ref, pool_ref,
    delta_ref, head_grad_ref, hid_ref, slope_ref, pooled_ref, hmid_ref, mslope_ref, st_ref, ylo_ref, yhi_ref, xlo_ref, xhi_ref,
):
    total = jnp.zeros((8, 32), F32)
    for x in range(4):
        delta, cot_lanes, decoded = delta_plane(dec_ref[:, x], cot_ref[:, x], head_ref[...])
        if x in (1, 2):
            delta_ref[x - 1] = delta
        decoded = jnp.concatenate([decoded[y] for y in range(24)], axis=1).astype(BF16)
        total = total + dot_nt(cot_lanes, decoded)
    head_grad_ref[...] = total
    low_rows, high_rows = [], []
    for x in range(4):
        pre = jnp.swapaxes(enc_ref[:, x].astype(F32), 0, 1)
        s = sigmoid(pre)
        hid_ref[x] = (pre * s).astype(BF16)
        slope_ref[x] = slope(pre, s)
        state = jnp.swapaxes(state_ref[:, x].astype(F32), 0, 1)
        st_ref[x] = state
        low_rows.append(state[0])
        high_rows.append(state[23])
    ylo_ref[64:96, :] = jnp.concatenate(low_rows, axis=0).astype(BF16)
    yhi_ref[64:96, :] = jnp.concatenate(high_rows, axis=0).astype(BF16)
    tilts = {}
    for bx in range(2):
        for m in range(6):
            acc = None
            for ex in range(2):
                for ey in range(2):
                    pair = jnp.concatenate(
                        [hid_ref[2 * bx + ex, 4 * m + ey], hid_ref[2 * bx + ex, 4 * m + 2 + ey]], axis=1
                    )
                    part = dot(pair, pool_ref[:, 128:256])
                    acc = part if acc is None else acc + part
            pooled = (acc * 0.125).astype(BF16)
            pooled_ref[bx, m] = pooled
            side_ref = xlo_ref if bx == 0 else xhi_ref
            side_ref[m * 32 : m * 32 + 32, :] = pooled
            pre = mid_ref[bx, m].astype(F32)
            s = sigmoid(pre)
            hmid_ref[bx, m] = (pre * s).astype(BF16)
            tilts[bx, m] = slope(pre, s)
            mslope_ref[bx, m] = tilts[bx, m]
    lower = lane_ids((64, 128)) < 64
    ylo_ref[0:64, :] = jnp.where(lower, tilts[0, 0], pltpu.roll(tilts[1, 0], 64, 1)).astype(BF16)
    yhi_ref[0:64, :] = jnp.where(lower, pltpu.roll(tilts[0, 5], 64, 1), tilts[1, 5]).astype(BF16)


def window_sums(rows_of, pool, put):
    got = dot(
        jnp.concatenate([jnp.concatenate([rows_of(x, j) for j in range(4)], axis=0) for x in range(6)], axis=0), pool
    )
    sums = []
    for x in range(6):
        at = [got[x * 128 + j * 32 : x * 128 + j * 32 + 32] for j in range(4)]
        sums.append([at[j] + at[j + 1] for j in (2, 1, 0)])
    for bx in range(2):
        for a, kx in enumerate((-1, 0, 1)):
            for b in range(3):
                both = (sums[2 * bx - kx + 1][b] + sums[2 * bx - kx + 2][b]).astype(BF16)
                for c in range(3):
                    put(bx, ((a * 3 + b) * 3 + c) * 32, both[:, c * 128 : c * 128 + 128])


def stack_of(row):
    return jnp.concatenate(
        [jnp.concatenate([row(x + 1 - kx) for x in range(4)], axis=1) for kx in (-1, 0, 1)], axis=0
    )


def skip_weights(w_ref):
    parts = [
        jnp.concatenate([w_ref[a, b].astype(F32).reshape(96, 96)[:, 64:96] for b in range(3)], axis=1)
        for a in range(3)
    ]
    return jnp.concatenate(parts, axis=0).T.astype(BF16)


def inner_body(xlo_ref, low_ref, delta_ref, high_ref, xhi_ref, pool_ref, w_ref, wmid_ref, acc_ref, wide_ref, win_ref, up_ref, wskip_ref, wm_ref):
    def put(x, v):
        parts = shifts(v.astype(F32).reshape(768, 128), 128)
        for a in range(3):
            wide_ref[x, :, a * 32 : a * 32 + 32, :] = parts[a].astype(BF16).reshape(24, 32, 128)

    for x, v in enumerate((xlo_ref[...], low_ref[...], delta_ref[0], delta_ref[1], high_ref[...], xhi_ref[...])):
        put(x, v)
    wskip_ref[...] = skip_weights(w_ref)
    acc_ref[...] = jnp.zeros(acc_ref.shape, F32)

    def step(i, carry):
        y = 4 * i
        out = dot(
            wskip_ref[...],
            jnp.concatenate([stack_of(lambda x, j=j: wide_ref[x, y + j]) for j in range(4)], axis=1),
        )
        for x in range(4):
            for r in range(6):
                parts = [
                    out[b * 32 : b * 32 + 32, ((r - b) * 4 + x) * 128 : ((r - b) * 4 + x) * 128 + 128]
                    for b in range(3)
                    if 0 <= r - b < 4
                ]
                acc_ref[x, y + r] += sum(parts[1:], parts[0])
        return carry

    lax.fori_loop(0, 6, step, 0)
    for m in range(1, 5):

        def rows_of(x, j):
            return jnp.concatenate(
                [wide_ref[x, 4 * m + j - 1, 32:64, :], wide_ref[x, 4 * m + j + 1, 32:64, :]], axis=1
            )

        def put_window(bx, row, v):
            lane = (bx * 4 + m - 1) * 128
            win_ref[row : row + 32, lane : lane + 128] = v

        window_sums(rows_of, pool_ref[...], put_window)
    w = w_ref[...].reshape(864, 96)
    up_ref[...] = dot_tn(w, win_ref[...])[:64]
    for a in range(3):
        for b in range(3):
            at = (a * 3 + b) * 32
            parts = [wmid_ref[a, b, c].astype(F32) for c in range(3)]
            wm_ref[at : at + 32, :] = jnp.concatenate(parts, axis=1).astype(BF16)


def outer_body(
    got_lo_ref, got_hi_ref, wide_ref, up_ref, mslope_ref, st_ref, pool_lo_ref, pool_hi_ref, pool_ref, w_ref, wskip_ref, wm_ref,
    edge_ref, rim_ref, win_ref, mid_ref, back_ref, face_lo_ref, face_hi_ref,
    total_ref,
):
    wskip = wskip_ref[...]

    def row(x, y):
        if y < 0:
            at = (x * 3 + y + 3) * 32
            return got_lo_ref[at : at + 32, :]
        if y > 23:
            at = (x * 3 + y - 24) * 32
            return got_hi_ref[at : at + 32, :]
        return wide_ref[x, y, 32:64, :]

    for x in range(6):
        v = jnp.concatenate([row(x, -1), row(x, 24)], axis=0).astype(F32)
        parts = shifts(v, 128)
        for a in range(3):
            rim_ref[x, :, a * 32 : a * 32 + 32, :] = parts[a].astype(BF16).reshape(2, 32, 128)
    outs = [dot(wskip, stack_of(lambda x, r=r: rim_ref[x, r])) for r in range(2)]
    for x in range(4):
        at = slice(x * 128, x * 128 + 128)
        edge_ref[x, 0] = outs[0][64:96, at]
        edge_ref[x, 1] = outs[1][0:32, at]

    for i, (left, right) in enumerate(((-1, 1), (19, 21), (23, -3))):

        def rows_of(x, j):
            return jnp.concatenate([row(x, left + j), row(x, right + j)], axis=1)

        def put_window(bx, r, v):
            lane = (bx * 3 + i) * 128
            win_ref[r : r + 32, lane : lane + 128] = v

        window_sums(rows_of, pool_ref[...], put_window)
    rim_up = dot_tn(w_ref[...].reshape(864, 96), win_ref[...])[:64]

    upper = lane_ids((64, 128)) >= 64
    before = got_lo_ref[576:640, :].astype(F32)
    after = got_hi_ref[576:640, :].astype(F32)
    rim_tilt = (
        jnp.where(upper, pltpu.roll(before, 64, 1), after),
        jnp.where(upper, before, pltpu.roll(after, 64, 1)),
    )
    for bx in range(2):
        for m in range(7):
            if 1 <= m <= 4:
                lane = (bx * 4 + m - 1) * 128
                v = up_ref[:, lane : lane + 128]
            else:
                lane = (bx * 3 + (0, 5, 6).index(m)) * 128
                v = rim_up[:, lane : lane + 128]
            tilt = rim_tilt[bx] if m == 6 else mslope_ref[bx, m]
            delta = (v * tilt).astype(BF16).astype(F32)
            lane = (bx * 7 + m) * 128
            for a, part in enumerate(shifts(delta, 64)):
                mid_ref[a * 64 : a * 64 + 64, lane : lane + 128] = part.astype(BF16)

    out = dot(wm_ref[...], mid_ref[...])
    total_ref[...] = jnp.zeros(total_ref.shape, F32)
    upper = lane_ids((32, 128)) >= 64
    for bx in range(2):
        for m in range(7):
            col = (bx * 7 + m) * 128
            for a in range(3):
                parts = [out[(a * 3 + b) * 32 : (a * 3 + b) * 32 + 32, col : col + 128] for b in range(3)]
                down = pltpu.roll(parts[0], 64, 1)
                up = pltpu.roll(parts[2], 64, 1)
                total_ref[bx + a, (m + 6) % 7] += jnp.where(upper, down, 0.0)
                total_ref[bx + a, m] += parts[1] + jnp.where(upper, up, down)
                total_ref[bx + a, (m + 1) % 7] += jnp.where(upper, 0.0, up)
    back_ref[...] = total_ref[1:3, 0:6]
    before = got_lo_ref[640:672, :].astype(F32)
    after = got_hi_ref[640:672, :].astype(F32)
    for x, face_ref, side_ref in ((0, face_lo_ref, pool_lo_ref), (3, face_hi_ref, pool_hi_ref)):
        face_ref[0:192, :] = total_ref[x, 0:6].astype(BF16).reshape(192, 128)
        face_ref[192:384, :] = side_ref[...]
        rows = (before[x * 8 : x * 8 + 8], st_ref[x].reshape(192, 128), after[x * 8 : x * 8 + 8])
        face_ref[384:592, :] = jnp.concatenate(rows, axis=0).astype(BF16)


def hidden_rows(hid_ref, ys):
    def tap(x, y):
        return hid_ref[x, y + 2]

    return jnp.concatenate(
        [jnp.concatenate([tap(x, y + b - 1) for y in ys for x in range(4)], axis=1) for b in range(3)], axis=0
    )


def pooled_taps(blocks):
    blocks = blocks + [jnp.zeros((32, 128), F32)]
    lower = lane_ids((32, 128)) < 64
    turned = [pltpu.roll(v, 64, 1) for v in blocks]
    taps = (
        [jnp.where(lower, turned[(m + 6) % 7], turned[m]) for m in range(7)],
        blocks,
        [jnp.where(lower, turned[m], turned[(m + 1) % 7]) for m in range(7)],
    )
    return jnp.concatenate([jnp.concatenate(v, axis=1) for v in taps], axis=0).astype(BF16)


def dec_grad_body(
    wide_ref, rim_ref, hid_ref, win_ref, rim_win_ref, hmid_ref, head_ref, pooled_ref, mid_ref,
    rows_ref, gmid_ref, hpad_ref, skip_ref,
):
    blank = jnp.zeros((2, 32, 128), BF16)
    for x in range(4):
        hpad_ref[x, 0:2] = blank
        hpad_ref[x, 26:28] = blank
        hpad_ref[x, 2:26] = hid_ref[x]
    rims = jnp.concatenate([stack_of(lambda x, r=r: rim_ref[x, r]) for r in (0, 1)], axis=1)
    skip_ref[...] = dot_nt(rims, hidden_rows(hpad_ref, (-1, 24)))

    def step(i, carry):
        y = 4 * i
        rows = jnp.concatenate([stack_of(lambda x, j=j: wide_ref[x, y + j]) for j in range(4)], axis=1)
        skip_ref[...] += dot_nt(rows, hidden_rows(hpad_ref, [y + j for j in range(4)]))
        return carry

    lax.fori_loop(0, 6, step, 0)
    rows_ref[0:288, :] = jnp.concatenate([skip_ref[...], jnp.zeros((288, 32), F32)], axis=1).astype(BF16)

    def side(bx, m):
        if 1 <= m <= 4:
            at = (bx * 4 + m - 1) * 128
            return win_ref[:, at : at + 128]
        at = (bx * 3 + (0 if m == 0 else 1)) * 128
        return rim_win_ref[:, at : at + 128]

    order = [(bx, m) for bx in range(2) for m in range(6)]
    windows = jnp.concatenate([side(bx, m) for bx, m in order], axis=1)
    hmid = jnp.concatenate([hmid_ref[bx, m] for bx, m in order], axis=1)
    lift = dot_nt(windows, hmid)
    rows_ref[288:720, :] = jnp.concatenate([lift[0:432], lift[432:864]], axis=1).astype(BF16)
    rows_ref[720:736, :] = jnp.concatenate(
        [jnp.concatenate([head_ref[...], jnp.zeros((8, 96), F32)], axis=1), jnp.zeros((8, 128), F32)], axis=0
    ).astype(BF16)
    taps = [pooled_taps([pooled_ref[bx, m].astype(F32) for m in range(6)]) for bx in range(2)]
    first, second = mid_ref[:, 0:896], mid_ref[:, 896:1792]
    gmid_ref[0:96, :] = dot_nt(taps[0], second)
    gmid_ref[96:192, :] = dot_nt(taps[0], first) + dot_nt(taps[1], second)
    gmid_ref[192:288, :] = dot_nt(taps[1], first)


def encoder_body(
    acc_ref, edge_ref, back_ref, rim_lo_ref, rim_hi_ref, got_lo_ref, got_hi_ref, slope_ref, w_ref, up_ref,
    mid_ref, gmid_ref, st_ref, dec_ref,
    rows_far, own_ref, face_lo_ref, face_hi_ref, edge_lo_ref, edge_hi_ref,
    enc_ref, total_ref, we_ref, rows_ref, sext_ref, sum_ref, sems,
):
    writes = fetch([(dec_ref, rows_far.at[0:736])], sems.at[0])

    def beyond(ref):
        side = ref[192:384, :].astype(F32)
        return pooled_taps([side[m * 32 : m * 32 + 32] for m in range(6)])

    gmid = jnp.concatenate(
        [
            gmid_ref[0:96, :] + dot_nt(beyond(got_lo_ref), mid_ref[:, 0:896]),
            gmid_ref[96:192, :],
            gmid_ref[192:288, :] + dot_nt(beyond(got_hi_ref), mid_ref[:, 896:1792]),
        ],
        axis=0,
    )
    rows_ref[0:288, :] = gmid[:, :128].astype(BF16)
    rows_ref[288:432, :] = jnp.concatenate([gmid[:144, 128:], gmid[144:, 128:]], axis=1).astype(BF16)
    writes += fetch([(rows_ref.at[0:432], rows_far.at[736:1168])], sems.at[1])

    sext_ref[1:5, 1:25] = st_ref[...]
    sext_ref[0] = got_lo_ref[384:592, :].astype(F32).reshape(26, 8, 128)
    sext_ref[5] = got_hi_ref[384:592, :].astype(F32).reshape(26, 8, 128)
    before = rim_lo_ref[640:672, :].astype(F32)
    after = rim_hi_ref[640:672, :].astype(F32)
    for x in range(4):
        sext_ref[x + 1, 0] = before[x * 8 : x * 8 + 8]
        sext_ref[x + 1, 25] = after[x * 8 : x * 8 + 8]

    for bx in range(2):
        for m in range(6):
            whole = back_ref[bx, m]
            whole = whole + (got_lo_ref if bx == 0 else got_hi_ref)[m * 32 : m * 32 + 32, :].astype(F32)
            whole = whole * 0.125
            high = whole.astype(BF16)
            low = (whole - high.astype(F32)).astype(BF16)
            wide = dot(jnp.concatenate([high, low], axis=1), up_ref[...])
            for half in range(2):
                fine = wide[:, half * 128 : half * 128 + 128]
                for ey in range(2):
                    y = 4 * m + 2 * half + ey
                    for ex in range(2):
                        x = 2 * bx + ex
                        sum_in = acc_ref[x, y + 1] + fine
                        if y in (0, 23):
                            sum_in = sum_in + edge_ref[x, (0, 23).index(y)]
                        delta = (sum_in * slope_ref[x, y]).astype(BF16).astype(F32)
                        lane = (y * 4 + x) * 128
                        for c, part in enumerate(shifts(delta, 128)):
                            enc_ref[c * 32 : c * 32 + 32, lane : lane + 128] = part.astype(BF16)

    for a in range(3):
        for b in range(3):
            at = (a * 3 + b) * 8
            we_ref[at : at + 8, :] = jnp.concatenate([w_ref[a, b, c].astype(F32) for c in range(3)], axis=1)
    w = we_ref[...].astype(BF16)
    total_ref[...] = jnp.zeros(total_ref.shape, F32)
    sum_ref[...] = jnp.zeros(sum_ref.shape, F32)

    def step(i, carry):
        y = 4 * i
        delta = enc_ref[:, pl.ds(pl.multiple_of(y * 512, 2048), 2048)]
        state = jnp.concatenate(
            [
                jnp.concatenate([sext_ref[x + a, y + j + b] for j in range(4) for x in range(4)], axis=1)
                for a in range(3)
                for b in range(3)
            ],
            axis=0,
        ).astype(BF16)
        sum_ref[...] += dot_nt(state, delta)
        out = dot(w, delta)
        for x in range(6):
            for r in range(6):
                parts = []
                for a in range(3):
                    for b in range(3):
                        j, own = r - b, x - a
                        if 0 <= j < 4 and 0 <= own < 4:
                            row, lane = (a * 3 + b) * 8, (j * 4 + own) * 128
                            parts.append(out[row : row + 8, lane : lane + 128])
                total_ref[x, y + r] += sum(parts[1:], parts[0])
        return carry

    lax.fori_loop(0, 6, step, 0)
    genc = jnp.concatenate([sum_ref[...], jnp.zeros((72, 32), F32)], axis=1)
    rows_ref[432:544, :] = jnp.concatenate([genc, jnp.zeros((40, 128), F32)], axis=0).astype(BF16)
    writes += fetch([(rows_ref.at[432:544], rows_far.at[1168:1280])], sems.at[2])
    own_ref[...] = total_ref[1:5, 1:25]
    face_lo_ref[...] = total_ref[0].reshape(208, 128).astype(BF16)
    face_hi_ref[...] = total_ref[5].reshape(208, 128).astype(BF16)
    edge_lo_ref[...] = total_ref[1:5, 0]
    edge_hi_ref[...] = total_ref[1:5, 25]
    for wait in writes:
        wait()


def corner_body(edge_lo_ref, edge_hi_ref, lo_ref, hi_ref, col_lo_ref, col_hi_ref):
    before = lo_ref[...].astype(F32)
    after = hi_ref[...].astype(F32)
    for edge_ref, at, col_ref in ((edge_lo_ref, 0, col_lo_ref), (edge_hi_ref, 200, col_hi_ref)):
        rows = [edge_ref[0] + before[at : at + 8], edge_ref[1], edge_ref[2], edge_ref[3] + after[at : at + 8]]
        col_ref[...] = jnp.concatenate(rows, axis=0).astype(BF16)


def final_body(cot_ref, own_ref, lo_ref, hi_ref, ylo_ref, yhi_ref, grad_ref):
    before = ylo_ref[...].astype(F32)
    after = yhi_ref[...].astype(F32)
    for x in range(4):
        total = own_ref[x]
        if x in (0, 3):
            side = (lo_ref if x == 0 else hi_ref)[...].astype(F32)
            total = total + side[8:200].reshape(24, 8, 128)
        at = slice(x * 8, x * 8 + 8)
        ends = [before[at][None], jnp.zeros((22, 8, 128), F32), after[at][None]]
        total = total + jnp.concatenate(ends, axis=0)
        grad_ref[:, x] = (cot_ref[:, x].astype(F32) + jnp.swapaxes(total, 0, 1)).astype(BF16)


def share_body(pieces_far, out_far, pieces_ref, copies_ref, sems, out_sems):
    count = pieces_ref.shape[0]
    part = count // 4
    spans = [pl.ds(i * part, part) for i in range(4)]
    waits = fetch([(pieces_far.at[span], pieces_ref.at[span]) for span in spans], sems)
    total = jnp.zeros(pieces_ref.shape[1:], F32)
    for i, wait in enumerate(waits):
        wait()
        for j in range(part):
            total = total + pieces_ref[i * part + j].astype(F32)
    total = total.astype(BF16)
    part = copies_ref.shape[0]
    for j in range(part):
        copies_ref[j] = total
    for wait in fetch([(copies_ref, out_far.at[pl.ds(i * part, part)]) for i in range(count // part)], out_sems):
        wait()


def unpack_body(scale, rows_ref, enc_ref, mid_ref, dec_ref, head_ref):
    def rows(at, count):
        return rows_ref[at : at + count, :].astype(F32) * scale

    skip = [rows(i * 32, 32) for i in range(9)]
    head_ref[...] = rows(720, 16)[:8, :32]
    mid_rest = [rows(1024 + i * 48, 48) for i in range(3)]
    mid_rest = jnp.concatenate(mid_rest, axis=0)
    mid_rest = jnp.concatenate([mid_rest[:, :64], mid_rest[:, 64:]], axis=0)
    enc = rows(1168, 80)
    lift = rows(288, 432)
    lift = jnp.concatenate([lift[:, :64], lift[:, 64:]], axis=0)
    for a in range(3):
        for b in range(3):
            tap = a * 3 + b
            pair = rows(736 + tap * 32, 32)
            mid_ref[a, b, 0] = pair[:, :64]
            mid_ref[a, b, 1] = pair[:, 64:]
            mid_ref[a, b, 2] = mid_rest[tap * 32 : tap * 32 + 32]
            for c in range(3):
                enc_ref[a, b, c] = enc[tap * 8 : tap * 8 + 8, c * 32 : c * 32 + 32]
                at = (tap * 3 + c) * 32
                dec_ref[a, b, c] = jnp.concatenate(
                    [lift[at : at + 32], skip[a * 3 + c][:, b * 32 : b * 32 + 32]], axis=1
                )


def pool_matrix():
    table = np.zeros((256, 3, 128), np.float32)
    for c, k in enumerate((-1, 0, 1)):
        for half in range(2):
            for q in range(64):
                for e in range(2):
                    z = 2 * q + e - k
                    if 0 <= z < 128:
                        table[half * 128 + z, c, half * 64 + q] = 1.0
    return jnp.asarray(table.reshape(256, 384), BF16)


def up_matrix():
    table = np.zeros((2, 128, 256), np.float32)
    for half in range(2):
        for z in range(128):
            table[:, half * 64 + z // 2, half * 128 + z] = 1.0
    return jnp.asarray(table.reshape(256, 256), BF16)


def both_ways(low, high, axis):
    ends = lax.axis_size(axis) - 1
    from_before = lax.ppermute(high, axis, [(i, i + 1) for i in range(ends)])
    from_after = lax.ppermute(low, axis, [(i + 1, i) for i in range(ends)])
    return from_before, from_after


def on_device(
    state_now, enc_pre, mid_pre, dec_pre, cotangent, enc_kernel, mid_kernel, dec_kernel, out_kernel
):
    state_now, enc_pre, mid_pre, dec_pre, cotangent = (
        v[0] for v in (state_now, enc_pre, mid_pre, dec_pre, cotangent)
    )
    cells = state_now[0].size * lax.axis_size("gx") * lax.axis_size("gy") * lax.axis_size("dp")
    grad_scale = 1.0 / math.sqrt(cells)
    pool = pool_matrix()
    dec_w = dec_kernel.transpose(2, 3, 4, 0, 1)
    mid_w = mid_kernel.transpose(2, 3, 4, 1, 0)
    enc_w = enc_kernel.transpose(2, 3, 4, 1, 0)

    plane = sds((24, 32, 128), BF16)
    delta_lo, delta_hi = call(
        face_body,
        [plane, plane],
        [
            pltpu.VMEM((2, 32, 24, 128), BF16),
            pltpu.VMEM((2, 8, 24, 128), BF16),
            pltpu.VMEM((8, 32), BF16),
            pltpu.VMEM((2, 24, 32, 128), BF16),
            pltpu.SemaphoreType.DMA((5,)),
            pltpu.SemaphoreType.DMA((2, 1)),
        ],
        (dec_pre, cotangent, out_kernel),
        200 << 20, 56, far=3, far_outs=2,
    )
    xlo, xhi = both_ways(delta_lo, delta_hi, "gx")
    mid_blocks = mid_pre.reshape(64, 2, 6, 2, 64).transpose(1, 2, 0, 3, 4).reshape(2, 6, 64, 128)
    (
        delta, head_grad, hidden, enc_slope, pooled, hidden_mid, mid_slope, state,
        tail_lo, tail_hi, pool_lo, pool_hi,
    ) = call(
        forward_body,
        [
            sds((2, 24, 32, 128), BF16),
            sds((8, 32), F32),
            sds((4, 24, 32, 128), BF16),
            sds((4, 24, 32, 128), F32),
            sds((2, 6, 32, 128), BF16),
            sds((2, 6, 64, 128), BF16),
            sds((2, 6, 64, 128), F32),
            sds((4, 24, 8, 128), F32),
            sds((96, 128), BF16),
            sds((96, 128), BF16),
            sds((192, 128), BF16),
            sds((192, 128), BF16),
        ],
        [],
        (dec_pre, cotangent, out_kernel, enc_pre, state_now, mid_blocks, pool),
        600 << 20, 16,
    )

    def column(at, tail):
        rows = (xlo[at], delta_lo[at], delta[0, at], delta[1, at], delta_hi[at], xhi[at], tail)
        return jnp.concatenate([v.reshape(-1, 128) for v in rows])

    ylo, yhi = both_ways(column(slice(0, 3), tail_lo), column(slice(21, 24), tail_hi), "gy")
    acc, wide, win, up, wskip, wmid = call(
        inner_body,
        [
            sds((4, 26, 32, 128), F32),
            sds((6, 24, 96, 128), BF16),
            sds((864, 1024), BF16),
            sds((64, 1024), F32),
            sds((96, 288), BF16),
            sds((288, 192), BF16),
        ],
        [],
        (xlo, delta_lo, delta, delta_hi, xhi, pool, dec_w, mid_w),
        3 << 30, 24,
    )
    edge, rim_wide, rim_win, mid_wide, back, face_lo, face_hi = call(
        outer_body,
        [
            sds((4, 2, 32, 128), F32),
            sds((6, 2, 96, 128), BF16),
            sds((864, 768), BF16),
            sds((192, 1792), BF16),
            sds((2, 6, 32, 128), F32),
            sds((592, 128), BF16),
            sds((592, 128), BF16),
        ],
        [pltpu.VMEM((4, 7, 32, 128), F32)],
        (ylo, yhi, wide, up, mid_slope, state, pool_lo, pool_hi, pool, dec_w, wskip, wmid),
        1 << 30, 24,
    )
    got_lo, got_hi = both_ways(face_lo, face_hi, "gx")
    dec_rows, mid_grad = call(
        dec_grad_body,
        [sds((736, 128), BF16), sds((288, 192), F32)],
        [pltpu.VMEM((4, 28, 32, 128), BF16), pltpu.VMEM((288, 96), F32)],
        (wide, rim_wide, hidden, win, rim_win, hidden_mid, head_grad, pooled, mid_wide),
        3 << 30, 20,
    )
    dec_rows, mid_grad, got_lo, got_hi = lax.optimization_barrier((dec_rows, mid_grad, got_lo, got_hi))
    rows, own, face_lo, face_hi, edge_lo, edge_hi = call(
        encoder_body,
        [
            sds((1280, 128), BF16),
            sds((4, 24, 8, 128), F32),
            sds((208, 128), BF16),
            sds((208, 128), BF16),
            sds((4, 8, 128), F32),
            sds((4, 8, 128), F32),
        ],
        [
            pltpu.VMEM((96, 24 * 512), BF16),
            pltpu.VMEM((6, 26, 8, 128), F32),
            pltpu.VMEM((72, 96), F32),
            pltpu.VMEM((544, 128), BF16),
            pltpu.VMEM((6, 26, 8, 128), F32),
            pltpu.VMEM((72, 96), F32),
            pltpu.SemaphoreType.DMA((3, 1)),
        ],
        (
            acc, edge, back, ylo, yhi, got_lo, got_hi, enc_slope, enc_w, up_matrix(),
            mid_wide, mid_grad, state, dec_rows,
        ),
        2 << 30, 24, far_outs=1,
    )
    last_lo, last_hi = both_ways(face_lo, face_hi, "gx")

    axes = ("dp", "gx", "gy")
    count = lax.axis_size(axes)
    share = 1280 // count // 2
    pieces = lax.all_to_all(rows.reshape(count, share, 2, 128), axes, 0, 0)
    (shares,) = call(
        share_body,
        [sds(pieces.shape, BF16)],
        [
            pltpu.VMEM(pieces.shape, BF16),
            pltpu.VMEM((count // 8,) + pieces.shape[1:], BF16),
            pltpu.SemaphoreType.DMA((4,)),
            pltpu.SemaphoreType.DMA((8,)),
        ],
        (pieces,),
        1 << 20, 8, far=1, far_outs=1,
    )
    shares, last_lo, last_hi = lax.optimization_barrier((shares, last_lo, last_hi))
    rows = lax.all_to_all(shares, axes, 0, 0).reshape(1280, 128)
    col_lo, col_hi = call(
        corner_body, [sds((32, 128), BF16)] * 2, [], (edge_lo, edge_hi, last_lo, last_hi), 1 << 16, 4
    )
    end_lo, end_hi = both_ways(col_lo, col_hi, "gy")
    genc, gmid, gdec, ghead = call(
        functools.partial(unpack_body, grad_scale),
        [sds((3, 3, 3, 8, 32), F32), sds((3, 3, 3, 32, 64), F32), sds((3, 3, 3, 32, 96), F32), sds((8, 32), F32)],
        [],
        (rows,),
        1 << 20, 12,
    )
    genc, end_lo, end_hi = lax.optimization_barrier((genc, end_lo, end_hi))
    (state_grad,) = call(
        final_body,
        [sds((8, 4, 24, 128), BF16)],
        [],
        (cotangent, own, last_lo, last_hi, end_lo, end_hi),
        1 << 20, 8,
    )
    return (
        state_grad[None],
        genc.transpose(4, 3, 0, 1, 2),
        gmid.transpose(4, 3, 0, 1, 2),
        gdec.transpose(3, 4, 0, 1, 2),
        ghead,
    )


def solution(mesh):
    grid = P("dp", None, "gx", "gy", None)
    return jax.shard_map(
        on_device,
        mesh=mesh,
        in_specs=(grid,) * 5 + (P(),) * 4,
        out_specs=(grid, P(), P(), P(), P()),
        check_vma=False,
    )
```

time: 555 us -> 94.7 us (0.17); the launches traced: 548 us -> 94.1 us
  local copies, waits for them, and re-layouts: 124 us -> 2.49 us
  waiting for transfers between devices: 138 us -> 20.1 us
  matrix products: 78.3 us -> 0 us
  blocking collectives: 70.2 us -> 0 us
  other arithmetic: 47 us -> 0 us
  starting transfers between devices: 75.6 us -> 47.3 us
  Pallas kernels: 0 us -> 23.1 us
  between operations: 15.2 us -> 1.09 us
    psum x1 -> x0, waiting for transfers between devices: 120 us -> none  [on_device(): lax.psum((enc_term, mid_term, dec_term, out_term), ('dp', 'gx', 'gy'))]
    conv_general_dilated x15 -> x0, local copies, waits for them, and re-layouts: 80.3 us -> none  [apply_conv(): lax.conv_general_dilated(values, kernel, (1, 1, 1), pads, dimension_numbe...]
    psum x1 -> x0, blocking collectives: 70.2 us -> none  [on_device(): lax.psum((enc_term, mid_term, dec_term, out_term), ('dp', 'gx', 'gy'))]
    ppermute x24 -> x10, starting transfers between devices: 75.6 us -> 28.3 us  [the longest x5 21.9 us: both_ways(): from_before = lax.ppermute(high, axis, [(i, i + 1) for i in range(ends)])]
    dot_general x83 -> x0, matrix products: 46.1 us -> none  [the longest x81 43.3 us: values_rim_grad(): jnp.einsum('bixyz,boxyz->oi', piece, delta, preferred_element_type=jnp.fl...]
    conv_general_dilated x3 -> x0, matrix products: 32.2 us -> none  [apply_conv(): lax.conv_general_dilated(values, kernel, (1, 1, 1), pads, dimension_numbe...]
    pallas_call x0 -> x10, Pallas kernels: none -> 23.1 us  [call(): pl.pallas_call(body, out_shape=outs, in_specs=[HBM] * far + [VMEM] * (len...]
    concatenate x9 -> x0, other arithmetic: 20.3 us -> none  [the longest x8 20.3 us: padded(): jnp.concatenate([lax.ppermute(tail, axis, [(i, (i + 1) % count) for i in...]
  transfers between devices with their start and end apart: 25 -> 12, of which waited for: 6 -> 5; matrix products, arithmetic and copies ran while one was open for 22% -> 3% of each run, Pallas kernels for 0% -> 15%
where the time goes in v1:
time: 94.7 us; the launch traced here: 94.1 us
  starting transfers between devices  47.3 us (50%)
  Pallas kernels  23.1 us (24%)
  waiting for transfers between devices  20.1 us (21%)
  local copies, waits for them, and re-layouts  2.49 us (3%)
  between operations  1.09 us (1%)
    pallas_call x10, Pallas kernels, call(): pl.pallas_call(body, out_shape=outs, in_specs=[HBM] * far + [VMEM] * (len...  23.1 us
    ppermute x5, starting transfers between devices, both_ways(): from_before = lax.ppermute(high, axis, [(i, i + 1) for i in range(ends)])  21.9 us
    all_to_all x1, starting transfers between devices, on_device(): pieces = lax.all_to_all(rows.reshape(count, share, 2, 128), axes, 0, 0)  12.5 us
    all_to_all x1, waiting for transfers between devices, on_device(): pieces = lax.all_to_all(rows.reshape(count, share, 2, 128), axes, 0, 0)  7.24 us
    ppermute x5, starting transfers between devices, both_ways(): from_after = lax.ppermute(low, axis, [(i + 1, i) for i in range(ends)])  6.46 us
    all_to_all x1, starting transfers between devices, on_device(): rows = lax.all_to_all(shares, axes, 0, 0).reshape(1280, 128)  6.44 us
    ppermute x5, waiting for transfers between devices, both_ways(): from_after = lax.ppermute(low, axis, [(i + 1, i) for i in range(ends)])  6.08 us
    all_to_all x1, waiting for transfers between devices, on_device(): rows = lax.all_to_all(shares, axes, 0, 0).reshape(1280, 128)  5.45 us
  transfers between devices with their start and end apart: 12, of which 5 were waited for; matrix products, arithmetic and copies ran while one was open for 3% of the time, Pallas kernels for 15%

profile of v1, /device:TPU:1, one launch (start us, length us, event | category | flops | bytes accessed | tf_op | source)
XLA Modules:
  0.0 94.1 jit_solution(13391125905280237811)
XLA Ops:
  0.7 2.5 %shard_map.146 = (bf16[24,32,128]{2,1,0:T(8,128)(2,1)}, bf16[24,32,128]{2,1,0:T(8,128)(2,1)}) custom-call(bf16[32,4,24,128]{3,2,1,0:T(8,128)(2,1)} %bitcast.29, bf16[8,4,24,128]{3,2,1,0:T(8,128)(2,1)} %bitcast.31, bf16[8,32]{1,0:T(8,128)(2,1)} %head_ref.1), custom_call_target="tpu_custom_call" | custom-call | flops 209715200 | bytes 4194304 | tf_op jit(solution)/shard_map/pallas_call | solution.py:21
  3.2 4.4 %collective-permute-start = (bf16[24,32,128]{2,1,0:T(8,128)(2,1)}, bf16[24,32,128]{2,1,0:T(8,128)(2,1)S(1)}, u32[]{:S(2)}, u32[]{:S(2)}) collective-permute-start(bf16[24,32,128]{2,1,0:T(8,128)(2,1)} %get-tuple-element.56.high_ref), channel_id=1, source_target_pairs={{0,8},{8,16},{16,24},{24,32},{32,40},{40,48},{48,56},{1,9},{9,17},... | collective-permute-start | bytes 589832 | tf_op jit(solution)/shard_map/ppermute | solution.py:568
  7.6 1.3 %collective-permute-start.1 = (bf16[24,32,128]{2,1,0:T(8,128)(2,1)}, bf16[24,32,128]{2,1,0:T(8,128)(2,1)S(1)}, u32[]{:S(2)}, u32[]{:S(2)}) collective-permute-start(bf16[24,32,128]{2,1,0:T(8,128)(2,1)} %get-tuple-element.57.low_ref), channel_id=1, source_target_pairs={{8,0},{16,8},{24,16},{32,24},{40,32},{48,40},{56,48},{9,1},{17,9},... | collective-permute-start | bytes 589832 | tf_op jit(solution)/shard_map/ppermute | solution.py:569
  11.3 2.3 %shard_map.147 = (bf16[2,24,32,128]{3,2,1,0:T(8,128)(2,1)S(1)}, f32[8,32]{1,0:T(8,128)S(1)}, bf16[4,24,32,128]{3,2,1,0:T(8,128)(2,1)S(1)}, f32[4,24,32,128]{3,2,...) custom-call(bf16[32,4,24,128]{3,2,1,0:T(8,128)(2,1)S(1)} %bitcast.30, ...), custom_call_target="tpu_custom_call" | custom-call | flops 629145600 | bytes 4194304 | tf_op jit(solution)/shard_map/pallas_call | solution.py:21
  13.7 1.5 %collective-permute-done.1.xhi_ref = bf16[24,32,128]{2,1,0:T(8,128)(2,1)S(1)} collective-permute-done((bf16[24,32,128]{2,1,0:T(8,128)(2,1)}, bf16[24,32,128]{2,1,0:T(8,128)(2,1)S(1)}, u32[]{:S(2)}, u32[]{:S(2)}) %collective-permute-start.1) | collective-permute-done | bytes 196640 | tf_op jit(solution)/shard_map/ppermute | solution.py:569
  15.1 1.3 %collective-permute-start.3 = (bf16[672,128]{1,0:T(8,128)(2,1)S(1)}, bf16[672,128]{1,0:T(8,128)(2,1)S(1)}, u32[]{:S(2)}, u32[]{:S(2)}) collective-permute-start(bf16[672,128]{1,0:T(8,128)(2,1)S(1)} %constant_dynamic-update-slice_fusion.7), channel_id=1, source_target_pairs={{1,0},{2,1},{3,2},{4,3},{5,4},{6,5},{7,6},{9,8},{10,9},{11,10},{12... | collective-permute-start | bytes 516104 | tf_op jit(solution)/shard_map/ppermute | solution.py:569
  16.5 5.8 %collective-permute-start.2 = (bf16[672,128]{1,0:T(8,128)(2,1)S(1)}, bf16[672,128]{1,0:T(8,128)(2,1)S(1)}, u32[]{:S(2)}, u32[]{:S(2)}) collective-permute-start(bf16[672,128]{1,0:T(8,128)(2,1)S(1)} %constant_dynamic-update-slice_fusion), channel_id=1, source_target_pairs={{0,1},{1,2},{2,3},{3,4},{4,5},{5,6},{6,7},{8,9},{9,10},{10,11},{11... | collective-permute-start | bytes 516104 | tf_op jit(solution)/shard_map/ppermute | solution.py:568
  22.4 4.8 %shard_map.148 = (f32[4,26,32,128]{3,2,1,0:T(8,128)S(1)}, bf16[6,24,96,128]{3,2,1,0:T(8,128)(2,1)S(1)}, bf16[864,1024]{1,0:T(8,128)(2,1)S(1)}, f32[64,1024]{1,0:...) custom-call(bf16[24,32,128]{2,1,0:T(8,128)(2,1)S(1)} %collective-permute-done.xlo_ref, ...), custom_call_target="tpu_custom_call" | custom-call | flops 3221225472 | bytes 4194304 | tf_op jit(solution)/shard_map/pallas_call | solution.py:21
  27.2 1.4 %collective-permute-done.2.got_lo_ref.rim_lo_ref = bf16[672,128]{1,0:T(8,128)(2,1)S(1)} collective-permute-done((bf16[672,128]{1,0:T(8,128)(2,1)S(1)}, bf16[672,128]{1,0:T(8,128)(2,1)S(1)}, u32[]{:S(2)}, u32[]{:S(2)}) %collective-permute-start.2) | collective-permute-done | bytes 172064 | tf_op jit(solution)/shard_map/ppermute | solution.py:568
  28.6 1.9 %shard_map.149 = (f32[4,2,32,128]{3,2,1,0:T(8,128)S(1)}, bf16[6,2,96,128]{3,2,1,0:T(8,128)(2,1)S(1)}, bf16[864,768]{1,0:T(8,128)(2,1)S(1)}, bf16[192,1792]{1,0:T...) custom-call(bf16[672,128]{1,0:T(8,128)(2,1)S(1)} %collective-permute-don, ...), custom_call_target="tpu_custom_call" | custom-call | flops 1073741824 | bytes 4194304 | tf_op jit(solution)/shard_map/pallas_call | solution.py:21
  30.4 3.0 %collective-permute-start.4 = (bf16[592,128]{1,0:T(8,128)(2,1)S(1)}, bf16[592,128]{1,0:T(8,128)(2,1)S(1)}, u32[]{:S(2)}, u32[]{:S(2)}) collective-permute-start(bf16[592,128]{1,0:T(8,128)(2,1)S(1)} %get-tuple-element.82), channel_id=1, source_target_pairs={{0,8},{8,16},{16,24},{24,32},{32,40},{40,48},{48,56},{1,9},{9,17},... | collective-permute-start | bytes 454664 | tf_op jit(solution)/shard_map/ppermute | solution.py:568
  33.5 1.3 %collective-permute-start.5 = (bf16[592,128]{1,0:T(8,128)(2,1)S(1)}, bf16[592,128]{1,0:T(8,128)(2,1)S(1)}, u32[]{:S(2)}, u32[]{:S(2)}) collective-permute-start(bf16[592,128]{1,0:T(8,128)(2,1)S(1)} %get-tuple-element.83), channel_id=1, source_target_pairs={{8,0},{16,8},{24,16},{32,24},{40,32},{48,40},{56,48},{9,1},{17,9},... | collective-permute-start | bytes 454664 | tf_op jit(solution)/shard_map/ppermute | solution.py:569
  34.8 4.5 %shard_map.150 = (bf16[736,128]{1,0:T(8,128)(2,1)S(1)}, f32[288,192]{1,0:T(8,128)S(1)}) custom-call(bf16[6,24,96,128]{3,2,1,0:T(8,128)(2,1)S(1)} %get-tuple-element.62.wide_ref, bf16[6,2,96,128]{3,2,1,0:T(8,128)(2,1)S(1)} %get-tuple-element.72.rim_ref, bf16[4,24,32,128]{3,2,1,0:T(8,128)(2,1)S(1)} %get-tuple-element.73.hid_ref, ...), custom_call_target="tpu_custom_call" | custom-call | flops 3221225472 | bytes 4194304 | tf_op jit(solution)/shard_map/pallas_call | solution.py:21
  39.3 4.6 %collective-permute-done.5.got_hi_ref = bf16[592,128]{1,0:T(8,128)(2,1)S(1)} collective-permute-done((bf16[592,128]{1,0:T(8,128)(2,1)S(1)}, bf16[592,128]{1,0:T(8,128)(2,1)S(1)}, u32[]{:S(2)}, u32[]{:S(2)}) %collective-permute-start.5) | collective-permute-done | bytes 151584 | tf_op jit(solution)/shard_map/ppermute | solution.py:569
  44.0 3.8 %shard_map.151 = (bf16[1280,128]{1,0:T(8,128)(2,1)}, f32[4,24,8,128]{3,2,1,0:T(8,128)S(1)}, bf16[208,128]{1,0:T(8,128)(2,1)S(1)}, bf16[208,128]{1,0:T(8,128)(2,1...) custom-call(f32[4,26,32,128]{3,2,1,0:T(8,128)S(1)} %get-tuple-element.59.acc_ref, ...), custom_call_target="tpu_custom_call" | custom-call | flops 2147483648 | bytes 4194304 | tf_op jit(solution)/shard_map/pallas_call | solution.py:21
  47.8 12.5 %all-to-all-start = ((bf16[128,5,2,128]{3,2,1,0:T(2,128)(2,1)}), bf16[128,5,2,128]{3,2,1,0:T(2,128)(2,1)S(1)}, u32[]{:S(2)}, u32[]{:S(2)}) async-start(bf16[128,5,2,128]{3,2,1,0:T(2,128)(2,1)} %bitcast.21), calls=%async_computation | async-start | bytes 655360 | tf_op jit(solution)/shard_map/all_to_all | solution.py:700
  60.3 3.4 %collective-permute-start.6 = (bf16[208,128]{1,0:T(8,128)(2,1)S(1)}, bf16[208,128]{1,0:T(8,128)(2,1)S(1)}, u32[]{:S(2)}, u32[]{:S(2)}) collective-permute-start(bf16[208,128]{1,0:T(8,128)(2,1)S(1)} %get-tuple-element.91), channel_id=1, source_target_pairs={{0,8},{8,16},{16,24},{24,32},{32,40},{40,48},{48,56},{1,9},{9,17},... | collective-permute-start | bytes 159752 | tf_op jit(solution)/shard_map/ppermute | solution.py:568
  63.7 1.3 %collective-permute-start.7 = (bf16[208,128]{1,0:T(8,128)(2,1)S(1)}, bf16[208,128]{1,0:T(8,128)(2,1)S(1)}, u32[]{:S(2)}, u32[]{:S(2)}) collective-permute-start(bf16[208,128]{1,0:T(8,128)(2,1)S(1)} %get-tuple-element.92), channel_id=1, source_target_pairs={{8,0},{16,8},{24,16},{32,24},{40,32},{48,40},{56,48},{9,1},{17,9},... | collective-permute-start | bytes 159752 | tf_op jit(solution)/shard_map/ppermute | solution.py:569
  65.0 7.2 %all-to-all-done.pieces_far = bf16[128,5,2,128]{3,2,1,0:T(2,128)(2,1)S(1)} async-done(((bf16[128,5,2,128]{3,2,1,0:T(2,128)(2,1)}), bf16[128,5,2,128]{3,2,1,0:T(2,128)(2,1)S(1)}, u32[]{:S(2)}, u32[]{:S(2)}) %all-to-all-start) | async-done | bytes 327712 | tf_op jit(solution)/shard_map/all_to_all | solution.py:700
  72.2 1.4 %shard_map.152 = bf16[128,5,2,128]{3,2,1,0:T(2,128)(2,1)} custom-call(bf16[128,5,2,128]{3,2,1,0:T(2,128)(2,1)S(1)} %all-to-all-done.pieces_far), custom_call_target="tpu_custom_call" | custom-call | flops 1048576 | bytes 4194304 | tf_op jit(solution)/shard_map/pallas_call | solution.py:21
  73.7 6.4 %all-to-all-start.1 = ((bf16[128,5,2,128]{3,2,1,0:T(2,128)(2,1)}), bf16[128,5,2,128]{3,2,1,0:T(2,128)(2,1)S(1)}, u32[]{:S(2)}, u32[]{:S(2)}) async-start(bf16[128,5,2,128]{3,2,1,0:T(2,128)(2,1)} %shard_map.152), calls=%async_computation.1 | async-start | bytes 655360 | tf_op jit(solution)/shard_map/all_to_all | solution.py:714
  80.1 5.2 %collective-permute-start.8 = (bf16[32,128]{1,0:T(8,128)(2,1)S(1)}, bf16[32,128]{1,0:T(8,128)(2,1)S(1)}, u32[]{:S(2)}, u32[]{:S(2)}) collective-permute-start(bf16[32,128]{1,0:T(8,128)(2,1)S(1)} %get-tuple-element.99), channel_id=1, source_target_pairs={{0,1},{1,2},{2,3},{3,4},{4,5},{5,6},{6,7},{8,9},{9,10},{10,11},{11... | collective-permute-start | bytes 24584 | tf_op jit(solution)/shard_map/ppermute | solution.py:568
  85.3 1.3 %collective-permute-start.9 = (bf16[32,128]{1,0:T(8,128)(2,1)S(1)}, bf16[32,128]{1,0:T(8,128)(2,1)S(1)}, u32[]{:S(2)}, u32[]{:S(2)}) collective-permute-start(bf16[32,128]{1,0:T(8,128)(2,1)S(1)} %get-tuple-element.100), channel_id=1, source_target_pairs={{1,0},{2,1},{3,2},{4,3},{5,4},{6,5},{7,6},{9,8},{10,9},{11,10},{12... | collective-permute-start | bytes 24584 | tf_op jit(solution)/shard_map/ppermute | solution.py:569
  86.6 5.5 %all-to-all-done.1 = bf16[128,5,2,128]{3,2,1,0:T(2,128)(2,1)S(1)} async-done(((bf16[128,5,2,128]{3,2,1,0:T(2,128)(2,1)}), bf16[128,5,2,128]{3,2,1,0:T(2,128)(2,1)S(1)}, u32[]{:S(2)}, u32[]{:S(2)}) %all-to-all-start.1) | async-done | bytes 327712 | tf_op jit(solution)/shard_map/all_to_all | solution.py:714
  (54 shorter events, 4.5 us)
Async XLA Ops:
  0.6 10.5 %copy-start.2 = (bf16[256,384]{1,0:T(8,128)(2,1)S(1)}, bf16[256,384]{1,0:T(8,128)(2,1)}, u32[]{:S(2)}) copy-start(bf16[256,384]{1,0:T(8,128)(2,1)} %constant.4.clone.pool_ref) | copy-start | bytes 589828
  0.6 10.5 %copy-start.8 = (bf16[8,32]{1,0:T(8,128)(2,1)S(1)}, bf16[8,32]{1,0:T(8,128)(2,1)}, u32[]{:S(2)}) copy-start(bf16[8,32]{1,0:T(8,128)(2,1)} %head_ref.1) | copy-start | bytes 1540
  0.7 10.5 %copy-start.1 = (bf16[1,8,4,24,128]{4,3,2,1,0:T(8,128)(2,1)S(1)}, bf16[1,8,4,24,128]{4,3,2,1,0:T(8,128)(2,1)}, u32[]{:S(2)}) copy-start(bf16[1,8,4,24,128]{4,3,2,1,0:T(8,128)(2,1)} %param.15) | copy-start | bytes 589828
  0.7 10.5 %copy-start = (bf16[1,32,4,24,128]{4,3,2,1,0:T(8,128)(2,1)S(1)}, bf16[1,32,4,24,128]{4,3,2,1,0:T(8,128)(2,1)}, u32[]{:S(2)}) copy-start(bf16[1,32,4,24,128]{4,3,2,1,0:T(8,128)(2,1)} %param.14) | copy-start | bytes 2359300
  0.7 10.5 %copy-start.3 = (bf16[1,32,4,24,128]{4,3,2,1,0:T(8,128)(2,1)S(1)}, bf16[1,32,4,24,128]{4,3,2,1,0:T(8,128)(2,1)}, u32[]{:S(2)}) copy-start(bf16[1,32,4,24,128]{4,3,2,1,0:T(8,128)(2,1)} %param.12) | copy-start | bytes 2359300
  0.7 10.5 %copy-start.5 = (bf16[1,8,4,24,128]{4,3,2,1,0:T(8,128)(2,1)S(1)}, bf16[1,8,4,24,128]{4,3,2,1,0:T(8,128)(2,1)}, u32[]{:S(2)}) copy-start(bf16[1,8,4,24,128]{4,3,2,1,0:T(8,128)(2,1)} %param.11) | copy-start | bytes 589828
  3.2 10.4 %collective-permute-start = (bf16[24,32,128]{2,1,0:T(8,128)(2,1)}, bf16[24,32,128]{2,1,0:T(8,128)(2,1)S(1)}, u32[]{:S(2)}, u32[]{:S(2)}) collective-permute-start(bf16[24,32,128]{2,1,0:T(8,128)(2,1)} %get-tuple-element.56.high_ref), channel_id=1, source_target_pairs={{0,8},{8,16},{16,24},{24,32},{32,40},{40,48},{48,56},{1,9},{9,17},... | collective-permute-start | bytes 589832 | tf_op jit(solution)/shard_map/ppermute | solution.py:568
  7.6 7.6 %collective-permute-start.1 = (bf16[24,32,128]{2,1,0:T(8,128)(2,1)}, bf16[24,32,128]{2,1,0:T(8,128)(2,1)S(1)}, u32[]{:S(2)}, u32[]{:S(2)}) collective-permute-start(bf16[24,32,128]{2,1,0:T(8,128)(2,1)} %get-tuple-element.57.low_ref), channel_id=1, source_target_pairs={{8,0},{16,8},{24,16},{32,24},{40,32},{48,40},{56,48},{9,1},{17,9},... | collective-permute-start | bytes 589832 | tf_op jit(solution)/shard_map/ppermute | solution.py:569
  11.2 11.2 %copy-start.4 = (bf16[32,96,3,3,3]{1,0,4,3,2:T(8,128)(2,1)S(1)}, bf16[32,96,3,3,3]{1,0,4,3,2:T(8,128)(2,1)}, u32[]{:S(2)}) copy-start(bf16[32,96,3,3,3]{1,0,4,3,2:T(8,128)(2,1)} %param.18) | copy-start | bytes 497668
  11.2 11.2 %copy-start.6 = (bf16[24,32,128]{2,1,0:T(8,128)(2,1)S(1)}, bf16[24,32,128]{2,1,0:T(8,128)(2,1)}, u32[]{:S(2)}) copy-start(bf16[24,32,128]{2,1,0:T(8,128)(2,1)} %get-tuple-element.57.low_ref) | copy-start | bytes 589828
  11.2 11.2 %copy-start.7 = (bf16[24,32,128]{2,1,0:T(8,128)(2,1)S(1)}, bf16[24,32,128]{2,1,0:T(8,128)(2,1)}, u32[]{:S(2)}) copy-start(bf16[24,32,128]{2,1,0:T(8,128)(2,1)} %get-tuple-element.56.high_ref) | copy-start | bytes 589828
  11.3 11.2 %copy-start.9 = (bf16[64,32,3,3,3]{0,1,4,3,2:T(8,128)(2,1)S(1)}, bf16[64,32,3,3,3]{0,1,4,3,2:T(8,128)(2,1)}, u32[]{:S(2)}) copy-start(bf16[64,32,3,3,3]{0,1,4,3,2:T(8,128)(2,1)} %param.17) | copy-start | bytes 331780
  15.1 12.1 %collective-permute-start.3 = (bf16[672,128]{1,0:T(8,128)(2,1)S(1)}, bf16[672,128]{1,0:T(8,128)(2,1)S(1)}, u32[]{:S(2)}, u32[]{:S(2)}) collective-permute-start(bf16[672,128]{1,0:T(8,128)(2,1)S(1)} %constant_dynamic-update-slice_fusion.7), channel_id=1, source_target_pairs={{1,0},{2,1},{3,2},{4,3},{5,4},{6,5},{7,6},{9,8},{10,9},{11,10},{12... | collective-permute-start | bytes 516104 | tf_op jit(solution)/shard_map/ppermute | solution.py:569
  16.5 12.0 %collective-permute-start.2 = (bf16[672,128]{1,0:T(8,128)(2,1)S(1)}, bf16[672,128]{1,0:T(8,128)(2,1)S(1)}, u32[]{:S(2)}, u32[]{:S(2)}) collective-permute-start(bf16[672,128]{1,0:T(8,128)(2,1)S(1)} %constant_dynamic-update-slice_fusion), channel_id=1, source_target_pairs={{0,1},{1,2},{2,3},{3,4},{4,5},{5,6},{6,7},{8,9},{9,10},{10,11},{11... | collective-permute-start | bytes 516104 | tf_op jit(solution)/shard_map/ppermute | solution.py:568
  30.4 8.9 %collective-permute-start.4 = (bf16[592,128]{1,0:T(8,128)(2,1)S(1)}, bf16[592,128]{1,0:T(8,128)(2,1)S(1)}, u32[]{:S(2)}, u32[]{:S(2)}) collective-permute-start(bf16[592,128]{1,0:T(8,128)(2,1)S(1)} %get-tuple-element.82), channel_id=1, source_target_pairs={{0,8},{8,16},{16,24},{24,32},{32,40},{40,48},{48,56},{1,9},{9,17},... | collective-permute-start | bytes 454664 | tf_op jit(solution)/shard_map/ppermute | solution.py:568
  33.5 10.5 %collective-permute-start.5 = (bf16[592,128]{1,0:T(8,128)(2,1)S(1)}, bf16[592,128]{1,0:T(8,128)(2,1)S(1)}, u32[]{:S(2)}, u32[]{:S(2)}) collective-permute-start(bf16[592,128]{1,0:T(8,128)(2,1)S(1)} %get-tuple-element.83), channel_id=1, source_target_pairs={{8,0},{16,8},{24,16},{32,24},{40,32},{48,40},{56,48},{9,1},{17,9},... | collective-permute-start | bytes 454664 | tf_op jit(solution)/shard_map/ppermute | solution.py:569
  34.8 9.2 %copy-start.10 = (bf16[32,8,3,3,3]{0,1,4,3,2:T(8,128)(2,1)S(1)}, bf16[32,8,3,3,3]{0,1,4,3,2:T(8,128)(2,1)}, u32[]{:S(2)}) copy-start(bf16[32,8,3,3,3]{0,1,4,3,2:T(8,128)(2,1)} %param.16) | copy-start | bytes 41476
  34.8 9.2 %copy-start.11 = (bf16[256,256]{1,0:T(8,128)(2,1)S(1)}, bf16[256,256]{1,0:T(8,128)(2,1)}, u32[]{:S(2)}) copy-start(bf16[256,256]{1,0:T(8,128)(2,1)} %constant.5.clone.up_ref) | copy-start | bytes 393220
  47.8 24.5 %all-to-all-start = ((bf16[128,5,2,128]{3,2,1,0:T(2,128)(2,1)}), bf16[128,5,2,128]{3,2,1,0:T(2,128)(2,1)S(1)}, u32[]{:S(2)}, u32[]{:S(2)}) async-start(bf16[128,5,2,128]{3,2,1,0:T(2,128)(2,1)} %bitcast.21), calls=%async_computation | async-start | bytes 655360 | tf_op jit(solution)/shard_map/all_to_all | solution.py:700
  60.3 13.4 %collective-permute-start.6 = (bf16[208,128]{1,0:T(8,128)(2,1)S(1)}, bf16[208,128]{1,0:T(8,128)(2,1)S(1)}, u32[]{:S(2)}, u32[]{:S(2)}) collective-permute-start(bf16[208,128]{1,0:T(8,128)(2,1)S(1)} %get-tuple-element.91), channel_id=1, source_target_pairs={{0,8},{8,16},{16,24},{24,32},{32,40},{40,48},{48,56},{1,9},{9,17},... | collective-permute-start | bytes 159752 | tf_op jit(solution)/shard_map/ppermute | solution.py:568
  63.7 10.0 %collective-permute-start.7 = (bf16[208,128]{1,0:T(8,128)(2,1)S(1)}, bf16[208,128]{1,0:T(8,128)(2,1)S(1)}, u32[]{:S(2)}, u32[]{:S(2)}) collective-permute-start(bf16[208,128]{1,0:T(8,128)(2,1)S(1)} %get-tuple-element.92), channel_id=1, source_target_pairs={{8,0},{16,8},{24,16},{32,24},{40,32},{48,40},{56,48},{9,1},{17,9},... | collective-permute-start | bytes 159752 | tf_op jit(solution)/shard_map/ppermute | solution.py:569
  73.7 18.4 %all-to-all-start.1 = ((bf16[128,5,2,128]{3,2,1,0:T(2,128)(2,1)}), bf16[128,5,2,128]{3,2,1,0:T(2,128)(2,1)S(1)}, u32[]{:S(2)}, u32[]{:S(2)}) async-start(bf16[128,5,2,128]{3,2,1,0:T(2,128)(2,1)} %shard_map.152), calls=%async_computation.1 | async-start | bytes 655360 | tf_op jit(solution)/shard_map/all_to_all | solution.py:714
  80.1 13.2 %collective-permute-start.8 = (bf16[32,128]{1,0:T(8,128)(2,1)S(1)}, bf16[32,128]{1,0:T(8,128)(2,1)S(1)}, u32[]{:S(2)}, u32[]{:S(2)}) collective-permute-start(bf16[32,128]{1,0:T(8,128)(2,1)S(1)} %get-tuple-element.99), channel_id=1, source_target_pairs={{0,1},{1,2},{2,3},{3,4},{4,5},{5,6},{6,7},{8,9},{9,10},{10,11},{11... | collective-permute-start | bytes 24584 | tf_op jit(solution)/shard_map/ppermute | solution.py:568
  85.3 8.0 %collective-permute-start.9 = (bf16[32,128]{1,0:T(8,128)(2,1)S(1)}, bf16[32,128]{1,0:T(8,128)(2,1)S(1)}, u32[]{:S(2)}, u32[]{:S(2)}) collective-permute-start(bf16[32,128]{1,0:T(8,128)(2,1)S(1)} %get-tuple-element.100), channel_id=1, source_target_pairs={{1,0},{2,1},{3,2},{4,3},{5,4},{6,5},{7,6},{9,8},{10,9},{11,10},{12... | collective-permute-start | bytes 24584 | tf_op jit(solution)/shard_map/ppermute | solution.py:569

commit v2 on v1

--- a/solution.py
+++ b/solution.py
@@ -179,7 +179,7 @@
     return jnp.concatenate(parts, axis=0).T.astype(BF16)
 
 
-def inner_body(xlo_ref, low_ref, delta_ref, high_ref, xhi_ref, pool_ref, w_ref, wmid_ref, acc_ref, wide_ref, win_ref, up_ref, wskip_ref, wm_ref):
+def inner_body(xlo_ref, low_ref, delta_ref, high_ref, xhi_ref, pool_ref, w_ref, wmid_ref, acc_ref, wide_ref, win_ref, up_ref, wskip_ref, wm_ref, wup_ref):
     def put(x, v):
         parts = shifts(v.astype(F32).reshape(768, 128), 128)
         for a in range(3):
@@ -219,8 +219,8 @@
             win_ref[row : row + 32, lane : lane + 128] = v
 
         window_sums(rows_of, pool_ref[...], put_window)
-    w = w_ref[...].reshape(864, 96)
-    up_ref[...] = dot_tn(w, win_ref[...])[:64]
+    wup_ref[...] = w_ref[...].reshape(864, 96).astype(F32).T[:64].astype(BF16)
+    up_ref[...] = dot(wup_ref[...], win_ref[...])
     for a in range(3):
         for b in range(3):
             at = (a * 3 + b) * 32
@@ -229,7 +229,7 @@
 
 
 def outer_body(
-    got_lo_ref, got_hi_ref, wide_ref, up_ref, mslope_ref, st_ref, pool_lo_ref, pool_hi_ref, pool_ref, w_ref, wskip_ref, wm_ref,
+    got_lo_ref, got_hi_ref, wide_ref, up_ref, mslope_ref, st_ref, pool_lo_ref, pool_hi_ref, pool_ref, wup_ref, wskip_ref, wm_ref,
     edge_ref, rim_ref, win_ref, mid_ref, back_ref, face_lo_ref, face_hi_ref,
     total_ref,
 ):
@@ -265,7 +265,7 @@
             win_ref[r : r + 32, lane : lane + 128] = v
 
         window_sums(rows_of, pool_ref[...], put_window)
-    rim_up = dot_tn(w_ref[...].reshape(864, 96), win_ref[...])[:64]
+    rim_up = dot(wup_ref[...], win_ref[...])
 
     upper = lane_ids((64, 128)) >= 64
     before = got_lo_ref[576:640, :].astype(F32)
@@ -289,18 +289,25 @@
                 mid_ref[a * 64 : a * 64 + 64, lane : lane + 128] = part.astype(BF16)
 
     out = dot(wm_ref[...], mid_ref[...])
-    total_ref[...] = jnp.zeros(total_ref.shape, F32)
     upper = lane_ids((32, 128)) >= 64
-    for bx in range(2):
-        for m in range(7):
-            col = (bx * 7 + m) * 128
-            for a in range(3):
-                parts = [out[(a * 3 + b) * 32 : (a * 3 + b) * 32 + 32, col : col + 128] for b in range(3)]
-                down = pltpu.roll(parts[0], 64, 1)
-                up = pltpu.roll(parts[2], 64, 1)
-                total_ref[bx + a, (m + 6) % 7] += jnp.where(upper, down, 0.0)
-                total_ref[bx + a, m] += parts[1] + jnp.where(upper, up, down)
-                total_ref[bx + a, (m + 1) % 7] += jnp.where(upper, 0.0, up)
+
+    def term(a, b, x, m):
+        if not 0 <= x - a < 2:
+            return None
+        col = ((x - a) * 7 + m) * 128
+        return out[(a * 3 + b) * 32 : (a * 3 + b) * 32 + 32, col : col + 128]
+
+    def tap_sum(b, x, m):
+        parts = [v for v in (term(a, b, x, m) for a in range(3)) if v is not None]
+        return sum(parts[1:], parts[0])
+
+    for x in range(4):
+        downs = [pltpu.roll(tap_sum(0, x, m), 64, 1) for m in range(7)]
+        ups = [pltpu.roll(tap_sum(2, x, m), 64, 1) for m in range(7)]
+        for m in range(6):
+            low = ups[(m + 6) % 7] + downs[m]
+            high = ups[m] + downs[m + 1]
+            total_ref[x, m] = tap_sum(1, x, m) + jnp.where(upper, high, low)
     back_ref[...] = total_ref[1:3, 0:6]
     before = got_lo_ref[640:672, :].astype(F32)
     after = got_hi_ref[640:672, :].astype(F32)
@@ -379,7 +386,7 @@
     acc_ref, edge_ref, back_ref, rim_lo_ref, rim_hi_ref, got_lo_ref, got_hi_ref, slope_ref, w_ref, up_ref,
     mid_ref, gmid_ref, st_ref, dec_ref,
     rows_far, own_ref, face_lo_ref, face_hi_ref, edge_lo_ref, edge_hi_ref,
-    enc_ref, total_ref, we_ref, rows_ref, sext_ref, sum_ref, sems,
+    enc_ref, wide_ref, total_ref, we_ref, rows_ref, sext_ref, sum_ref, sems,
 ):
     writes = fetch([(dec_ref, rows_far.at[0:736])], sems.at[0])
 
@@ -408,16 +415,17 @@
         sext_ref[x + 1, 0] = before[x * 8 : x * 8 + 8]
         sext_ref[x + 1, 25] = after[x * 8 : x * 8 + 8]
 
+    whole = [back_ref[bx].reshape(192, 128) for bx in range(2)]
+    whole = [v + ref[0:192, :].astype(F32) for v, ref in zip(whole, (got_lo_ref, got_hi_ref))]
+    whole = jnp.concatenate(whole, axis=0) * 0.125
+    high = whole.astype(BF16)
+    low = (whole - high.astype(F32)).astype(BF16)
+    wide_ref[...] = dot(jnp.concatenate([high, low], axis=1), up_ref[...])
     for bx in range(2):
         for m in range(6):
-            whole = back_ref[bx, m]
-            whole = whole + (got_lo_ref if bx == 0 else got_hi_ref)[m * 32 : m * 32 + 32, :].astype(F32)
-            whole = whole * 0.125
-            high = whole.astype(BF16)
-            low = (whole - high.astype(F32)).astype(BF16)
-            wide = dot(jnp.concatenate([high, low], axis=1), up_ref[...])
+            at = (bx * 6 + m) * 32
             for half in range(2):
-                fine = wide[:, half * 128 : half * 128 + 128]
+                fine = wide_ref[at : at + 32, half * 128 : half * 128 + 128]
                 for ey in range(2):
                     y = 4 * m + 2 * half + ey
                     for ex in range(2):
@@ -463,7 +471,7 @@
                 total_ref[x, y + r] += sum(parts[1:], parts[0])
         return carry
 
-    lax.fori_loop(0, 6, step, 0)
+    lax.fori_loop(0, 6, step, 0, unroll=3)
     genc = jnp.concatenate([sum_ref[...], jnp.zeros((72, 32), F32)], axis=1)
     rows_ref[432:544, :] = jnp.concatenate([genc, jnp.zeros((40, 128), F32)], axis=0).astype(BF16)
     writes += fetch([(rows_ref.at[432:544], rows_far.at[1168:1280])], sems.at[2])
@@ -629,7 +637,7 @@
         return jnp.concatenate([v.reshape(-1, 128) for v in rows])
 
     ylo, yhi = both_ways(column(slice(0, 3), tail_lo), column(slice(21, 24), tail_hi), "gy")
-    acc, wide, win, up, wskip, wmid = call(
+    acc, wide, win, up, wskip, wmid, wup = call(
         inner_body,
         [
             sds((4, 26, 32, 128), F32),
@@ -638,6 +646,7 @@
             sds((64, 1024), F32),
             sds((96, 288), BF16),
             sds((288, 192), BF16),
+            sds((64, 864), BF16),
         ],
         [],
         (xlo, delta_lo, delta, delta_hi, xhi, pool, dec_w, mid_w),
@@ -654,8 +663,8 @@
             sds((592, 128), BF16),
             sds((592, 128), BF16),
         ],
-        [pltpu.VMEM((4, 7, 32, 128), F32)],
-        (ylo, yhi, wide, up, mid_slope, state, pool_lo, pool_hi, pool, dec_w, wskip, wmid),
+        [pltpu.VMEM((4, 6, 32, 128), F32)],
+        (ylo, yhi, wide, up, mid_slope, state, pool_lo, pool_hi, pool, wup, wskip, wmid),
         1 << 30, 24,
     )
     got_lo, got_hi = both_ways(face_lo, face_hi, "gx")
@@ -679,6 +688,7 @@
         ],
         [
             pltpu.VMEM((96, 24 * 512), BF16),
+            pltpu.VMEM((384, 256), F32),
             pltpu.VMEM((6, 26, 8, 128), F32),
             pltpu.VMEM((72, 96), F32),
             pltpu.VMEM((544, 128), BF16),

time: 94.7 us -> 94 us (level)
  no operation moved by 1% of the time
where the time goes in v2:
time: 94 us; the launch traced here: 93.4 us
  starting transfers between devices  47.3 us (50%)
  Pallas kernels  22.4 us (24%)
  waiting for transfers between devices  20.1 us (21%)
  local copies, waits for them, and re-layouts  2.49 us (3%)
  between operations  1.08 us (1%)
    pallas_call x10, Pallas kernels, call(): pl.pallas_call(body, out_shape=outs, in_specs=[HBM] * far + [VMEM] * (len...  22.4 us
    ppermute x5, starting transfers between devices, both_ways(): from_before = lax.ppermute(high, axis, [(i, i + 1) for i in range(ends)])  21.9 us
    all_to_all x1, starting transfers between devices, on_device(): pieces = lax.all_to_all(rows.reshape(count, share, 2, 128), axes, 0, 0)  12.5 us
    all_to_all x1, waiting for transfers between devices, on_device(): pieces = lax.all_to_all(rows.reshape(count, share, 2, 128), axes, 0, 0)  7.24 us
    ppermute x5, starting transfers between devices, both_ways(): from_after = lax.ppermute(low, axis, [(i + 1, i) for i in range(ends)])  6.46 us
    all_to_all x1, starting transfers between devices, on_device(): rows = lax.all_to_all(shares, axes, 0, 0).reshape(1280, 128)  6.44 us
    ppermute x5, waiting for transfers between devices, both_ways(): from_after = lax.ppermute(low, axis, [(i + 1, i) for i in range(ends)])  6.1 us
    all_to_all x1, waiting for transfers between devices, on_device(): rows = lax.all_to_all(shares, axes, 0, 0).reshape(1280, 128)  5.45 us
  transfers between devices with their start and end apart: 12, of which 5 were waited for; matrix products, arithmetic and copies ran while one was open for 3% of the time, Pallas kernels for 15%

profile of v2, /device:TPU:1, one launch (start us, length us, event | category | flops | bytes accessed | tf_op | source)
XLA Modules:
  0.0 93.4 jit_solution(9092176387586168897)
XLA Ops:
  0.7 2.5 %shard_map.146 = (bf16[24,32,128]{2,1,0:T(8,128)(2,1)}, bf16[24,32,128]{2,1,0:T(8,128)(2,1)}) custom-call(bf16[32,4,24,128]{3,2,1,0:T(8,128)(2,1)} %bitcast.29, bf16[8,4,24,128]{3,2,1,0:T(8,128)(2,1)} %bitcast.31, bf16[8,32]{1,0:T(8,128)(2,1)} %head_ref.1), custom_call_target="tpu_custom_call" | custom-call | flops 209715200 | bytes 4194304 | tf_op jit(solution)/shard_map/pallas_call | solution.py:21
  3.2 4.4 %collective-permute-start = (bf16[24,32,128]{2,1,0:T(8,128)(2,1)}, bf16[24,32,128]{2,1,0:T(8,128)(2,1)S(1)}, u32[]{:S(2)}, u32[]{:S(2)}) collective-permute-start(bf16[24,32,128]{2,1,0:T(8,128)(2,1)} %get-tuple-element.57.high_ref), channel_id=1, source_target_pairs={{0,8},{8,16},{16,24},{24,32},{32,40},{40,48},{48,56},{1,9},{9,17},... | collective-permute-start | bytes 589832 | tf_op jit(solution)/shard_map/ppermute | solution.py:576
  7.6 1.3 %collective-permute-start.1 = (bf16[24,32,128]{2,1,0:T(8,128)(2,1)}, bf16[24,32,128]{2,1,0:T(8,128)(2,1)S(1)}, u32[]{:S(2)}, u32[]{:S(2)}) collective-permute-start(bf16[24,32,128]{2,1,0:T(8,128)(2,1)} %get-tuple-element.58.low_ref), channel_id=1, source_target_pairs={{8,0},{16,8},{24,16},{32,24},{40,32},{48,40},{56,48},{9,1},{17,9},... | collective-permute-start | bytes 589832 | tf_op jit(solution)/shard_map/ppermute | solution.py:577
  11.3 2.3 %shard_map.147 = (bf16[2,24,32,128]{3,2,1,0:T(8,128)(2,1)S(1)}, f32[8,32]{1,0:T(8,128)S(1)}, bf16[4,24,32,128]{3,2,1,0:T(8,128)(2,1)S(1)}, f32[4,24,32,128]{3,2,...) custom-call(bf16[32,4,24,128]{3,2,1,0:T(8,128)(2,1)S(1)} %bitcast.30, ...), custom_call_target="tpu_custom_call" | custom-call | flops 629145600 | bytes 4194304 | tf_op jit(solution)/shard_map/pallas_call | solution.py:21
  13.7 1.5 %collective-permute-done.1.xhi_ref = bf16[24,32,128]{2,1,0:T(8,128)(2,1)S(1)} collective-permute-done((bf16[24,32,128]{2,1,0:T(8,128)(2,1)}, bf16[24,32,128]{2,1,0:T(8,128)(2,1)S(1)}, u32[]{:S(2)}, u32[]{:S(2)}) %collective-permute-start.1) | collective-permute-done | bytes 196640 | tf_op jit(solution)/shard_map/ppermute | solution.py:577
  15.1 1.3 %collective-permute-start.3 = (bf16[672,128]{1,0:T(8,128)(2,1)S(1)}, bf16[672,128]{1,0:T(8,128)(2,1)S(1)}, u32[]{:S(2)}, u32[]{:S(2)}) collective-permute-start(bf16[672,128]{1,0:T(8,128)(2,1)S(1)} %constant_dynamic-update-slice_fusion.7), channel_id=1, source_target_pairs={{1,0},{2,1},{3,2},{4,3},{5,4},{6,5},{7,6},{9,8},{10,9},{11,10},{12... | collective-permute-start | bytes 516104 | tf_op jit(solution)/shard_map/ppermute | solution.py:577
  16.5 5.8 %collective-permute-start.2 = (bf16[672,128]{1,0:T(8,128)(2,1)S(1)}, bf16[672,128]{1,0:T(8,128)(2,1)S(1)}, u32[]{:S(2)}, u32[]{:S(2)}) collective-permute-start(bf16[672,128]{1,0:T(8,128)(2,1)S(1)} %constant_dynamic-update-slice_fusion), channel_id=1, source_target_pairs={{0,1},{1,2},{2,3},{3,4},{4,5},{5,6},{6,7},{8,9},{9,10},{10,11},{11... | collective-permute-start | bytes 516104 | tf_op jit(solution)/shard_map/ppermute | solution.py:576
  22.4 4.8 %shard_map.148 = (f32[4,26,32,128]{3,2,1,0:T(8,128)S(1)}, bf16[6,24,96,128]{3,2,1,0:T(8,128)(2,1)S(1)}, bf16[864,1024]{1,0:T(8,128)(2,1)S(1)}, f32[64,1024]{1,0:...) custom-call(bf16[24,32,128]{2,1,0:T(8,128)(2,1)S(1)} %collective-permute-done.x, ...), custom_call_target="tpu_custom_call" | custom-call | flops 3221225472 | bytes 4194304 | tf_op jit(solution)/shard_map/pallas_call | solution.py:21
  27.2 1.3 %collective-permute-done.2.got_lo_ref.rim_lo_ref = bf16[672,128]{1,0:T(8,128)(2,1)S(1)} collective-permute-done((bf16[672,128]{1,0:T(8,128)(2,1)S(1)}, bf16[672,128]{1,0:T(8,128)(2,1)S(1)}, u32[]{:S(2)}, u32[]{:S(2)}) %collective-permute-start.2) | collective-permute-done | bytes 172064 | tf_op jit(solution)/shard_map/ppermute | solution.py:576
  28.6 1.8 %shard_map.149 = (f32[4,2,32,128]{3,2,1,0:T(8,128)S(1)}, bf16[6,2,96,128]{3,2,1,0:T(8,128)(2,1)S(1)}, bf16[864,768]{1,0:T(8,128)(2,1)S(1)}, bf16[192,1792]{1,0:T...) custom-call(bf16[672,128]{1,0:T(8,128)(2,1)S(1)} %collective-permute-don, ...), custom_call_target="tpu_custom_call" | custom-call | flops 1073741824 | bytes 4194304 | tf_op jit(solution)/shard_map/pallas_call | solution.py:21
  30.4 3.0 %collective-permute-start.4 = (bf16[592,128]{1,0:T(8,128)(2,1)S(1)}, bf16[592,128]{1,0:T(8,128)(2,1)S(1)}, u32[]{:S(2)}, u32[]{:S(2)}) collective-permute-start(bf16[592,128]{1,0:T(8,128)(2,1)S(1)} %get-tuple-element.84), channel_id=1, source_target_pairs={{0,8},{8,16},{16,24},{24,32},{32,40},{40,48},{48,56},{1,9},{9,17},... | collective-permute-start | bytes 454664 | tf_op jit(solution)/shard_map/ppermute | solution.py:576
  33.4 1.3 %collective-permute-start.5 = (bf16[592,128]{1,0:T(8,128)(2,1)S(1)}, bf16[592,128]{1,0:T(8,128)(2,1)S(1)}, u32[]{:S(2)}, u32[]{:S(2)}) collective-permute-start(bf16[592,128]{1,0:T(8,128)(2,1)S(1)} %get-tuple-element.85), channel_id=1, source_target_pairs={{8,0},{16,8},{24,16},{32,24},{40,32},{48,40},{56,48},{9,1},{17,9},... | collective-permute-start | bytes 454664 | tf_op jit(solution)/shard_map/ppermute | solution.py:577
  34.8 4.5 %shard_map.150 = (bf16[736,128]{1,0:T(8,128)(2,1)S(1)}, f32[288,192]{1,0:T(8,128)S(1)}) custom-call(bf16[6,24,96,128]{3,2,1,0:T(8,128)(2,1)S(1)} %get-tuple-element.63.wide_ref, bf16[6,2,96,128]{3,2,1,0:T(8,128)(2,1)S(1)} %get-tuple-element.74.rim_ref, bf16[4,24,32,128]{3,2,1,0:T(8,128)(2,1)S(1)} %get-tuple-element.75.hid_ref, ...), custom_call_target="tpu_custom_call" | custom-call | flops 3221225472 | bytes 4194304 | tf_op jit(solution)/shard_map/pallas_call | solution.py:21
  39.3 4.6 %collective-permute-done.5.got_hi_ref = bf16[592,128]{1,0:T(8,128)(2,1)S(1)} collective-permute-done((bf16[592,128]{1,0:T(8,128)(2,1)S(1)}, bf16[592,128]{1,0:T(8,128)(2,1)S(1)}, u32[]{:S(2)}, u32[]{:S(2)}) %collective-permute-start.5) | collective-permute-done | bytes 151584 | tf_op jit(solution)/shard_map/ppermute | solution.py:577
  43.9 3.2 %shard_map.151 = (bf16[1280,128]{1,0:T(8,128)(2,1)}, f32[4,24,8,128]{3,2,1,0:T(8,128)S(1)}, bf16[208,128]{1,0:T(8,128)(2,1)S(1)}, bf16[208,128]{1,0:T(8,128)(2,1...) custom-call(f32[4,26,32,128]{3,2,1,0:T(8,128)S(1)} %get-tuple-element.60.acc_ref, ...), custom_call_target="tpu_custom_call" | custom-call | flops 2147483648 | bytes 4194304 | tf_op jit(solution)/shard_map/pallas_call | solution.py:21
  47.1 12.5 %all-to-all-start = ((bf16[128,5,2,128]{3,2,1,0:T(2,128)(2,1)}), bf16[128,5,2,128]{3,2,1,0:T(2,128)(2,1)S(1)}, u32[]{:S(2)}, u32[]{:S(2)}) async-start(bf16[128,5,2,128]{3,2,1,0:T(2,128)(2,1)} %bitcast.21), calls=%async_computation | async-start | bytes 655360 | tf_op jit(solution)/shard_map/all_to_all | solution.py:710
  59.6 3.4 %collective-permute-start.6 = (bf16[208,128]{1,0:T(8,128)(2,1)S(1)}, bf16[208,128]{1,0:T(8,128)(2,1)S(1)}, u32[]{:S(2)}, u32[]{:S(2)}) collective-permute-start(bf16[208,128]{1,0:T(8,128)(2,1)S(1)} %get-tuple-element.93), channel_id=1, source_target_pairs={{0,8},{8,16},{16,24},{24,32},{32,40},{40,48},{48,56},{1,9},{9,17},... | collective-permute-start | bytes 159752 | tf_op jit(solution)/shard_map/ppermute | solution.py:576
  63.0 1.3 %collective-permute-start.7 = (bf16[208,128]{1,0:T(8,128)(2,1)S(1)}, bf16[208,128]{1,0:T(8,128)(2,1)S(1)}, u32[]{:S(2)}, u32[]{:S(2)}) collective-permute-start(bf16[208,128]{1,0:T(8,128)(2,1)S(1)} %get-tuple-element.94), channel_id=1, source_target_pairs={{8,0},{16,8},{24,16},{32,24},{40,32},{48,40},{56,48},{9,1},{17,9},... | collective-permute-start | bytes 159752 | tf_op jit(solution)/shard_map/ppermute | solution.py:577
  64.3 7.2 %all-to-all-done.pieces_far = bf16[128,5,2,128]{3,2,1,0:T(2,128)(2,1)S(1)} async-done(((bf16[128,5,2,128]{3,2,1,0:T(2,128)(2,1)}), bf16[128,5,2,128]{3,2,1,0:T(2,128)(2,1)S(1)}, u32[]{:S(2)}, u32[]{:S(2)}) %all-to-all-start) | async-done | bytes 327712 | tf_op jit(solution)/shard_map/all_to_all | solution.py:710
  71.6 1.4 %shard_map.152 = bf16[128,5,2,128]{3,2,1,0:T(2,128)(2,1)} custom-call(bf16[128,5,2,128]{3,2,1,0:T(2,128)(2,1)S(1)} %all-to-all-done.pieces_far), custom_call_target="tpu_custom_call" | custom-call | flops 1048576 | bytes 4194304 | tf_op jit(solution)/shard_map/pallas_call | solution.py:21
  73.0 6.4 %all-to-all-start.1 = ((bf16[128,5,2,128]{3,2,1,0:T(2,128)(2,1)}), bf16[128,5,2,128]{3,2,1,0:T(2,128)(2,1)S(1)}, u32[]{:S(2)}, u32[]{:S(2)}) async-start(bf16[128,5,2,128]{3,2,1,0:T(2,128)(2,1)} %shard_map.152), calls=%async_computation.1 | async-start | bytes 655360 | tf_op jit(solution)/shard_map/all_to_all | solution.py:724
  79.5 5.2 %collective-permute-start.8 = (bf16[32,128]{1,0:T(8,128)(2,1)S(1)}, bf16[32,128]{1,0:T(8,128)(2,1)S(1)}, u32[]{:S(2)}, u32[]{:S(2)}) collective-permute-start(bf16[32,128]{1,0:T(8,128)(2,1)S(1)} %get-tuple-element.101), channel_id=1, source_target_pairs={{0,1},{1,2},{2,3},{3,4},{4,5},{5,6},{6,7},{8,9},{9,10},{10,11},{11... | collective-permute-start | bytes 24584 | tf_op jit(solution)/shard_map/ppermute | solution.py:576
  84.7 1.3 %collective-permute-start.9 = (bf16[32,128]{1,0:T(8,128)(2,1)S(1)}, bf16[32,128]{1,0:T(8,128)(2,1)S(1)}, u32[]{:S(2)}, u32[]{:S(2)}) collective-permute-start(bf16[32,128]{1,0:T(8,128)(2,1)S(1)} %get-tuple-element.102), channel_id=1, source_target_pairs={{1,0},{2,1},{3,2},{4,3},{5,4},{6,5},{7,6},{9,8},{10,9},{11,10},{12... | collective-permute-start | bytes 24584 | tf_op jit(solution)/shard_map/ppermute | solution.py:577
  86.0 5.5 %all-to-all-done.1 = bf16[128,5,2,128]{3,2,1,0:T(2,128)(2,1)S(1)} async-done(((bf16[128,5,2,128]{3,2,1,0:T(2,128)(2,1)}), bf16[128,5,2,128]{3,2,1,0:T(2,128)(2,1)S(1)}, u32[]{:S(2)}, u32[]{:S(2)}) %all-to-all-start.1) | async-done | bytes 327712 | tf_op jit(solution)/shard_map/all_to_all | solution.py:724
  (54 shorter events, 4.5 us)
Async XLA Ops:
  0.6 10.5 %copy-start.2 = (bf16[256,384]{1,0:T(8,128)(2,1)S(1)}, bf16[256,384]{1,0:T(8,128)(2,1)}, u32[]{:S(2)}) copy-start(bf16[256,384]{1,0:T(8,128)(2,1)} %constant.4.clone.pool_ref) | copy-start | bytes 589828
  0.6 10.5 %copy-start.7 = (bf16[8,32]{1,0:T(8,128)(2,1)S(1)}, bf16[8,32]{1,0:T(8,128)(2,1)}, u32[]{:S(2)}) copy-start(bf16[8,32]{1,0:T(8,128)(2,1)} %head_ref.1) | copy-start | bytes 1540
  0.7 10.5 %copy-start.1 = (bf16[1,8,4,24,128]{4,3,2,1,0:T(8,128)(2,1)S(1)}, bf16[1,8,4,24,128]{4,3,2,1,0:T(8,128)(2,1)}, u32[]{:S(2)}) copy-start(bf16[1,8,4,24,128]{4,3,2,1,0:T(8,128)(2,1)} %param.15) | copy-start | bytes 589828
  0.7 10.5 %copy-start = (bf16[1,32,4,24,128]{4,3,2,1,0:T(8,128)(2,1)S(1)}, bf16[1,32,4,24,128]{4,3,2,1,0:T(8,128)(2,1)}, u32[]{:S(2)}) copy-start(bf16[1,32,4,24,128]{4,3,2,1,0:T(8,128)(2,1)} %param.14) | copy-start | bytes 2359300
  0.7 10.5 %copy-start.3 = (bf16[1,32,4,24,128]{4,3,2,1,0:T(8,128)(2,1)S(1)}, bf16[1,32,4,24,128]{4,3,2,1,0:T(8,128)(2,1)}, u32[]{:S(2)}) copy-start(bf16[1,32,4,24,128]{4,3,2,1,0:T(8,128)(2,1)} %param.12) | copy-start | bytes 2359300
  0.7 10.5 %copy-start.4 = (bf16[1,8,4,24,128]{4,3,2,1,0:T(8,128)(2,1)S(1)}, bf16[1,8,4,24,128]{4,3,2,1,0:T(8,128)(2,1)}, u32[]{:S(2)}) copy-start(bf16[1,8,4,24,128]{4,3,2,1,0:T(8,128)(2,1)} %param.11) | copy-start | bytes 589828
  3.2 10.4 %collective-permute-start = (bf16[24,32,128]{2,1,0:T(8,128)(2,1)}, bf16[24,32,128]{2,1,0:T(8,128)(2,1)S(1)}, u32[]{:S(2)}, u32[]{:S(2)}) collective-permute-start(bf16[24,32,128]{2,1,0:T(8,128)(2,1)} %get-tuple-element.57.high_ref), channel_id=1, source_target_pairs={{0,8},{8,16},{16,24},{24,32},{32,40},{40,48},{48,56},{1,9},{9,17},... | collective-permute-start | bytes 589832 | tf_op jit(solution)/shard_map/ppermute | solution.py:576
  7.6 7.6 %collective-permute-start.1 = (bf16[24,32,128]{2,1,0:T(8,128)(2,1)}, bf16[24,32,128]{2,1,0:T(8,128)(2,1)S(1)}, u32[]{:S(2)}, u32[]{:S(2)}) collective-permute-start(bf16[24,32,128]{2,1,0:T(8,128)(2,1)} %get-tuple-element.58.low_ref), channel_id=1, source_target_pairs={{8,0},{16,8},{24,16},{32,24},{40,32},{48,40},{56,48},{9,1},{17,9},... | collective-permute-start | bytes 589832 | tf_op jit(solution)/shard_map/ppermute | solution.py:577
  11.2 11.2 %copy-start.5 = (bf16[24,32,128]{2,1,0:T(8,128)(2,1)S(1)}, bf16[24,32,128]{2,1,0:T(8,128)(2,1)}, u32[]{:S(2)}) copy-start(bf16[24,32,128]{2,1,0:T(8,128)(2,1)} %get-tuple-element.58.low_ref) | copy-start | bytes 589828
  11.2 11.2 %copy-start.6 = (bf16[24,32,128]{2,1,0:T(8,128)(2,1)S(1)}, bf16[24,32,128]{2,1,0:T(8,128)(2,1)}, u32[]{:S(2)}) copy-start(bf16[24,32,128]{2,1,0:T(8,128)(2,1)} %get-tuple-element.57.high_ref) | copy-start | bytes 589828
  11.2 11.2 %copy-start.8 = (bf16[32,96,3,3,3]{1,0,4,3,2:T(8,128)(2,1)S(1)}, bf16[32,96,3,3,3]{1,0,4,3,2:T(8,128)(2,1)}, u32[]{:S(2)}) copy-start(bf16[32,96,3,3,3]{1,0,4,3,2:T(8,128)(2,1)} %param.18) | copy-start | bytes 497668
  11.3 11.2 %copy-start.9 = (bf16[64,32,3,3,3]{0,1,4,3,2:T(8,128)(2,1)S(1)}, bf16[64,32,3,3,3]{0,1,4,3,2:T(8,128)(2,1)}, u32[]{:S(2)}) copy-start(bf16[64,32,3,3,3]{0,1,4,3,2:T(8,128)(2,1)} %param.17) | copy-start | bytes 331780
  15.1 12.1 %collective-permute-start.3 = (bf16[672,128]{1,0:T(8,128)(2,1)S(1)}, bf16[672,128]{1,0:T(8,128)(2,1)S(1)}, u32[]{:S(2)}, u32[]{:S(2)}) collective-permute-start(bf16[672,128]{1,0:T(8,128)(2,1)S(1)} %constant_dynamic-update-slice_fusion.7), channel_id=1, source_target_pairs={{1,0},{2,1},{3,2},{4,3},{5,4},{6,5},{7,6},{9,8},{10,9},{11,10},{12... | collective-permute-start | bytes 516104 | tf_op jit(solution)/shard_map/ppermute | solution.py:577
  16.5 12.0 %collective-permute-start.2 = (bf16[672,128]{1,0:T(8,128)(2,1)S(1)}, bf16[672,128]{1,0:T(8,128)(2,1)S(1)}, u32[]{:S(2)}, u32[]{:S(2)}) collective-permute-start(bf16[672,128]{1,0:T(8,128)(2,1)S(1)} %constant_dynamic-update-slice_fusion), channel_id=1, source_target_pairs={{0,1},{1,2},{2,3},{3,4},{4,5},{5,6},{6,7},{8,9},{9,10},{10,11},{11... | collective-permute-start | bytes 516104 | tf_op jit(solution)/shard_map/ppermute | solution.py:576
  30.4 8.9 %collective-permute-start.4 = (bf16[592,128]{1,0:T(8,128)(2,1)S(1)}, bf16[592,128]{1,0:T(8,128)(2,1)S(1)}, u32[]{:S(2)}, u32[]{:S(2)}) collective-permute-start(bf16[592,128]{1,0:T(8,128)(2,1)S(1)} %get-tuple-element.84), channel_id=1, source_target_pairs={{0,8},{8,16},{16,24},{24,32},{32,40},{40,48},{48,56},{1,9},{9,17},... | collective-permute-start | bytes 454664 | tf_op jit(solution)/shard_map/ppermute | solution.py:576
  33.4 10.5 %collective-permute-start.5 = (bf16[592,128]{1,0:T(8,128)(2,1)S(1)}, bf16[592,128]{1,0:T(8,128)(2,1)S(1)}, u32[]{:S(2)}, u32[]{:S(2)}) collective-permute-start(bf16[592,128]{1,0:T(8,128)(2,1)S(1)} %get-tuple-element.85), channel_id=1, source_target_pairs={{8,0},{16,8},{24,16},{32,24},{40,32},{48,40},{56,48},{9,1},{17,9},... | collective-permute-start | bytes 454664 | tf_op jit(solution)/shard_map/ppermute | solution.py:577
  34.7 9.2 %copy-start.10 = (bf16[32,8,3,3,3]{0,1,4,3,2:T(8,128)(2,1)S(1)}, bf16[32,8,3,3,3]{0,1,4,3,2:T(8,128)(2,1)}, u32[]{:S(2)}) copy-start(bf16[32,8,3,3,3]{0,1,4,3,2:T(8,128)(2,1)} %param.16) | copy-start | bytes 41476
  34.7 9.2 %copy-start.11 = (bf16[256,256]{1,0:T(8,128)(2,1)S(1)}, bf16[256,256]{1,0:T(8,128)(2,1)}, u32[]{:S(2)}) copy-start(bf16[256,256]{1,0:T(8,128)(2,1)} %constant.5.clone.up_ref) | copy-start | bytes 393220
  47.1 24.5 %all-to-all-start = ((bf16[128,5,2,128]{3,2,1,0:T(2,128)(2,1)}), bf16[128,5,2,128]{3,2,1,0:T(2,128)(2,1)S(1)}, u32[]{:S(2)}, u32[]{:S(2)}) async-start(bf16[128,5,2,128]{3,2,1,0:T(2,128)(2,1)} %bitcast.21), calls=%async_computation | async-start | bytes 655360 | tf_op jit(solution)/shard_map/all_to_all | solution.py:710
  59.6 13.4 %collective-permute-start.6 = (bf16[208,128]{1,0:T(8,128)(2,1)S(1)}, bf16[208,128]{1,0:T(8,128)(2,1)S(1)}, u32[]{:S(2)}, u32[]{:S(2)}) collective-permute-start(bf16[208,128]{1,0:T(8,128)(2,1)S(1)} %get-tuple-element.93), channel_id=1, source_target_pairs={{0,8},{8,16},{16,24},{24,32},{32,40},{40,48},{48,56},{1,9},{9,17},... | collective-permute-start | bytes 159752 | tf_op jit(solution)/shard_map/ppermute | solution.py:576
  63.0 10.0 %collective-permute-start.7 = (bf16[208,128]{1,0:T(8,128)(2,1)S(1)}, bf16[208,128]{1,0:T(8,128)(2,1)S(1)}, u32[]{:S(2)}, u32[]{:S(2)}) collective-permute-start(bf16[208,128]{1,0:T(8,128)(2,1)S(1)} %get-tuple-element.94), channel_id=1, source_target_pairs={{8,0},{16,8},{24,16},{32,24},{40,32},{48,40},{56,48},{9,1},{17,9},... | collective-permute-start | bytes 159752 | tf_op jit(solution)/shard_map/ppermute | solution.py:577
  73.0 18.4 %all-to-all-start.1 = ((bf16[128,5,2,128]{3,2,1,0:T(2,128)(2,1)}), bf16[128,5,2,128]{3,2,1,0:T(2,128)(2,1)S(1)}, u32[]{:S(2)}, u32[]{:S(2)}) async-start(bf16[128,5,2,128]{3,2,1,0:T(2,128)(2,1)} %shard_map.152), calls=%async_computation.1 | async-start | bytes 655360 | tf_op jit(solution)/shard_map/all_to_all | solution.py:724
  79.5 13.2 %collective-permute-start.8 = (bf16[32,128]{1,0:T(8,128)(2,1)S(1)}, bf16[32,128]{1,0:T(8,128)(2,1)S(1)}, u32[]{:S(2)}, u32[]{:S(2)}) collective-permute-start(bf16[32,128]{1,0:T(8,128)(2,1)S(1)} %get-tuple-element.101), channel_id=1, source_target_pairs={{0,1},{1,2},{2,3},{3,4},{4,5},{5,6},{6,7},{8,9},{9,10},{10,11},{11... | collective-permute-start | bytes 24584 | tf_op jit(solution)/shard_map/ppermute | solution.py:576
  84.7 8.0 %collective-permute-start.9 = (bf16[32,128]{1,0:T(8,128)(2,1)S(1)}, bf16[32,128]{1,0:T(8,128)(2,1)S(1)}, u32[]{:S(2)}, u32[]{:S(2)}) collective-permute-start(bf16[32,128]{1,0:T(8,128)(2,1)S(1)} %get-tuple-element.102), channel_id=1, source_target_pairs={{1,0},{2,1},{3,2},{4,3},{5,4},{6,5},{7,6},{9,8},{10,9},{11,10},{12... | collective-permute-start | bytes 24584 | tf_op jit(solution)/shard_map/ppermute | solution.py:577

commit v3 on v2

--- a/solution.py
+++ b/solution.py
@@ -60,6 +60,15 @@
     return s * (1.0 + v * (1.0 - s))
 
 
+def parity(axis):
+    return jnp.bitwise_and(lax.axis_index(axis), 1)
+
+
+def in_order(axis, first, second):
+    odd = parity(axis) == 1
+    return jnp.where(odd, first, second), jnp.where(odd, second, first)
+
+
 def lane_ids(shape):
     return lax.broadcasted_iota(jnp.int32, shape, len(shape) - 1)
 
@@ -83,15 +92,16 @@
     return (back * slope(pre, s)).astype(BF16), cot_lanes, pre * s
 
 
-def face_body(dec_far, cot_far, head_far, low_far, high_far, dec_ref, cot_ref, head_ref, delta_ref, sems, out_sems):
-    planes = (0, 3)
+def face_body(dec_far, cot_far, head_far, first_far, second_far, dec_ref, cot_ref, head_ref, delta_ref, sems, out_sems):
+    odd = parity("gx")
+    planes = (3 - 3 * odd, 3 * odd)
     pairs = [(head_far, head_ref)]
     for i, x in enumerate(planes):
         pairs += [(cot_far.at[:, x], cot_ref.at[i]), (dec_far.at[:, x], dec_ref.at[i])]
     waits = fetch(pairs, sems)
     waits[0]()
     writes = []
-    for i, far in enumerate((low_far, high_far)):
+    for i, far in enumerate((first_far, second_far)):
         waits[2 * i + 1]()
         waits[2 * i + 2]()
         delta_ref[i] = delta_plane(dec_ref[i], cot_ref[i], head_ref[...])[0]
@@ -102,7 +112,7 @@
 
 def forward_body(
     dec_ref, cot_ref, head_ref, enc_ref, state_ref, mid_ref, pool_ref,
-    delta_ref, head_grad_ref, hid_ref, slope_ref, pooled_ref, hmid_ref, mslope_ref, st_ref, ylo_ref, yhi_ref, xlo_ref, xhi_ref,
+    delta_ref, head_grad_ref, hid_ref, slope_ref, pooled_ref, hmid_ref, mslope_ref, st_ref, ylo_ref, yhi_ref,
 ):
     total = jnp.zeros((8, 32), F32)
     for x in range(4):
@@ -137,8 +147,6 @@
                     acc = part if acc is None else acc + part
             pooled = (acc * 0.125).astype(BF16)
             pooled_ref[bx, m] = pooled
-            side_ref = xlo_ref if bx == 0 else xhi_ref
-            side_ref[m * 32 : m * 32 + 32, :] = pooled
             pre = mid_ref[bx, m].astype(F32)
             s = sigmoid(pre)
             hmid_ref[bx, m] = (pre * s).astype(BF16)
@@ -179,14 +187,19 @@
     return jnp.concatenate(parts, axis=0).T.astype(BF16)
 
 
-def inner_body(xlo_ref, low_ref, delta_ref, high_ref, xhi_ref, pool_ref, w_ref, wmid_ref, acc_ref, wide_ref, win_ref, up_ref, wskip_ref, wm_ref, wup_ref):
+def inner_body(got1_ref, face1_ref, delta_ref, face2_ref, got2_ref, pool_ref, w_ref, wmid_ref, acc_ref, wide_ref, win_ref, up_ref, wskip_ref, wm_ref, wup_ref):
     def put(x, v):
         parts = shifts(v.astype(F32).reshape(768, 128), 128)
         for a in range(3):
             wide_ref[x, :, a * 32 : a * 32 + 32, :] = parts[a].astype(BF16).reshape(24, 32, 128)
 
-    for x, v in enumerate((xlo_ref[...], low_ref[...], delta_ref[0], delta_ref[1], high_ref[...], xhi_ref[...])):
-        put(x, v)
+    odd = parity("gx")
+    put(5 - 5 * odd, got1_ref[...])
+    put(4 - 3 * odd, face1_ref[...])
+    put(2, delta_ref[0])
+    put(3, delta_ref[1])
+    put(1 + 3 * odd, face2_ref[...])
+    put(5 * odd, got2_ref[...])
     wskip_ref[...] = skip_weights(w_ref)
     acc_ref[...] = jnp.zeros(acc_ref.shape, F32)
 
@@ -229,20 +242,21 @@
 
 
 def outer_body(
-    got_lo_ref, got_hi_ref, wide_ref, up_ref, mslope_ref, st_ref, pool_lo_ref, pool_hi_ref, pool_ref, wup_ref, wskip_ref, wm_ref,
-    edge_ref, rim_ref, win_ref, mid_ref, back_ref, face_lo_ref, face_hi_ref,
-    total_ref,
+    got1_ref, got2_ref, wide_ref, up_ref, mslope_ref, st_ref, pooled_ref, pool_ref, wup_ref, wskip_ref, wm_ref,
+    edge_ref, rim_ref, win_ref, mid_ref, back_ref, face1_ref, face2_ref,
+    total_ref, got_ref,
 ):
     wskip = wskip_ref[...]
+    odd_x, odd_y = parity("gx"), parity("gy")
+    got_ref[1 - odd_y] = got1_ref[...]
+    got_ref[odd_y] = got2_ref[...]
 
     def row(x, y):
-        if y < 0:
-            at = (x * 3 + y + 3) * 32
-            return got_lo_ref[at : at + 32, :]
-        if y > 23:
-            at = (x * 3 + y - 24) * 32
-            return got_hi_ref[at : at + 32, :]
-        return wide_ref[x, y, 32:64, :]
+        if 0 <= y <= 23:
+            return wide_ref[x, y, 32:64, :]
+        slot = x + (1 - odd_x) * (5, 3, 0, 0, -3, -5)[x]
+        at = (slot * 3 + (y + 3 if y < 0 else y - 24)) * 32
+        return got_ref[0 if y < 0 else 1, pl.ds(pl.multiple_of(at, 32), 32), :]
 
     for x in range(6):
         v = jnp.concatenate([row(x, -1), row(x, 24)], axis=0).astype(F32)
@@ -268,8 +282,8 @@
     rim_up = dot(wup_ref[...], win_ref[...])
 
     upper = lane_ids((64, 128)) >= 64
-    before = got_lo_ref[576:640, :].astype(F32)
-    after = got_hi_ref[576:640, :].astype(F32)
+    before = got_ref[0, 576:640, :].astype(F32)
+    after = got_ref[1, 576:640, :].astype(F32)
     rim_tilt = (
         jnp.where(upper, pltpu.roll(before, 64, 1), after),
         jnp.where(upper, before, pltpu.roll(after, 64, 1)),
@@ -309,12 +323,16 @@
             high = ups[m] + downs[m + 1]
             total_ref[x, m] = tap_sum(1, x, m) + jnp.where(upper, high, low)
     back_ref[...] = total_ref[1:3, 0:6]
-    before = got_lo_ref[640:672, :].astype(F32)
-    after = got_hi_ref[640:672, :].astype(F32)
-    for x, face_ref, side_ref in ((0, face_lo_ref, pool_lo_ref), (3, face_hi_ref, pool_hi_ref)):
-        face_ref[0:192, :] = total_ref[x, 0:6].astype(BF16).reshape(192, 128)
-        face_ref[192:384, :] = side_ref[...]
-        rows = (before[x * 8 : x * 8 + 8], st_ref[x].reshape(192, 128), after[x * 8 : x * 8 + 8])
+    before = got_ref[0, 640:672, :].astype(F32)
+    after = got_ref[1, 640:672, :].astype(F32)
+    for face_ref, last in ((face1_ref, 1 - odd_x), (face2_ref, odd_x)):
+        face_ref[0:192, :] = total_ref[3 * last].astype(BF16).reshape(192, 128)
+        face_ref[192:384, :] = pooled_ref[last].reshape(192, 128)
+        rows = (
+            jnp.where(last == 1, before[24:32], before[0:8]),
+            st_ref[3 * last].reshape(192, 128),
+            jnp.where(last == 1, after[24:32], after[0:8]),
+        )
         face_ref[384:592, :] = jnp.concatenate(rows, axis=0).astype(BF16)
 
 
@@ -383,11 +401,15 @@
 
 
 def encoder_body(
-    acc_ref, edge_ref, back_ref, rim_lo_ref, rim_hi_ref, got_lo_ref, got_hi_ref, slope_ref, w_ref, up_ref,
+    acc_ref, edge_ref, back_ref, rim1_ref, rim2_ref, got1_ref, got2_ref, slope_ref, w_ref, up_ref,
     mid_ref, gmid_ref, st_ref, dec_ref,
-    rows_far, own_ref, face_lo_ref, face_hi_ref, edge_lo_ref, edge_hi_ref,
-    enc_ref, wide_ref, total_ref, we_ref, rows_ref, sext_ref, sum_ref, sems,
+    rows_far, own_ref, face1_ref, face2_ref, edge_lo_ref, edge_hi_ref,
+    enc_ref, wide_ref, total_ref, we_ref, rows_ref, sext_ref, sum_ref, got_ref, sems,
 ):
+    odd_x = parity("gx")
+    got_ref[1 - odd_x] = got1_ref[...]
+    got_ref[odd_x] = got2_ref[...]
+    got_lo_ref, got_hi_ref = got_ref.at[0], got_ref.at[1]
     writes = fetch([(dec_ref, rows_far.at[0:736])], sems.at[0])
 
     def beyond(ref):
@@ -409,8 +431,7 @@
     sext_ref[1:5, 1:25] = st_ref[...]
     sext_ref[0] = got_lo_ref[384:592, :].astype(F32).reshape(26, 8, 128)
     sext_ref[5] = got_hi_ref[384:592, :].astype(F32).reshape(26, 8, 128)
-    before = rim_lo_ref[640:672, :].astype(F32)
-    after = rim_hi_ref[640:672, :].astype(F32)
+    before, after = in_order("gy", rim1_ref[640:672, :].astype(F32), rim2_ref[640:672, :].astype(F32))
     for x in range(4):
         sext_ref[x + 1, 0] = before[x * 8 : x * 8 + 8]
         sext_ref[x + 1, 25] = after[x * 8 : x * 8 + 8]
@@ -476,30 +497,32 @@
     rows_ref[432:544, :] = jnp.concatenate([genc, jnp.zeros((40, 128), F32)], axis=0).astype(BF16)
     writes += fetch([(rows_ref.at[432:544], rows_far.at[1168:1280])], sems.at[2])
     own_ref[...] = total_ref[1:5, 1:25]
-    face_lo_ref[...] = total_ref[0].reshape(208, 128).astype(BF16)
-    face_hi_ref[...] = total_ref[5].reshape(208, 128).astype(BF16)
+    face1_ref[...] = total_ref[5 - 5 * odd_x].reshape(208, 128).astype(BF16)
+    face2_ref[...] = total_ref[5 * odd_x].reshape(208, 128).astype(BF16)
     edge_lo_ref[...] = total_ref[1:5, 0]
     edge_hi_ref[...] = total_ref[1:5, 25]
     for wait in writes:
         wait()
 
 
-def corner_body(edge_lo_ref, edge_hi_ref, lo_ref, hi_ref, col_lo_ref, col_hi_ref):
-    before = lo_ref[...].astype(F32)
-    after = hi_ref[...].astype(F32)
-    for edge_ref, at, col_ref in ((edge_lo_ref, 0, col_lo_ref), (edge_hi_ref, 200, col_hi_ref)):
+def corner_body(edge_lo_ref, edge_hi_ref, got1_ref, got2_ref, col1_ref, col2_ref):
+    before, after = in_order("gx", got1_ref[...].astype(F32), got2_ref[...].astype(F32))
+    cols = []
+    for edge_ref, at in ((edge_lo_ref, 0), (edge_hi_ref, 200)):
         rows = [edge_ref[0] + before[at : at + 8], edge_ref[1], edge_ref[2], edge_ref[3] + after[at : at + 8]]
-        col_ref[...] = jnp.concatenate(rows, axis=0).astype(BF16)
-
-
-def final_body(cot_ref, own_ref, lo_ref, hi_ref, ylo_ref, yhi_ref, grad_ref):
-    before = ylo_ref[...].astype(F32)
-    after = yhi_ref[...].astype(F32)
+        cols.append(jnp.concatenate(rows, axis=0))
+    first, second = in_order("gy", *cols)
+    col1_ref[...] = first.astype(BF16)
+    col2_ref[...] = second.astype(BF16)
+
+
+def final_body(cot_ref, own_ref, got1_ref, got2_ref, end1_ref, end2_ref, grad_ref):
+    sides = in_order("gx", got1_ref[...].astype(F32), got2_ref[...].astype(F32))
+    before, after = in_order("gy", end1_ref[...].astype(F32), end2_ref[...].astype(F32))
     for x in range(4):
         total = own_ref[x]
         if x in (0, 3):
-            side = (lo_ref if x == 0 else hi_ref)[...].astype(F32)
-            total = total + side[8:200].reshape(24, 8, 128)
+            total = total + sides[x // 3][8:200].reshape(24, 8, 128)
         at = slice(x * 8, x * 8 + 8)
         ends = [before[at][None], jnp.zeros((22, 8, 128), F32), after[at][None]]
         total = total + jnp.concatenate(ends, axis=0)
@@ -571,11 +594,12 @@
     return jnp.asarray(table.reshape(256, 256), BF16)
 
 
-def both_ways(low, high, axis):
-    ends = lax.axis_size(axis) - 1
-    from_before = lax.ppermute(high, axis, [(i, i + 1) for i in range(ends)])
-    from_after = lax.ppermute(low, axis, [(i + 1, i) for i in range(ends)])
-    return from_before, from_after
+def swaps(first, second, axis):
+    count = lax.axis_size(axis)
+    pairs = [(i, i + 1) for i in range(0, count - 1, 2)], [(i, i + 1) for i in range(1, count - 1, 2)]
+    return tuple(
+        lax.ppermute(v, axis, ahead + [(b, a) for a, b in ahead]) for v, ahead in zip((first, second), pairs)
+    )
 
 
 def on_device(
@@ -592,7 +616,7 @@
     enc_w = enc_kernel.transpose(2, 3, 4, 1, 0)
 
     plane = sds((24, 32, 128), BF16)
-    delta_lo, delta_hi = call(
+    face1, face2 = call(
         face_body,
         [plane, plane],
         [
@@ -606,11 +630,11 @@
         (dec_pre, cotangent, out_kernel),
         200 << 20, 56, far=3, far_outs=2,
     )
-    xlo, xhi = both_ways(delta_lo, delta_hi, "gx")
+    got1, got2 = swaps(face1, face2, "gx")
     mid_blocks = mid_pre.reshape(64, 2, 6, 2, 64).transpose(1, 2, 0, 3, 4).reshape(2, 6, 64, 128)
     (
         delta, head_grad, hidden, enc_slope, pooled, hidden_mid, mid_slope, state,
-        tail_lo, tail_hi, pool_lo, pool_hi,
+        tail_lo, tail_hi,
     ) = call(
         forward_body,
         [
@@ -624,19 +648,21 @@
             sds((4, 24, 8, 128), F32),
             sds((96, 128), BF16),
             sds((96, 128), BF16),
-            sds((192, 128), BF16),
-            sds((192, 128), BF16),
         ],
         [],
         (dec_pre, cotangent, out_kernel, enc_pre, state_now, mid_blocks, pool),
         600 << 20, 16,
     )
 
-    def column(at, tail):
-        rows = (xlo[at], delta_lo[at], delta[0, at], delta[1, at], delta_hi[at], xhi[at], tail)
-        return jnp.concatenate([v.reshape(-1, 128) for v in rows])
-
-    ylo, yhi = both_ways(column(slice(0, 3), tail_lo), column(slice(21, 24), tail_hi), "gy")
+    odd_y = parity("gy")
+
+    def column(start, tail):
+        planes = (got1, face1, delta[0], delta[1], face2, got2)
+        rows = [lax.dynamic_slice_in_dim(v, start, 3, axis=0).reshape(96, 128) for v in planes]
+        return jnp.concatenate(rows + [tail])
+
+    tails = in_order("gy", tail_lo, tail_hi)
+    rim1, rim2 = swaps(column(21 - 21 * odd_y, tails[0]), column(21 * odd_y, tails[1]), "gy")
     acc, wide, win, up, wskip, wmid, wup = call(
         inner_body,
         [
@@ -649,10 +675,10 @@
             sds((64, 864), BF16),
         ],
         [],
-        (xlo, delta_lo, delta, delta_hi, xhi, pool, dec_w, mid_w),
+        (got1, face1, delta, face2, got2, pool, dec_w, mid_w),
         3 << 30, 24,
     )
-    edge, rim_wide, rim_win, mid_wide, back, face_lo, face_hi = call(
+    edge, rim_wide, rim_win, mid_wide, back, face1, face2 = call(
         outer_body,
         [
             sds((4, 2, 32, 128), F32),
@@ -663,11 +689,11 @@
             sds((592, 128), BF16),
             sds((592, 128), BF16),
         ],
-        [pltpu.VMEM((4, 6, 32, 128), F32)],
-        (ylo, yhi, wide, up, mid_slope, state, pool_lo, pool_hi, pool, wup, wskip, wmid),
+        [pltpu.VMEM((4, 6, 32, 128), F32), pltpu.VMEM((2, 672, 128), BF16)],
+        (rim1, rim2, wide, up, mid_slope, state, pooled, pool, wup, wskip, wmid),
         1 << 30, 24,
     )
-    got_lo, got_hi = both_ways(face_lo, face_hi, "gx")
+    got1, got2 = swaps(face1, face2, "gx")
     dec_rows, mid_grad = call(
         dec_grad_body,
         [sds((736, 128), BF16), sds((288, 192), F32)],
@@ -675,8 +701,8 @@
         (wide, rim_wide, hidden, win, rim_win, hidden_mid, head_grad, pooled, mid_wide),
         3 << 30, 20,
     )
-    dec_rows, mid_grad, got_lo, got_hi = lax.optimization_barrier((dec_rows, mid_grad, got_lo, got_hi))
-    rows, own, face_lo, face_hi, edge_lo, edge_hi = call(
+    dec_rows, mid_grad, got1, got2 = lax.optimization_barrier((dec_rows, mid_grad, got1, got2))
+    rows, own, face1, face2, edge_lo, edge_hi = call(
         encoder_body,
         [
             sds((1280, 128), BF16),
@@ -694,15 +720,16 @@
             pltpu.VMEM((544, 128), BF16),
             pltpu.VMEM((6, 26, 8, 128), F32),
             pltpu.VMEM((72, 96), F32),
+            pltpu.VMEM((2, 592, 128), BF16),
             pltpu.SemaphoreType.DMA((3, 1)),
         ],
         (
-            acc, edge, back, ylo, yhi, got_lo, got_hi, enc_slope, enc_w, up_matrix(),
+            acc, edge, back, rim1, rim2, got1, got2, enc_slope, enc_w, up_matrix(),
             mid_wide, mid_grad, state, dec_rows,
         ),
         2 << 30, 24, far_outs=1,
     )
-    last_lo, last_hi = both_ways(face_lo, face_hi, "gx")
+    last1, last2 = swaps(face1, face2, "gx")
 
     axes = ("dp", "gx", "gy")
     count = lax.axis_size(axes)
@@ -720,12 +747,12 @@
         (pieces,),
         1 << 20, 8, far=1, far_outs=1,
     )
-    shares, last_lo, last_hi = lax.optimization_barrier((shares, last_lo, last_hi))
+    shares, last1, last2 = lax.optimization_barrier((shares, last1, last2))
     rows = lax.all_to_all(shares, axes, 0, 0).reshape(1280, 128)
-    col_lo, col_hi = call(
-        corner_body, [sds((32, 128), BF16)] * 2, [], (edge_lo, edge_hi, last_lo, last_hi), 1 << 16, 4
-    )
-    end_lo, end_hi = both_ways(col_lo, col_hi, "gy")
+    col1, col2 = call(
+        corner_body, [sds((32, 128), BF16)] * 2, [], (edge_lo, edge_hi, last1, last2), 1 << 16, 4
+    )
+    end1, end2 = swaps(col1, col2, "gy")
     genc, gmid, gdec, ghead = call(
         functools.partial(unpack_body, grad_scale),
         [sds((3, 3, 3, 8, 32), F32), sds((3, 3, 3, 32, 64), F32), sds((3, 3, 3, 32, 96), F32), sds((8, 32), F32)],
@@ -733,12 +760,12 @@
         (rows,),
         1 << 20, 12,
     )
-    genc, end_lo, end_hi = lax.optimization_barrier((genc, end_lo, end_hi))
+    genc, end1, end2 = lax.optimization_barrier((genc, end1, end2))
     (state_grad,) = call(
         final_body,
         [sds((8, 4, 24, 128), BF16)],
         [],
-        (cotangent, own, last_lo, last_hi, end_lo, end_hi),
+        (cotangent, own, last1, last2, end1, end2),
         1 << 20, 8,
     )
     return (

time: 94 us -> 91.1 us (0.969)
  starting transfers between devices: 47.3 us -> 38.6 us
  local copies, waits for them, and re-layouts: 2.49 us -> 8.05 us
  Pallas kernels: 22.4 us -> 23.6 us
    ppermute x10, starting transfers between devices: 28.3 us -> 19.8 us  [swaps(): lax.ppermute(v, axis, ahead + [(b, a) for a, b in ahead])]
    ppermute x10, waiting for transfers between devices: 7.45 us -> 1.69 us  [swaps(): lax.ppermute(v, axis, ahead + [(b, a) for a, b in ahead])]
    unnamed x36 -> x60, local copies, waits for them, and re-layouts: 0.17 us -> 4.79 us
    all_to_all x1, waiting for transfers between devices: 7.24 us -> 9.71 us  [on_device(): pieces = lax.all_to_all(rows.reshape(count, share, 2, 128), axes, 0, 0)]
    all_to_all x1, waiting for transfers between devices: 5.45 us -> 7.92 us  [on_device(): rows = lax.all_to_all(shares, axes, 0, 0).reshape(1280, 128)]
    dynamic_slice x0 -> x3, local copies, waits for them, and re-layouts: none -> 1.76 us  [column(): lax.dynamic_slice_in_dim(v, start, 3, axis=0).reshape(96, 128)]
    all_to_all x1, starting transfers between devices: 6.44 us -> 4.8 us  [on_device(): rows = lax.all_to_all(shares, axes, 0, 0).reshape(1280, 128)]
    all_to_all x1, starting transfers between devices: 12.5 us -> 13.9 us  [on_device(): pieces = lax.all_to_all(rows.reshape(count, share, 2, 128), axes, 0, 0)]
  transfers between devices with their start and end apart: 12 -> 12, of which waited for: 5 -> 3; matrix products, arithmetic and copies ran while one was open for 3% -> 3% of each run, Pallas kernels for 15% -> 17%
where the time goes in v3:
time: 91.1 us; the launch traced here: 90.7 us
  starting transfers between devices  38.6 us (42%)
  Pallas kernels  23.6 us (26%)
  waiting for transfers between devices  19.3 us (21%)
  local copies, waits for them, and re-layouts  8.05 us (9%)
  between operations  1.09 us (1%)
    pallas_call x10, Pallas kernels, call(): pl.pallas_call(body, out_shape=outs, in_specs=[HBM] * far + [VMEM] * (len...  23.6 us
    ppermute x10, starting transfers between devices, swaps(): lax.ppermute(v, axis, ahead + [(b, a) for a, b in ahead])  19.8 us
    all_to_all x1, starting transfers between devices, on_device(): pieces = lax.all_to_all(rows.reshape(count, share, 2, 128), axes, 0, 0)  13.9 us
    all_to_all x1, waiting for transfers between devices, on_device(): pieces = lax.all_to_all(rows.reshape(count, share, 2, 128), axes, 0, 0)  9.71 us
    all_to_all x1, waiting for transfers between devices, on_device(): rows = lax.all_to_all(shares, axes, 0, 0).reshape(1280, 128)  7.92 us
    all_to_all x1, starting transfers between devices, on_device(): rows = lax.all_to_all(shares, axes, 0, 0).reshape(1280, 128)  4.8 us
    unnamed x60, local copies, waits for them, and re-layouts  4.79 us
  transfers between devices with their start and end apart: 12, of which 3 were waited for; matrix products, arithmetic and copies ran while one was open for 3% of the time, Pallas kernels for 17%

profile of v3, /device:TPU:1, one launch (start us, length us, event | category | flops | bytes accessed | tf_op | source)
XLA Modules:
  0.0 90.7 jit_solution(754104028574945636)
XLA Ops:
  0.7 2.5 %shard_map.146 = (bf16[24,32,128]{2,1,0:T(8,128)(2,1)}, bf16[24,32,128]{2,1,0:T(8,128)(2,1)}) custom-call(bf16[32,4,24,128]{3,2,1,0:T(8,128)(2,1)} %bitcast.29, bf16[8,4,24,128]{3,2,1,0:T(8,128)(2,1)} %bitcast.31, bf16[8,32]{1,0:T(8,128)(2,1)} %head_ref.1), custom_call_target="tpu_custom_call" | custom-call | flops 209715200 | bytes 4194304 | tf_op jit(solution)/shard_map/pallas_call | solution.py:21
  3.2 2.5 %collective-permute-start = (bf16[24,32,128]{2,1,0:T(8,128)(2,1)}, bf16[24,32,128]{2,1,0:T(8,128)(2,1)}, u32[]{:S(2)}, u32[]{:S(2)}) collective-permute-start(bf16[24,32,128]{2,1,0:T(8,128)(2,1)} %get-tuple-element.55.face1_ref), channel_id=1, source_target_pairs={{0,8},{16,24},{32,40},{48,56},{8,0},{24,16},{40,32},{56,48},{1,9},... | collective-permute-start | bytes 589832 | tf_op jit(solution)/shard_map/ppermute | solution.py:601
  5.7 1.3 %collective-permute-start.1 = (bf16[24,32,128]{2,1,0:T(8,128)(2,1)}, bf16[24,32,128]{2,1,0:T(8,128)(2,1)}, u32[]{:S(2)}, u32[]{:S(2)}) collective-permute-start(bf16[24,32,128]{2,1,0:T(8,128)(2,1)} %get-tuple-element.57.face2_ref), channel_id=1, source_target_pairs={{8,16},{24,32},{40,48},{16,8},{32,24},{48,40},{9,17},{25,33},{41,4... | collective-permute-start | bytes 589832 | tf_op jit(solution)/shard_map/ppermute | solution.py:601
  7.1 1.3 %copy.18 = bf16[64,2,6,2,64]{4,3,0,2,1:T(2,128)(2,1)S(1)} copy(bf16[64,2,6,2,64]{4,1,3,2,0:T(2,128)(2,1)} %bitcast.41) | data formatting | bytes 393216 | tf_op jit(solution)/shard_map/reshape;squeeze | solution.py:634
  8.6 2.2 %shard_map.147 = (bf16[2,24,32,128]{3,2,1,0:T(8,128)(2,1)S(1)}, f32[8,32]{1,0:T(8,128)S(1)}, bf16[4,24,32,128]{3,2,1,0:T(8,128)(2,1)S(1)}, f32[4,24,32,128]{3,2,...) custom-call(bf16[32,4,24,128]{3,2,1,0:T(8,128)(2,1)S(1)} %bitcast.30, ...), custom_call_target="tpu_custom_call" | custom-call | flops 629145600 | bytes 4194304 | tf_op jit(solution)/shard_map/pallas_call | solution.py:21
  12.7 1.2 %copy-done.14 = f32[4,24,32,128]{3,2,1,0:T(8,128)} copy-done((f32[4,24,32,128]{3,2,1,0:T(8,128)}, f32[4,24,32,128]{3,2,1,0:T(8,128)S(1)}, u32[]{:S(2)}) %copy-start.14) | copy-done | bytes 1572888
  13.9 0.9 copy-done.16
  15.5 0.9 %constant_dynamic-slice_fusion.1 = (bf16[3,32,128]{2,1,0:T(8,128)(2,1)S(1)}, bf16[3,32,128]{2,1,0:T(8,128)(2,1)S(1)}, bf16[3,32,128]{2,1,0:T(8,128)(2,1)S(1)}, bf16[3,32,128]{2,1,0:T(8,128)(2,1)S(1)}) fusion(bf16[24,32,128]{2,1,0:T(8,128)(2,1)} %get-tuple-element.57.face2_ref, s32[]{:T(128)S(6)} %select_n.31, s32[]{:T(128)S(6)} %select_n.28, ...), kind=kLoop, calls=%fused_computation.16 | loop fusion | bytes 196616 | tf_op jit(solution)/shard_map/dynamic_slice | solution.py:661
  18.2 5.2 %collective-permute-start.2 = (bf16[672,128]{1,0:T(8,128)(2,1)S(1)}, bf16[672,128]{1,0:T(8,128)(2,1)S(1)}, u32[]{:S(2)}, u32[]{:S(2)}) collective-permute-start(bf16[672,128]{1,0:T(8,128)(2,1)S(1)} %get-tuple-element.120), channel_id=1, source_target_pairs={{0,1},{2,3},{4,5},{6,7},{1,0},{3,2},{5,4},{7,6},{8,9},{10,11},{12,... | collective-permute-start | bytes 516104 | tf_op jit(solution)/shard_map/ppermute | solution.py:601
  23.4 5.9 %shard_map.148 = (f32[4,26,32,128]{3,2,1,0:T(8,128)S(1)}, bf16[6,24,96,128]{3,2,1,0:T(8,128)(2,1)S(1)}, bf16[864,1024]{1,0:T(8,128)(2,1)S(1)}, f32[64,1024]{1,0:...) custom-call(bf16[24,32,128]{2,1,0:T(8,128)(2,1)} %collective-permute-done.got1_, ...), custom_call_target="tpu_custom_call" | custom-call | flops 3221225472 | bytes 4194304 | tf_op jit(solution)/shard_map/pallas_call | solution.py:21
  29.3 1.7 %collective-permute-done.2.got1_ref.rim1_ref = bf16[672,128]{1,0:T(8,128)(2,1)S(1)} collective-permute-done((bf16[672,128]{1,0:T(8,128)(2,1)S(1)}, bf16[672,128]{1,0:T(8,128)(2,1)S(1)}, u32[]{:S(2)}, u32[]{:S(2)}) %collective-permute-start.2) | collective-permute-done | bytes 172064 | tf_op jit(solution)/shard_map/ppermute | solution.py:601
  31.0 1.9 %shard_map.149 = (f32[4,2,32,128]{3,2,1,0:T(8,128)S(1)}, bf16[6,2,96,128]{3,2,1,0:T(8,128)(2,1)S(1)}, bf16[864,768]{1,0:T(8,128)(2,1)S(1)}, bf16[192,1792]{1,0:T...) custom-call(bf16[672,128]{1,0:T(8,128)(2,1)S(1)} %collective-permute-don, ...), custom_call_target="tpu_custom_call" | custom-call | flops 1073741824 | bytes 4194304 | tf_op jit(solution)/shard_map/pallas_call | solution.py:21
  32.9 3.0 %collective-permute-start.4 = (bf16[592,128]{1,0:T(8,128)(2,1)S(1)}, bf16[592,128]{1,0:T(8,128)(2,1)S(1)}, u32[]{:S(2)}, u32[]{:S(2)}) collective-permute-start(bf16[592,128]{1,0:T(8,128)(2,1)S(1)} %get-tuple-element.80), channel_id=1, source_target_pairs={{0,8},{16,24},{32,40},{48,56},{8,0},{24,16},{40,32},{56,48},{1,9},... | collective-permute-start | bytes 454664 | tf_op jit(solution)/shard_map/ppermute | solution.py:601
  35.8 0.8 collective-permute-start.5
  36.7 4.5 %shard_map.150 = (bf16[736,128]{1,0:T(8,128)(2,1)S(1)}, f32[288,192]{1,0:T(8,128)S(1)}) custom-call(bf16[6,24,96,128]{3,2,1,0:T(8,128)(2,1)S(1)} %get-tuple-element.61.wide_ref, bf16[6,2,96,128]{3,2,1,0:T(8,128)(2,1)S(1)} %get-tuple-element.71.rim_ref, bf16[4,24,32,128]{3,2,1,0:T(8,128)(2,1)S(1)} %copy-done.17, ...), custom_call_target="tpu_custom_call" | custom-call | flops 3221225472 | bytes 4194304 | tf_op jit(solution)/shard_map/pallas_call | solution.py:21
  41.3 3.2 %shard_map.151 = (bf16[1280,128]{1,0:T(8,128)(2,1)}, f32[4,24,8,128]{3,2,1,0:T(8,128)S(1)}, bf16[208,128]{1,0:T(8,128)(2,1)S(1)}, bf16[208,128]{1,0:T(8,128)(2,1...) custom-call(f32[4,26,32,128]{3,2,1,0:T(8,128)S(1)} %get-tuple-element.58.acc_ref, ...), custom_call_target="tpu_custom_call" | custom-call | flops 2147483648 | bytes 4194304 | tf_op jit(solution)/shard_map/pallas_call | solution.py:21
  44.5 13.9 %all-to-all-start = ((bf16[128,5,2,128]{3,2,1,0:T(2,128)(2,1)}), bf16[128,5,2,128]{3,2,1,0:T(2,128)(2,1)S(1)}, u32[]{:S(2)}, u32[]{:S(2)}) async-start(bf16[128,5,2,128]{3,2,1,0:T(2,128)(2,1)} %bitcast.21), calls=%async_computation | async-start | bytes 655360 | tf_op jit(solution)/shard_map/all_to_all | solution.py:737
  58.5 1.6 %collective-permute-start.6 = (bf16[208,128]{1,0:T(8,128)(2,1)S(1)}, bf16[208,128]{1,0:T(8,128)(2,1)S(1)}, u32[]{:S(2)}, u32[]{:S(2)}) collective-permute-start(bf16[208,128]{1,0:T(8,128)(2,1)S(1)} %get-tuple-element.89), channel_id=1, source_target_pairs={{0,8},{16,24},{32,40},{48,56},{8,0},{24,16},{40,32},{56,48},{1,9},... | collective-permute-start | bytes 159752 | tf_op jit(solution)/shard_map/ppermute | solution.py:601
  60.7 9.7 %all-to-all-done.pieces_far = bf16[128,5,2,128]{3,2,1,0:T(2,128)(2,1)S(1)} async-done(((bf16[128,5,2,128]{3,2,1,0:T(2,128)(2,1)}), bf16[128,5,2,128]{3,2,1,0:T(2,128)(2,1)S(1)}, u32[]{:S(2)}, u32[]{:S(2)}) %all-to-all-start) | async-done | bytes 327712 | tf_op jit(solution)/shard_map/all_to_all | solution.py:737
  70.4 1.4 %shard_map.152 = bf16[128,5,2,128]{3,2,1,0:T(2,128)(2,1)} custom-call(bf16[128,5,2,128]{3,2,1,0:T(2,128)(2,1)S(1)} %all-to-all-done.pieces_far), custom_call_target="tpu_custom_call" | custom-call | flops 1048576 | bytes 4194304 | tf_op jit(solution)/shard_map/pallas_call | solution.py:21
  71.8 4.8 %all-to-all-start.1 = ((bf16[128,5,2,128]{3,2,1,0:T(2,128)(2,1)}), bf16[128,5,2,128]{3,2,1,0:T(2,128)(2,1)S(1)}, u32[]{:S(2)}, u32[]{:S(2)}) async-start(bf16[128,5,2,128]{3,2,1,0:T(2,128)(2,1)} %shard_map.152), calls=%async_computation.1 | async-start | bytes 655360 | tf_op jit(solution)/shard_map/all_to_all | solution.py:751
  76.7 3.4 %collective-permute-start.8 = (bf16[32,128]{1,0:T(8,128)(2,1)S(1)}, bf16[32,128]{1,0:T(8,128)(2,1)S(1)}, u32[]{:S(2)}, u32[]{:S(2)}) collective-permute-start(bf16[32,128]{1,0:T(8,128)(2,1)S(1)} %get-tuple-element.97), channel_id=1, source_target_pairs={{0,1},{2,3},{4,5},{6,7},{1,0},{3,2},{5,4},{7,6},{8,9},{10,11},{12,... | collective-permute-start | bytes 24584 | tf_op jit(solution)/shard_map/ppermute | solution.py:601
  80.7 7.9 %all-to-all-done.1 = bf16[128,5,2,128]{3,2,1,0:T(2,128)(2,1)S(1)} async-done(((bf16[128,5,2,128]{3,2,1,0:T(2,128)(2,1)}), bf16[128,5,2,128]{3,2,1,0:T(2,128)(2,1)S(1)}, u32[]{:S(2)}, u32[]{:S(2)}) %all-to-all-start.1) | async-done | bytes 327712 | tf_op jit(solution)/shard_map/all_to_all | solution.py:751
  88.6 1.2 %shard_map.153 = (f32[3,3,3,8,32]{4,3,2,1,0:T(8,128)}, f32[3,3,3,32,64]{4,3,2,1,0:T(8,128)}, f32[3,3,3,32,96]{4,3,2,1,0:T(8,128)}, f32[8,32]{1,0:T(8,128)}) custom-call(bf16[1280,128]{1,0:T(8,128)(2,1)S(1)} %bitcast.34), custom_call_target="tpu_custom_call" | custom-call | flops 1048576 | bytes 4194304 | tf_op jit(solution)/shard_map/pallas_call | solution.py:21
  (77 shorter events, 6.6 us)
Async XLA Ops:
  0.6 7.9 %copy-start.2 = (bf16[256,384]{1,0:T(8,128)(2,1)S(1)}, bf16[256,384]{1,0:T(8,128)(2,1)}, u32[]{:S(2)}) copy-start(bf16[256,384]{1,0:T(8,128)(2,1)} %constant.22.clone.pool_ref) | copy-start | bytes 589828
  0.6 7.9 %copy-start.13 = (bf16[8,32]{1,0:T(8,128)(2,1)S(1)}, bf16[8,32]{1,0:T(8,128)(2,1)}, u32[]{:S(2)}) copy-start(bf16[8,32]{1,0:T(8,128)(2,1)} %head_ref.1) | copy-start | bytes 1540
  0.7 7.9 %copy-start.1 = (bf16[1,8,4,24,128]{4,3,2,1,0:T(8,128)(2,1)S(1)}, bf16[1,8,4,24,128]{4,3,2,1,0:T(8,128)(2,1)}, u32[]{:S(2)}) copy-start(bf16[1,8,4,24,128]{4,3,2,1,0:T(8,128)(2,1)} %param.15) | copy-start | bytes 589828
  0.7 7.9 %copy-start = (bf16[1,32,4,24,128]{4,3,2,1,0:T(8,128)(2,1)S(1)}, bf16[1,32,4,24,128]{4,3,2,1,0:T(8,128)(2,1)}, u32[]{:S(2)}) copy-start(bf16[1,32,4,24,128]{4,3,2,1,0:T(8,128)(2,1)} %param.14) | copy-start | bytes 2359300
  0.7 7.9 %copy-start.3 = (bf16[1,32,4,24,128]{4,3,2,1,0:T(8,128)(2,1)S(1)}, bf16[1,32,4,24,128]{4,3,2,1,0:T(8,128)(2,1)}, u32[]{:S(2)}) copy-start(bf16[1,32,4,24,128]{4,3,2,1,0:T(8,128)(2,1)} %param.12) | copy-start | bytes 2359300
  0.7 7.9 %copy-start.4 = (bf16[1,8,4,24,128]{4,3,2,1,0:T(8,128)(2,1)S(1)}, bf16[1,8,4,24,128]{4,3,2,1,0:T(8,128)(2,1)}, u32[]{:S(2)}) copy-start(bf16[1,8,4,24,128]{4,3,2,1,0:T(8,128)(2,1)} %param.11) | copy-start | bytes 589828
  3.2 13.3 %collective-permute-start = (bf16[24,32,128]{2,1,0:T(8,128)(2,1)}, bf16[24,32,128]{2,1,0:T(8,128)(2,1)}, u32[]{:S(2)}, u32[]{:S(2)}) collective-permute-start(bf16[24,32,128]{2,1,0:T(8,128)(2,1)} %get-tuple-element.55.face1_ref), channel_id=1, source_target_pairs={{0,8},{16,24},{32,40},{48,56},{8,0},{24,16},{40,32},{56,48},{1,9},... | collective-permute-start | bytes 589832 | tf_op jit(solution)/shard_map/ppermute | solution.py:601
  5.7 10.8 %collective-permute-start.1 = (bf16[24,32,128]{2,1,0:T(8,128)(2,1)}, bf16[24,32,128]{2,1,0:T(8,128)(2,1)}, u32[]{:S(2)}, u32[]{:S(2)}) collective-permute-start(bf16[24,32,128]{2,1,0:T(8,128)(2,1)} %get-tuple-element.57.face2_ref), channel_id=1, source_target_pairs={{8,16},{24,32},{40,48},{16,8},{32,24},{48,40},{9,17},{25,33},{41,4... | collective-permute-start | bytes 589832 | tf_op jit(solution)/shard_map/ppermute | solution.py:601
  15.5 8.0 %copy-start.11 = (bf16[24,32,128]{2,1,0:T(8,128)(2,1)S(1)}, bf16[24,32,128]{2,1,0:T(8,128)(2,1)}, u32[]{:S(2)}) copy-start(bf16[24,32,128]{2,1,0:T(8,128)(2,1)} %get-tuple-element.55.face1_ref) | copy-start | bytes 589828
  15.5 8.0 %copy-start.12 = (bf16[24,32,128]{2,1,0:T(8,128)(2,1)S(1)}, bf16[24,32,128]{2,1,0:T(8,128)(2,1)}, u32[]{:S(2)}) copy-start(bf16[24,32,128]{2,1,0:T(8,128)(2,1)} %get-tuple-element.57.face2_ref) | copy-start | bytes 589828
  15.5 8.0 %copy-start.18 = (bf16[32,96,3,3,3]{1,0,4,3,2:T(8,128)(2,1)S(1)}, bf16[32,96,3,3,3]{1,0,4,3,2:T(8,128)(2,1)}, u32[]{:S(2)}) copy-start(bf16[32,96,3,3,3]{1,0,4,3,2:T(8,128)(2,1)} %param.18) | copy-start | bytes 497668
  15.5 8.0 %copy-start.19 = (bf16[64,32,3,3,3]{0,1,4,3,2:T(8,128)(2,1)S(1)}, bf16[64,32,3,3,3]{0,1,4,3,2:T(8,128)(2,1)}, u32[]{:S(2)}) copy-start(bf16[64,32,3,3,3]{0,1,4,3,2:T(8,128)(2,1)} %param.17) | copy-start | bytes 331780
  17.5 11.8 %collective-permute-start.3 = (bf16[672,128]{1,0:T(8,128)(2,1)S(1)}, bf16[672,128]{1,0:T(8,128)(2,1)S(1)}, u32[]{:S(2)}, u32[]{:S(2)}) collective-permute-start(bf16[672,128]{1,0:T(8,128)(2,1)S(1)} %get-tuple-element.119), channel_id=1, source_target_pairs={{1,2},{3,4},{5,6},{2,1},{4,3},{6,5},{9,10},{11,12},{13,14},{10,9},... | collective-permute-start | bytes 516104 | tf_op jit(solution)/shard_map/ppermute | solution.py:601
  18.2 12.8 %collective-permute-start.2 = (bf16[672,128]{1,0:T(8,128)(2,1)S(1)}, bf16[672,128]{1,0:T(8,128)(2,1)S(1)}, u32[]{:S(2)}, u32[]{:S(2)}) collective-permute-start(bf16[672,128]{1,0:T(8,128)(2,1)S(1)} %get-tuple-element.120), channel_id=1, source_target_pairs={{0,1},{2,3},{4,5},{6,7},{1,0},{3,2},{5,4},{7,6},{8,9},{10,11},{12,... | collective-permute-start | bytes 516104 | tf_op jit(solution)/shard_map/ppermute | solution.py:601
  23.4 7.6 %copy-start.6 = (bf16[2,6,32,128]{3,2,1,0:T(8,128)(2,1)S(1)}, bf16[2,6,32,128]{3,2,1,0:T(8,128)(2,1)}, u32[]{:S(2)}) copy-start(bf16[2,6,32,128]{3,2,1,0:T(8,128)(2,1)} %copy-done.5) | copy-start | bytes 294916
  31.0 5.7 %copy-start.21 = (bf16[2,6,64,128]{3,2,1,0:T(8,128)(2,1)S(1)}, bf16[2,6,64,128]{3,2,1,0:T(8,128)(2,1)}, u32[]{:S(2)}) copy-start(bf16[2,6,64,128]{3,2,1,0:T(8,128)(2,1)} %copy-done.20) | copy-start | bytes 589828
  32.9 8.4 %collective-permute-start.4 = (bf16[592,128]{1,0:T(8,128)(2,1)S(1)}, bf16[592,128]{1,0:T(8,128)(2,1)S(1)}, u32[]{:S(2)}, u32[]{:S(2)}) collective-permute-start(bf16[592,128]{1,0:T(8,128)(2,1)S(1)} %get-tuple-element.80), channel_id=1, source_target_pairs={{0,8},{16,24},{32,40},{48,56},{8,0},{24,16},{40,32},{56,48},{1,9},... | collective-permute-start | bytes 454664 | tf_op jit(solution)/shard_map/ppermute | solution.py:601
  35.8 5.4 %collective-permute-start.5 = (bf16[592,128]{1,0:T(8,128)(2,1)S(1)}, bf16[592,128]{1,0:T(8,128)(2,1)S(1)}, u32[]{:S(2)}, u32[]{:S(2)}) collective-permute-start(bf16[592,128]{1,0:T(8,128)(2,1)S(1)} %get-tuple-element.81), channel_id=1, source_target_pairs={{8,16},{24,32},{40,48},{16,8},{32,24},{48,40},{9,17},{25,33},{41,4... | collective-permute-start | bytes 454664 | tf_op jit(solution)/shard_map/ppermute | solution.py:601
  44.5 25.9 %all-to-all-start = ((bf16[128,5,2,128]{3,2,1,0:T(2,128)(2,1)}), bf16[128,5,2,128]{3,2,1,0:T(2,128)(2,1)S(1)}, u32[]{:S(2)}, u32[]{:S(2)}) async-start(bf16[128,5,2,128]{3,2,1,0:T(2,128)(2,1)} %bitcast.21), calls=%async_computation | async-start | bytes 655360 | tf_op jit(solution)/shard_map/all_to_all | solution.py:737
  58.5 13.4 %collective-permute-start.6 = (bf16[208,128]{1,0:T(8,128)(2,1)S(1)}, bf16[208,128]{1,0:T(8,128)(2,1)S(1)}, u32[]{:S(2)}, u32[]{:S(2)}) collective-permute-start(bf16[208,128]{1,0:T(8,128)(2,1)S(1)} %get-tuple-element.89), channel_id=1, source_target_pairs={{0,8},{16,24},{32,40},{48,56},{8,0},{24,16},{40,32},{56,48},{1,9},... | collective-permute-start | bytes 159752 | tf_op jit(solution)/shard_map/ppermute | solution.py:601
  60.0 11.8 %collective-permute-start.7 = (bf16[208,128]{1,0:T(8,128)(2,1)S(1)}, bf16[208,128]{1,0:T(8,128)(2,1)S(1)}, u32[]{:S(2)}, u32[]{:S(2)}) collective-permute-start(bf16[208,128]{1,0:T(8,128)(2,1)S(1)} %get-tuple-element.90), channel_id=1, source_target_pairs={{8,16},{24,32},{40,48},{16,8},{32,24},{48,40},{9,17},{25,33},{41,4... | collective-permute-start | bytes 159752 | tf_op jit(solution)/shard_map/ppermute | solution.py:601
  71.8 16.8 %all-to-all-start.1 = ((bf16[128,5,2,128]{3,2,1,0:T(2,128)(2,1)}), bf16[128,5,2,128]{3,2,1,0:T(2,128)(2,1)S(1)}, u32[]{:S(2)}, u32[]{:S(2)}) async-start(bf16[128,5,2,128]{3,2,1,0:T(2,128)(2,1)} %shard_map.152), calls=%async_computation.1 | async-start | bytes 655360 | tf_op jit(solution)/shard_map/all_to_all | solution.py:751
  76.7 13.2 %collective-permute-start.8 = (bf16[32,128]{1,0:T(8,128)(2,1)S(1)}, bf16[32,128]{1,0:T(8,128)(2,1)S(1)}, u32[]{:S(2)}, u32[]{:S(2)}) collective-permute-start(bf16[32,128]{1,0:T(8,128)(2,1)S(1)} %get-tuple-element.97), channel_id=1, source_target_pairs={{0,1},{2,3},{4,5},{6,7},{1,0},{3,2},{5,4},{7,6},{8,9},{10,11},{12,... | collective-permute-start | bytes 24584 | tf_op jit(solution)/shard_map/ppermute | solution.py:601
  80.0 9.8 %collective-permute-start.9 = (bf16[32,128]{1,0:T(8,128)(2,1)S(1)}, bf16[32,128]{1,0:T(8,128)(2,1)S(1)}, u32[]{:S(2)}, u32[]{:S(2)}) collective-permute-start(bf16[32,128]{1,0:T(8,128)(2,1)S(1)} %get-tuple-element.98), channel_id=1, source_target_pairs={{1,2},{3,4},{5,6},{2,1},{4,3},{6,5},{9,10},{11,12},{13,14},{10,9},... | collective-permute-start | bytes 24584 | tf_op jit(solution)/shard_map/ppermute | solution.py:601
  (12 other events, 28.0 us)

commit v4 on v3

--- a/solution.py
+++ b/solution.py
@@ -654,15 +654,13 @@
         600 << 20, 16,
     )
 
-    odd_y = parity("gy")
-
-    def column(start, tail):
-        planes = (got1, face1, delta[0], delta[1], face2, got2)
-        rows = [lax.dynamic_slice_in_dim(v, start, 3, axis=0).reshape(96, 128) for v in planes]
-        return jnp.concatenate(rows + [tail])
-
-    tails = in_order("gy", tail_lo, tail_hi)
-    rim1, rim2 = swaps(column(21 - 21 * odd_y, tails[0]), column(21 * odd_y, tails[1]), "gy")
+
+    def column(at, tail):
+        rows = (got1[at], face1[at], delta[0, at], delta[1, at], face2[at], got2[at], tail)
+        return jnp.concatenate([v.reshape(-1, 128) for v in rows])
+
+    ends = column(slice(0, 3), tail_lo), column(slice(21, 24), tail_hi)
+    rim1, rim2 = swaps(*in_order("gy", *ends), "gy")
     acc, wide, win, up, wskip, wmid, wup = call(
         inner_body,
         [

time: 91.1 us -> 86.9 us (0.954)
  local copies, waits for them, and re-layouts: 8.05 us -> 2.49 us
  starting transfers between devices: 38.6 us -> 42.6 us
  waiting for transfers between devices: 19.3 us -> 17.7 us
  Pallas kernels: 23.6 us -> 22.6 us
    unnamed x60 -> x36, local copies, waits for them, and re-layouts: 4.79 us -> 0.17 us
    ppermute x10, starting transfers between devices: 19.8 us -> 23 us  [swaps(): lax.ppermute(v, axis, ahead + [(b, a) for a, b in ahead])]
    dynamic_slice x3 -> x0, local copies, waits for them, and re-layouts: 1.76 us -> none  [column(): lax.dynamic_slice_in_dim(v, start, 3, axis=0).reshape(96, 128)]
    ppermute x10, waiting for transfers between devices: 1.69 us -> 0.03 us  [swaps(): lax.ppermute(v, axis, ahead + [(b, a) for a, b in ahead])]
    pallas_call x10, Pallas kernels: 23.6 us -> 22.6 us  [call(): pl.pallas_call(body, out_shape=outs, in_specs=[HBM] * far + [VMEM] * (len...]
  transfers between devices with their start and end apart: 12 -> 12, of which waited for: 3 -> 2; matrix products, arithmetic and copies ran while one was open for 3% -> 3% of each run, Pallas kernels for 17% -> 16%
where the time goes in v4:
time: 86.9 us; the launch traced here: 86.5 us
  starting transfers between devices  42.6 us (49%)
  Pallas kernels  22.6 us (26%)
  waiting for transfers between devices  17.7 us (20%)
  local copies, waits for them, and re-layouts  2.49 us (3%)
  between operations  1.08 us (1%)
    ppermute x10, starting transfers between devices, swaps(): lax.ppermute(v, axis, ahead + [(b, a) for a, b in ahead])  23 us
    pallas_call x10, Pallas kernels, call(): pl.pallas_call(body, out_shape=outs, in_specs=[HBM] * far + [VMEM] * (len...  22.6 us
    all_to_all x1, starting transfers between devices, on_device(): pieces = lax.all_to_all(rows.reshape(count, share, 2, 128), axes, 0, 0)  14.8 us
    all_to_all x1, waiting for transfers between devices, on_device(): pieces = lax.all_to_all(rows.reshape(count, share, 2, 128), axes, 0, 0)  9.71 us
    all_to_all x1, waiting for transfers between devices, on_device(): rows = lax.all_to_all(shares, axes, 0, 0).reshape(1280, 128)  7.92 us
    all_to_all x1, starting transfers between devices, on_device(): rows = lax.all_to_all(shares, axes, 0, 0).reshape(1280, 128)  4.8 us
  transfers between devices with their start and end apart: 12, of which 2 were waited for; matrix products, arithmetic and copies ran while one was open for 3% of the time, Pallas kernels for 16%

profile of v4, /device:TPU:1, one launch (start us, length us, event | category | flops | bytes accessed | tf_op | source)
XLA Modules:
  0.0 86.5 jit_solution(12569719041200975680)
XLA Ops:
  0.7 2.5 %shard_map.146 = (bf16[24,32,128]{2,1,0:T(8,128)(2,1)}, bf16[24,32,128]{2,1,0:T(8,128)(2,1)}) custom-call(bf16[32,4,24,128]{3,2,1,0:T(8,128)(2,1)} %bitcast.29, bf16[8,4,24,128]{3,2,1,0:T(8,128)(2,1)} %bitcast.31, bf16[8,32]{1,0:T(8,128)(2,1)} %head_ref.1), custom_call_target="tpu_custom_call" | custom-call | flops 209715200 | bytes 4194304 | tf_op jit(solution)/shard_map/pallas_call | solution.py:21
  3.2 2.5 %collective-permute-start = (bf16[24,32,128]{2,1,0:T(8,128)(2,1)}, bf16[24,32,128]{2,1,0:T(8,128)(2,1)S(1)}, u32[]{:S(2)}, u32[]{:S(2)}) collective-permute-start(bf16[24,32,128]{2,1,0:T(8,128)(2,1)} %get-tuple-element.55.face1_ref), channel_id=1, source_target_pairs={{0,8},{16,24},{32,40},{48,56},{8,0},{24,16},{40,32},{56,48},{1,9},... | collective-permute-start | bytes 589832 | tf_op jit(solution)/shard_map/ppermute | solution.py:601
  5.7 0.7 collective-permute-start.1
  6.4 0.8 fusion.2
  7.2 1.3 %copy.18 = bf16[64,2,6,2,64]{4,3,0,2,1:T(2,128)(2,1)S(1)} copy(bf16[64,2,6,2,64]{4,1,3,2,0:T(2,128)(2,1)} %bitcast.41) | data formatting | bytes 393216 | tf_op jit(solution)/shard_map/reshape;squeeze | solution.py:634
  8.8 2.3 %shard_map.147 = (bf16[2,24,32,128]{3,2,1,0:T(8,128)(2,1)S(1)}, f32[8,32]{1,0:T(8,128)S(1)}, bf16[4,24,32,128]{3,2,1,0:T(8,128)(2,1)S(1)}, f32[4,24,32,128]{3,2,...) custom-call(bf16[32,4,24,128]{3,2,1,0:T(8,128)(2,1)S(1)} %bitcast.30, ...), custom_call_target="tpu_custom_call" | custom-call | flops 629145600 | bytes 4194304 | tf_op jit(solution)/shard_map/pallas_call | solution.py:21
  11.4 0.7 collective-permute-start.3
  12.0 5.2 %collective-permute-start.2 = (bf16[672,128]{1,0:T(8,128)(2,1)S(1)}, bf16[672,128]{1,0:T(8,128)(2,1)S(1)}, u32[]{:S(2)}, u32[]{:S(2)}) collective-permute-start(bf16[672,128]{1,0:T(8,128)(2,1)S(1)} %get-tuple-element.110), channel_id=1, source_target_pairs={{0,1},{2,3},{4,5},{6,7},{1,0},{3,2},{5,4},{7,6},{8,9},{10,11},{12,... | collective-permute-start | bytes 516104 | tf_op jit(solution)/shard_map/ppermute | solution.py:601
  17.3 4.8 %shard_map.148 = (f32[4,26,32,128]{3,2,1,0:T(8,128)S(1)}, bf16[6,24,96,128]{3,2,1,0:T(8,128)(2,1)S(1)}, bf16[864,1024]{1,0:T(8,128)(2,1)S(1)}, f32[64,1024]{1,0:...) custom-call(bf16[24,32,128]{2,1,0:T(8,128)(2,1)S(1)} %collective-permute-done.g, ...), custom_call_target="tpu_custom_call" | custom-call | flops 3221225472 | bytes 4194304 | tf_op jit(solution)/shard_map/pallas_call | solution.py:21
  22.1 1.9 %shard_map.149 = (f32[4,2,32,128]{3,2,1,0:T(8,128)S(1)}, bf16[6,2,96,128]{3,2,1,0:T(8,128)(2,1)S(1)}, bf16[864,768]{1,0:T(8,128)(2,1)S(1)}, bf16[192,1792]{1,0:T...) custom-call(bf16[672,128]{1,0:T(8,128)(2,1)S(1)} %collective-permute-don, ...), custom_call_target="tpu_custom_call" | custom-call | flops 1073741824 | bytes 4194304 | tf_op jit(solution)/shard_map/pallas_call | solution.py:21
  24.0 7.0 %collective-permute-start.4 = (bf16[592,128]{1,0:T(8,128)(2,1)S(1)}, bf16[592,128]{1,0:T(8,128)(2,1)S(1)}, u32[]{:S(2)}, u32[]{:S(2)}) collective-permute-start(bf16[592,128]{1,0:T(8,128)(2,1)S(1)} %get-tuple-element.80), channel_id=1, source_target_pairs={{0,8},{16,24},{32,40},{48,56},{8,0},{24,16},{40,32},{56,48},{1,9},... | collective-permute-start | bytes 454664 | tf_op jit(solution)/shard_map/ppermute | solution.py:601
  30.9 0.7 collective-permute-start.5
  31.6 4.5 %shard_map.150 = (bf16[736,128]{1,0:T(8,128)(2,1)S(1)}, f32[288,192]{1,0:T(8,128)S(1)}) custom-call(bf16[6,24,96,128]{3,2,1,0:T(8,128)(2,1)S(1)} %get-tuple-element.61.wide_ref, bf16[6,2,96,128]{3,2,1,0:T(8,128)(2,1)S(1)} %get-tuple-element.71.rim_ref, bf16[4,24,32,128]{3,2,1,0:T(8,128)(2,1)S(1)} %get-tuple-element.72.hid_ref, ...), custom_call_target="tpu_custom_call" | custom-call | flops 3221225472 | bytes 4194304 | tf_op jit(solution)/shard_map/pallas_call | solution.py:21
  36.2 3.2 %shard_map.151 = (bf16[1280,128]{1,0:T(8,128)(2,1)}, f32[4,24,8,128]{3,2,1,0:T(8,128)S(1)}, bf16[208,128]{1,0:T(8,128)(2,1)S(1)}, bf16[208,128]{1,0:T(8,128)(2,1...) custom-call(f32[4,26,32,128]{3,2,1,0:T(8,128)S(1)} %get-tuple-element.58.acc_ref, ...), custom_call_target="tpu_custom_call" | custom-call | flops 2147483648 | bytes 4194304 | tf_op jit(solution)/shard_map/pallas_call | solution.py:21
  39.4 14.8 %all-to-all-start = ((bf16[128,5,2,128]{3,2,1,0:T(2,128)(2,1)}), bf16[128,5,2,128]{3,2,1,0:T(2,128)(2,1)S(1)}, u32[]{:S(2)}, u32[]{:S(2)}) async-start(bf16[128,5,2,128]{3,2,1,0:T(2,128)(2,1)} %bitcast.21), calls=%async_computation | async-start | bytes 655360 | tf_op jit(solution)/shard_map/all_to_all | solution.py:735
  54.3 1.6 %collective-permute-start.6 = (bf16[208,128]{1,0:T(8,128)(2,1)S(1)}, bf16[208,128]{1,0:T(8,128)(2,1)S(1)}, u32[]{:S(2)}, u32[]{:S(2)}) collective-permute-start(bf16[208,128]{1,0:T(8,128)(2,1)S(1)} %get-tuple-element.89), channel_id=1, source_target_pairs={{0,8},{16,24},{32,40},{48,56},{8,0},{24,16},{40,32},{56,48},{1,9},... | collective-permute-start | bytes 159752 | tf_op jit(solution)/shard_map/ppermute | solution.py:601
  55.9 0.7 collective-permute-start.7
  56.5 9.7 %all-to-all-done.pieces_far = bf16[128,5,2,128]{3,2,1,0:T(2,128)(2,1)S(1)} async-done(((bf16[128,5,2,128]{3,2,1,0:T(2,128)(2,1)}), bf16[128,5,2,128]{3,2,1,0:T(2,128)(2,1)S(1)}, u32[]{:S(2)}, u32[]{:S(2)}) %all-to-all-start) | async-done | bytes 327712 | tf_op jit(solution)/shard_map/all_to_all | solution.py:735
  66.2 1.4 %shard_map.152 = bf16[128,5,2,128]{3,2,1,0:T(2,128)(2,1)} custom-call(bf16[128,5,2,128]{3,2,1,0:T(2,128)(2,1)S(1)} %all-to-all-done.pieces_far), custom_call_target="tpu_custom_call" | custom-call | flops 1048576 | bytes 4194304 | tf_op jit(solution)/shard_map/pallas_call | solution.py:21
  67.7 4.8 %all-to-all-start.1 = ((bf16[128,5,2,128]{3,2,1,0:T(2,128)(2,1)}), bf16[128,5,2,128]{3,2,1,0:T(2,128)(2,1)S(1)}, u32[]{:S(2)}, u32[]{:S(2)}) async-start(bf16[128,5,2,128]{3,2,1,0:T(2,128)(2,1)} %shard_map.152), calls=%async_computation.1 | async-start | bytes 655360 | tf_op jit(solution)/shard_map/all_to_all | solution.py:749
  72.5 3.4 %collective-permute-start.8 = (bf16[32,128]{1,0:T(8,128)(2,1)S(1)}, bf16[32,128]{1,0:T(8,128)(2,1)S(1)}, u32[]{:S(2)}, u32[]{:S(2)}) collective-permute-start(bf16[32,128]{1,0:T(8,128)(2,1)S(1)} %get-tuple-element.97), channel_id=1, source_target_pairs={{0,1},{2,3},{4,5},{6,7},{1,0},{3,2},{5,4},{7,6},{8,9},{10,11},{12,... | collective-permute-start | bytes 24584 | tf_op jit(solution)/shard_map/ppermute | solution.py:601
  76.5 7.9 %all-to-all-done.1 = bf16[128,5,2,128]{3,2,1,0:T(2,128)(2,1)S(1)} async-done(((bf16[128,5,2,128]{3,2,1,0:T(2,128)(2,1)}), bf16[128,5,2,128]{3,2,1,0:T(2,128)(2,1)S(1)}, u32[]{:S(2)}, u32[]{:S(2)}) %all-to-all-start.1) | async-done | bytes 327712 | tf_op jit(solution)/shard_map/all_to_all | solution.py:749
  84.4 1.2 %shard_map.153 = (f32[3,3,3,8,32]{4,3,2,1,0:T(8,128)}, f32[3,3,3,32,64]{4,3,2,1,0:T(8,128)}, f32[3,3,3,32,96]{4,3,2,1,0:T(8,128)}, f32[8,32]{1,0:T(8,128)}) custom-call(bf16[1280,128]{1,0:T(8,128)(2,1)S(1)} %bitcast.34), custom_call_target="tpu_custom_call" | custom-call | flops 1048576 | bytes 4194304 | tf_op jit(solution)/shard_map/pallas_call | solution.py:21
  85.7 0.8 shard_map.155
  (55 shorter events, 1.1 us)
Async XLA Ops:
  0.6 8.1 %copy-start.2 = (bf16[256,384]{1,0:T(8,128)(2,1)S(1)}, bf16[256,384]{1,0:T(8,128)(2,1)}, u32[]{:S(2)}) copy-start(bf16[256,384]{1,0:T(8,128)(2,1)} %constant.10.clone.pool_ref) | copy-start | bytes 589828
  0.6 8.1 %copy-start.7 = (bf16[8,32]{1,0:T(8,128)(2,1)S(1)}, bf16[8,32]{1,0:T(8,128)(2,1)}, u32[]{:S(2)}) copy-start(bf16[8,32]{1,0:T(8,128)(2,1)} %head_ref.1) | copy-start | bytes 1540
  0.7 8.1 %copy-start.1 = (bf16[1,8,4,24,128]{4,3,2,1,0:T(8,128)(2,1)S(1)}, bf16[1,8,4,24,128]{4,3,2,1,0:T(8,128)(2,1)}, u32[]{:S(2)}) copy-start(bf16[1,8,4,24,128]{4,3,2,1,0:T(8,128)(2,1)} %param.15) | copy-start | bytes 589828
  0.7 8.1 %copy-start = (bf16[1,32,4,24,128]{4,3,2,1,0:T(8,128)(2,1)S(1)}, bf16[1,32,4,24,128]{4,3,2,1,0:T(8,128)(2,1)}, u32[]{:S(2)}) copy-start(bf16[1,32,4,24,128]{4,3,2,1,0:T(8,128)(2,1)} %param.14) | copy-start | bytes 2359300
  0.7 8.1 %copy-start.3 = (bf16[1,32,4,24,128]{4,3,2,1,0:T(8,128)(2,1)S(1)}, bf16[1,32,4,24,128]{4,3,2,1,0:T(8,128)(2,1)}, u32[]{:S(2)}) copy-start(bf16[1,32,4,24,128]{4,3,2,1,0:T(8,128)(2,1)} %param.12) | copy-start | bytes 2359300
  0.7 8.1 %copy-start.4 = (bf16[1,8,4,24,128]{4,3,2,1,0:T(8,128)(2,1)S(1)}, bf16[1,8,4,24,128]{4,3,2,1,0:T(8,128)(2,1)}, u32[]{:S(2)}) copy-start(bf16[1,8,4,24,128]{4,3,2,1,0:T(8,128)(2,1)} %param.11) | copy-start | bytes 589828
  3.2 7.9 %collective-permute-start = (bf16[24,32,128]{2,1,0:T(8,128)(2,1)}, bf16[24,32,128]{2,1,0:T(8,128)(2,1)S(1)}, u32[]{:S(2)}, u32[]{:S(2)}) collective-permute-start(bf16[24,32,128]{2,1,0:T(8,128)(2,1)} %get-tuple-element.55.face1_ref), channel_id=1, source_target_pairs={{0,8},{16,24},{32,40},{48,56},{8,0},{24,16},{40,32},{56,48},{1,9},... | collective-permute-start | bytes 589832 | tf_op jit(solution)/shard_map/ppermute | solution.py:601
  5.7 5.5 %collective-permute-start.1 = (bf16[24,32,128]{2,1,0:T(8,128)(2,1)}, bf16[24,32,128]{2,1,0:T(8,128)(2,1)S(1)}, u32[]{:S(2)}, u32[]{:S(2)}) collective-permute-start(bf16[24,32,128]{2,1,0:T(8,128)(2,1)} %get-tuple-element.57.face2_ref), channel_id=1, source_target_pairs={{8,16},{24,32},{40,48},{16,8},{32,24},{48,40},{9,17},{25,33},{41,4... | collective-permute-start | bytes 589832 | tf_op jit(solution)/shard_map/ppermute | solution.py:601
  8.7 8.5 %copy-start.5 = (bf16[24,32,128]{2,1,0:T(8,128)(2,1)S(1)}, bf16[24,32,128]{2,1,0:T(8,128)(2,1)}, u32[]{:S(2)}) copy-start(bf16[24,32,128]{2,1,0:T(8,128)(2,1)} %get-tuple-element.55.face1_ref) | copy-start | bytes 589828
  8.8 8.5 %copy-start.6 = (bf16[24,32,128]{2,1,0:T(8,128)(2,1)S(1)}, bf16[24,32,128]{2,1,0:T(8,128)(2,1)}, u32[]{:S(2)}) copy-start(bf16[24,32,128]{2,1,0:T(8,128)(2,1)} %get-tuple-element.57.face2_ref) | copy-start | bytes 589828
  8.8 8.5 %copy-start.8 = (bf16[32,96,3,3,3]{1,0,4,3,2:T(8,128)(2,1)S(1)}, bf16[32,96,3,3,3]{1,0,4,3,2:T(8,128)(2,1)}, u32[]{:S(2)}) copy-start(bf16[32,96,3,3,3]{1,0,4,3,2:T(8,128)(2,1)} %param.18) | copy-start | bytes 497668
  8.8 8.5 %copy-start.9 = (bf16[64,32,3,3,3]{0,1,4,3,2:T(8,128)(2,1)S(1)}, bf16[64,32,3,3,3]{0,1,4,3,2:T(8,128)(2,1)}, u32[]{:S(2)}) copy-start(bf16[64,32,3,3,3]{0,1,4,3,2:T(8,128)(2,1)} %param.17) | copy-start | bytes 331780
  11.4 10.7 %collective-permute-start.3 = (bf16[672,128]{1,0:T(8,128)(2,1)S(1)}, bf16[672,128]{1,0:T(8,128)(2,1)S(1)}, u32[]{:S(2)}, u32[]{:S(2)}) collective-permute-start(bf16[672,128]{1,0:T(8,128)(2,1)S(1)} %get-tuple-element.109), channel_id=1, source_target_pairs={{1,2},{3,4},{5,6},{2,1},{4,3},{6,5},{9,10},{11,12},{13,14},{10,9},... | collective-permute-start | bytes 516104 | tf_op jit(solution)/shard_map/ppermute | solution.py:601
  12.0 10.0 %collective-permute-start.2 = (bf16[672,128]{1,0:T(8,128)(2,1)S(1)}, bf16[672,128]{1,0:T(8,128)(2,1)S(1)}, u32[]{:S(2)}, u32[]{:S(2)}) collective-permute-start(bf16[672,128]{1,0:T(8,128)(2,1)S(1)} %get-tuple-element.110), channel_id=1, source_target_pairs={{0,1},{2,3},{4,5},{6,7},{1,0},{3,2},{5,4},{7,6},{8,9},{10,11},{12,... | collective-permute-start | bytes 516104 | tf_op jit(solution)/shard_map/ppermute | solution.py:601
  24.0 12.2 %collective-permute-start.4 = (bf16[592,128]{1,0:T(8,128)(2,1)S(1)}, bf16[592,128]{1,0:T(8,128)(2,1)S(1)}, u32[]{:S(2)}, u32[]{:S(2)}) collective-permute-start(bf16[592,128]{1,0:T(8,128)(2,1)S(1)} %get-tuple-element.80), channel_id=1, source_target_pairs={{0,8},{16,24},{32,40},{48,56},{8,0},{24,16},{40,32},{56,48},{1,9},... | collective-permute-start | bytes 454664 | tf_op jit(solution)/shard_map/ppermute | solution.py:601
  30.9 5.2 %collective-permute-start.5 = (bf16[592,128]{1,0:T(8,128)(2,1)S(1)}, bf16[592,128]{1,0:T(8,128)(2,1)S(1)}, u32[]{:S(2)}, u32[]{:S(2)}) collective-permute-start(bf16[592,128]{1,0:T(8,128)(2,1)S(1)} %get-tuple-element.81), channel_id=1, source_target_pairs={{8,16},{24,32},{40,48},{16,8},{32,24},{48,40},{9,17},{25,33},{41,4... | collective-permute-start | bytes 454664 | tf_op jit(solution)/shard_map/ppermute | solution.py:601
  31.6 4.6 %copy-start.10 = (bf16[32,8,3,3,3]{0,1,4,3,2:T(8,128)(2,1)S(1)}, bf16[32,8,3,3,3]{0,1,4,3,2:T(8,128)(2,1)}, u32[]{:S(2)}) copy-start(bf16[32,8,3,3,3]{0,1,4,3,2:T(8,128)(2,1)} %param.16) | copy-start | bytes 41476
  31.6 4.6 %copy-start.11 = (bf16[256,256]{1,0:T(8,128)(2,1)S(1)}, bf16[256,256]{1,0:T(8,128)(2,1)}, u32[]{:S(2)}) copy-start(bf16[256,256]{1,0:T(8,128)(2,1)} %constant.11.clone.up_ref) | copy-start | bytes 393220
  39.4 26.8 %all-to-all-start = ((bf16[128,5,2,128]{3,2,1,0:T(2,128)(2,1)}), bf16[128,5,2,128]{3,2,1,0:T(2,128)(2,1)S(1)}, u32[]{:S(2)}, u32[]{:S(2)}) async-start(bf16[128,5,2,128]{3,2,1,0:T(2,128)(2,1)} %bitcast.21), calls=%async_computation | async-start | bytes 655360 | tf_op jit(solution)/shard_map/all_to_all | solution.py:735
  54.3 13.4 %collective-permute-start.6 = (bf16[208,128]{1,0:T(8,128)(2,1)S(1)}, bf16[208,128]{1,0:T(8,128)(2,1)S(1)}, u32[]{:S(2)}, u32[]{:S(2)}) collective-permute-start(bf16[208,128]{1,0:T(8,128)(2,1)S(1)} %get-tuple-element.89), channel_id=1, source_target_pairs={{0,8},{16,24},{32,40},{48,56},{8,0},{24,16},{40,32},{56,48},{1,9},... | collective-permute-start | bytes 159752 | tf_op jit(solution)/shard_map/ppermute | solution.py:601
  55.9 11.8 %collective-permute-start.7 = (bf16[208,128]{1,0:T(8,128)(2,1)S(1)}, bf16[208,128]{1,0:T(8,128)(2,1)S(1)}, u32[]{:S(2)}, u32[]{:S(2)}) collective-permute-start(bf16[208,128]{1,0:T(8,128)(2,1)S(1)} %get-tuple-element.90), channel_id=1, source_target_pairs={{8,16},{24,32},{40,48},{16,8},{32,24},{48,40},{9,17},{25,33},{41,4... | collective-permute-start | bytes 159752 | tf_op jit(solution)/shard_map/ppermute | solution.py:601
  67.7 16.8 %all-to-all-start.1 = ((bf16[128,5,2,128]{3,2,1,0:T(2,128)(2,1)}), bf16[128,5,2,128]{3,2,1,0:T(2,128)(2,1)S(1)}, u32[]{:S(2)}, u32[]{:S(2)}) async-start(bf16[128,5,2,128]{3,2,1,0:T(2,128)(2,1)} %shard_map.152), calls=%async_computation.1 | async-start | bytes 655360 | tf_op jit(solution)/shard_map/all_to_all | solution.py:749
  72.5 13.2 %collective-permute-start.8 = (bf16[32,128]{1,0:T(8,128)(2,1)S(1)}, bf16[32,128]{1,0:T(8,128)(2,1)S(1)}, u32[]{:S(2)}, u32[]{:S(2)}) collective-permute-start(bf16[32,128]{1,0:T(8,128)(2,1)S(1)} %get-tuple-element.97), channel_id=1, source_target_pairs={{0,1},{2,3},{4,5},{6,7},{1,0},{3,2},{5,4},{7,6},{8,9},{10,11},{12,... | collective-permute-start | bytes 24584 | tf_op jit(solution)/shard_map/ppermute | solution.py:601
  75.9 9.8 %collective-permute-start.9 = (bf16[32,128]{1,0:T(8,128)(2,1)S(1)}, bf16[32,128]{1,0:T(8,128)(2,1)S(1)}, u32[]{:S(2)}, u32[]{:S(2)}) collective-permute-start(bf16[32,128]{1,0:T(8,128)(2,1)S(1)} %get-tuple-element.98), channel_id=1, source_target_pairs={{1,2},{3,4},{5,6},{2,1},{4,3},{6,5},{9,10},{11,12},{13,14},{10,9},... | collective-permute-start | bytes 24584 | tf_op jit(solution)/shard_map/ppermute | solution.py:601

commit v5 on v4

--- a/solution.py
+++ b/solution.py
@@ -492,7 +492,7 @@
                 total_ref[x, y + r] += sum(parts[1:], parts[0])
         return carry
 
-    lax.fori_loop(0, 6, step, 0, unroll=3)
+    lax.fori_loop(0, 6, step, 0, unroll=6)
     genc = jnp.concatenate([sum_ref[...], jnp.zeros((72, 32), F32)], axis=1)
     rows_ref[432:544, :] = jnp.concatenate([genc, jnp.zeros((40, 128), F32)], axis=0).astype(BF16)
     writes += fetch([(rows_ref.at[432:544], rows_far.at[1168:1280])], sems.at[2])
@@ -529,22 +529,15 @@
         grad_ref[:, x] = (cot_ref[:, x].astype(F32) + jnp.swapaxes(total, 0, 1)).astype(BF16)
 
 
-def share_body(pieces_far, out_far, pieces_ref, copies_ref, sems, out_sems):
-    count = pieces_ref.shape[0]
-    part = count // 4
-    spans = [pl.ds(i * part, part) for i in range(4)]
-    waits = fetch([(pieces_far.at[span], pieces_ref.at[span]) for span in spans], sems)
-    total = jnp.zeros(pieces_ref.shape[1:], F32)
-    for i, wait in enumerate(waits):
-        wait()
-        for j in range(part):
-            total = total + pieces_ref[i * part + j].astype(F32)
-    total = total.astype(BF16)
-    part = copies_ref.shape[0]
-    for j in range(part):
-        copies_ref[j] = total
-    for wait in fetch([(copies_ref, out_far.at[pl.ds(i * part, part)]) for i in range(count // part)], out_sems):
-        wait()
+def share_body(share, pieces_ref, out_ref):
+    size = -(-share // 16) * 16
+    rows = pieces_ref.shape[0]
+    place = lax.broadcasted_iota(jnp.int32, (size, rows), 1)
+    piece = ((place.astype(F32) + 0.5) * (1.0 / share)).astype(jnp.int32)
+    same = place - piece * share == lax.broadcasted_iota(jnp.int32, (size, rows), 0)
+    pick = jnp.where(same, 1.0, 0.0).astype(BF16)
+    total = dot(pick, pieces_ref[...]).astype(BF16)
+    out_ref[...] = dot_tn(pick, total).astype(BF16)
 
 
 def unpack_body(scale, rows_ref, enc_ref, mid_ref, dec_ref, head_ref):
@@ -731,22 +724,14 @@
 
     axes = ("dp", "gx", "gy")
     count = lax.axis_size(axes)
-    share = 1280 // count // 2
-    pieces = lax.all_to_all(rows.reshape(count, share, 2, 128), axes, 0, 0)
+    share = 1280 // count
+    shape = (count, share // 2, 2, 128)
+    pieces = lax.all_to_all(rows.reshape(shape), axes, 0, 0).reshape(1280, 128)
     (shares,) = call(
-        share_body,
-        [sds(pieces.shape, BF16)],
-        [
-            pltpu.VMEM(pieces.shape, BF16),
-            pltpu.VMEM((count // 8,) + pieces.shape[1:], BF16),
-            pltpu.SemaphoreType.DMA((4,)),
-            pltpu.SemaphoreType.DMA((8,)),
-        ],
-        (pieces,),
-        1 << 20, 8, far=1, far_outs=1,
+        functools.partial(share_body, share), [sds((1280, 128), BF16)], [], (pieces,), 1 << 20, 8
     )
     shares, last1, last2 = lax.optimization_barrier((shares, last1, last2))
-    rows = lax.all_to_all(shares, axes, 0, 0).reshape(1280, 128)
+    rows = lax.all_to_all(shares.reshape(shape), axes, 0, 0).reshape(1280, 128)
     col1, col2 = call(
         corner_body, [sds((32, 128), BF16)] * 2, [], (edge_lo, edge_hi, last1, last2), 1 << 16, 4
     )

time: 86.9 us -> 86.4 us (level)
  no operation moved by 1% of the time
where the time goes in v5:
time: 86.4 us; the launch traced here: 85.9 us
  starting transfers between devices  42.9 us (50%)
  Pallas kernels  21.8 us (25%)
  waiting for transfers between devices  17.7 us (20%)
  local copies, waits for them, and re-layouts  2.49 us (3%)
  between operations  1.06 us (1%)
    ppermute x10, starting transfers between devices, swaps(): lax.ppermute(v, axis, ahead + [(b, a) for a, b in ahead])  23.1 us
    pallas_call x10, Pallas kernels, call(): pl.pallas_call(body, out_shape=outs, in_specs=[HBM] * far + [VMEM] * (len...  21.8 us
    all_to_all x1, starting transfers between devices, on_device(): pieces = lax.all_to_all(rows.reshape(shape), axes, 0, 0).reshape(1280, 128)  14.6 us
    all_to_all x1, waiting for transfers between devices, on_device(): pieces = lax.all_to_all(rows.reshape(shape), axes, 0, 0).reshape(1280, 128)  9.71 us
    all_to_all x1, waiting for transfers between devices, on_device(): rows = lax.all_to_all(shares.reshape(shape), axes, 0, 0).reshape(1280, 128)  7.92 us
    all_to_all x1, starting transfers between devices, on_device(): rows = lax.all_to_all(shares.reshape(shape), axes, 0, 0).reshape(1280, 128)  5.11 us
  transfers between devices with their start and end apart: 12, of which 2 were waited for; matrix products, arithmetic and copies ran while one was open for 3% of the time, Pallas kernels for 16%

profile of v5, /device:TPU:1, one launch (start us, length us, event | category | flops | bytes accessed | tf_op | source)
XLA Modules:
  0.0 85.9 jit_solution(5669826291161301613)
XLA Ops:
  0.7 2.5 %shard_map.146 = (bf16[24,32,128]{2,1,0:T(8,128)(2,1)}, bf16[24,32,128]{2,1,0:T(8,128)(2,1)}) custom-call(bf16[32,4,24,128]{3,2,1,0:T(8,128)(2,1)} %bitcast.31, bf16[8,4,24,128]{3,2,1,0:T(8,128)(2,1)} %bitcast.33, bf16[8,32]{1,0:T(8,128)(2,1)} %head_ref.1), custom_call_target="tpu_custom_call" | custom-call | flops 209715200 | bytes 4194304 | tf_op jit(solution)/shard_map/pallas_call | solution.py:21
  3.2 2.5 %collective-permute-start = (bf16[24,32,128]{2,1,0:T(8,128)(2,1)}, bf16[24,32,128]{2,1,0:T(8,128)(2,1)S(1)}, u32[]{:S(2)}, u32[]{:S(2)}) collective-permute-start(bf16[24,32,128]{2,1,0:T(8,128)(2,1)} %get-tuple-element.55.face1_ref), channel_id=1, source_target_pairs={{0,8},{16,24},{32,40},{48,56},{8,0},{24,16},{40,32},{56,48},{1,9},... | collective-permute-start | bytes 589832 | tf_op jit(solution)/shard_map/ppermute | solution.py:594
  5.7 0.7 collective-permute-start.1
  6.4 0.8 fusion.2
  7.2 1.3 %copy.18 = bf16[64,2,6,2,64]{4,3,0,2,1:T(2,128)(2,1)S(1)} copy(bf16[64,2,6,2,64]{4,1,3,2,0:T(2,128)(2,1)} %bitcast.44) | data formatting | bytes 393216 | tf_op jit(solution)/shard_map/reshape;squeeze | solution.py:627
  8.8 2.3 %shard_map.147 = (bf16[2,24,32,128]{3,2,1,0:T(8,128)(2,1)S(1)}, f32[8,32]{1,0:T(8,128)S(1)}, bf16[4,24,32,128]{3,2,1,0:T(8,128)(2,1)S(1)}, f32[4,24,32,128]{3,2,...) custom-call(bf16[32,4,24,128]{3,2,1,0:T(8,128)(2,1)S(1)} %bitcast.32, ...), custom_call_target="tpu_custom_call" | custom-call | flops 629145600 | bytes 4194304 | tf_op jit(solution)/shard_map/pallas_call | solution.py:21
  11.4 0.7 collective-permute-start.3
  12.0 5.2 %collective-permute-start.2 = (bf16[672,128]{1,0:T(8,128)(2,1)S(1)}, bf16[672,128]{1,0:T(8,128)(2,1)S(1)}, u32[]{:S(2)}, u32[]{:S(2)}) collective-permute-start(bf16[672,128]{1,0:T(8,128)(2,1)S(1)} %get-tuple-element.110), channel_id=1, source_target_pairs={{0,1},{2,3},{4,5},{6,7},{1,0},{3,2},{5,4},{7,6},{8,9},{10,11},{12,... | collective-permute-start | bytes 516104 | tf_op jit(solution)/shard_map/ppermute | solution.py:594
  17.3 4.8 %shard_map.148 = (f32[4,26,32,128]{3,2,1,0:T(8,128)S(1)}, bf16[6,24,96,128]{3,2,1,0:T(8,128)(2,1)S(1)}, bf16[864,1024]{1,0:T(8,128)(2,1)S(1)}, f32[64,1024]{1,0:...) custom-call(bf16[24,32,128]{2,1,0:T(8,128)(2,1)S(1)} %collective-permute-done.g, ...), custom_call_target="tpu_custom_call" | custom-call | flops 3221225472 | bytes 4194304 | tf_op jit(solution)/shard_map/pallas_call | solution.py:21
  22.1 1.9 %shard_map.149 = (f32[4,2,32,128]{3,2,1,0:T(8,128)S(1)}, bf16[6,2,96,128]{3,2,1,0:T(8,128)(2,1)S(1)}, bf16[864,768]{1,0:T(8,128)(2,1)S(1)}, bf16[192,1792]{1,0:T...) custom-call(bf16[672,128]{1,0:T(8,128)(2,1)S(1)} %collective-permute-don, ...), custom_call_target="tpu_custom_call" | custom-call | flops 1073741824 | bytes 4194304 | tf_op jit(solution)/shard_map/pallas_call | solution.py:21
  24.0 7.0 %collective-permute-start.4 = (bf16[592,128]{1,0:T(8,128)(2,1)S(1)}, bf16[592,128]{1,0:T(8,128)(2,1)S(1)}, u32[]{:S(2)}, u32[]{:S(2)}) collective-permute-start(bf16[592,128]{1,0:T(8,128)(2,1)S(1)} %get-tuple-element.80), channel_id=1, source_target_pairs={{0,8},{16,24},{32,40},{48,56},{8,0},{24,16},{40,32},{56,48},{1,9},... | collective-permute-start | bytes 454664 | tf_op jit(solution)/shard_map/ppermute | solution.py:594
  30.9 0.8 collective-permute-start.5
  31.8 4.5 %shard_map.150 = (bf16[736,128]{1,0:T(8,128)(2,1)S(1)}, f32[288,192]{1,0:T(8,128)S(1)}) custom-call(bf16[6,24,96,128]{3,2,1,0:T(8,128)(2,1)S(1)} %get-tuple-element.61.wide_ref, bf16[6,2,96,128]{3,2,1,0:T(8,128)(2,1)S(1)} %get-tuple-element.71.rim_ref, bf16[4,24,32,128]{3,2,1,0:T(8,128)(2,1)S(1)} %get-tuple-element.72.hid_ref, ...), custom_call_target="tpu_custom_call" | custom-call | flops 3221225472 | bytes 4194304 | tf_op jit(solution)/shard_map/pallas_call | solution.py:21
  36.4 2.7 %shard_map.151 = (bf16[1280,128]{1,0:T(8,128)(2,1)}, f32[4,24,8,128]{3,2,1,0:T(8,128)S(1)}, bf16[208,128]{1,0:T(8,128)(2,1)S(1)}, bf16[208,128]{1,0:T(8,128)(2,1...) custom-call(f32[4,26,32,128]{3,2,1,0:T(8,128)S(1)} %get-tuple-element.58.acc_ref, ...), custom_call_target="tpu_custom_call" | custom-call | flops 2147483648 | bytes 4194304 | tf_op jit(solution)/shard_map/pallas_call | solution.py:21
  39.1 14.6 %all-to-all-start = ((bf16[128,5,2,128]{3,2,1,0:T(2,128)(2,1)}), bf16[128,5,2,128]{3,2,1,0:T(2,128)(2,1)S(1)}, u32[]{:S(2)}, u32[]{:S(2)}) async-start(bf16[128,5,2,128]{3,2,1,0:T(2,128)(2,1)} %bitcast.21), calls=%async_computation | async-start | bytes 655360 | tf_op jit(solution)/shard_map/all_to_all | solution.py:729
  53.7 1.6 %collective-permute-start.6 = (bf16[208,128]{1,0:T(8,128)(2,1)S(1)}, bf16[208,128]{1,0:T(8,128)(2,1)S(1)}, u32[]{:S(2)}, u32[]{:S(2)}) collective-permute-start(bf16[208,128]{1,0:T(8,128)(2,1)S(1)} %get-tuple-element.89), channel_id=1, source_target_pairs={{0,8},{16,24},{32,40},{48,56},{8,0},{24,16},{40,32},{56,48},{1,9},... | collective-permute-start | bytes 159752 | tf_op jit(solution)/shard_map/ppermute | solution.py:594
  55.3 0.7 collective-permute-start.7
  56.0 9.7 %all-to-all-done = bf16[128,5,2,128]{3,2,1,0:T(2,128)(2,1)S(1)} async-done(((bf16[128,5,2,128]{3,2,1,0:T(2,128)(2,1)}), bf16[128,5,2,128]{3,2,1,0:T(2,128)(2,1)S(1)}, u32[]{:S(2)}, u32[]{:S(2)}) %all-to-all-start) | async-done | bytes 327712 | tf_op jit(solution)/shard_map/all_to_all | solution.py:729
  65.7 1.1 %shard_map.152 = bf16[1280,128]{1,0:T(8,128)(2,1)} custom-call(bf16[1280,128]{1,0:T(8,128)(2,1)S(1)} %bitcast.37), custom_call_target="tpu_custom_call" | custom-call | flops 1048576 | bytes 4194304 | tf_op jit(solution)/shard_map/pallas_call | solution.py:21
  66.8 5.1 %all-to-all-start.1 = ((bf16[128,5,2,128]{3,2,1,0:T(2,128)(2,1)}), bf16[128,5,2,128]{3,2,1,0:T(2,128)(2,1)S(1)}, u32[]{:S(2)}, u32[]{:S(2)}) async-start(bf16[128,5,2,128]{3,2,1,0:T(2,128)(2,1)} %bitcast.23), calls=%async_computation.1 | async-start | bytes 655360 | tf_op jit(solution)/shard_map/all_to_all | solution.py:734
  72.0 3.4 %collective-permute-start.8 = (bf16[32,128]{1,0:T(8,128)(2,1)S(1)}, bf16[32,128]{1,0:T(8,128)(2,1)S(1)}, u32[]{:S(2)}, u32[]{:S(2)}) collective-permute-start(bf16[32,128]{1,0:T(8,128)(2,1)S(1)} %get-tuple-element.97), channel_id=1, source_target_pairs={{0,1},{2,3},{4,5},{6,7},{1,0},{3,2},{5,4},{7,6},{8,9},{10,11},{12,... | collective-permute-start | bytes 24584 | tf_op jit(solution)/shard_map/ppermute | solution.py:594
  76.0 7.9 %all-to-all-done.1 = bf16[128,5,2,128]{3,2,1,0:T(2,128)(2,1)S(1)} async-done(((bf16[128,5,2,128]{3,2,1,0:T(2,128)(2,1)}), bf16[128,5,2,128]{3,2,1,0:T(2,128)(2,1)S(1)}, u32[]{:S(2)}, u32[]{:S(2)}) %all-to-all-start.1) | async-done | bytes 327712 | tf_op jit(solution)/shard_map/all_to_all | solution.py:734
  83.9 1.2 %shard_map.153 = (f32[3,3,3,8,32]{4,3,2,1,0:T(8,128)}, f32[3,3,3,32,64]{4,3,2,1,0:T(8,128)}, f32[3,3,3,32,96]{4,3,2,1,0:T(8,128)}, f32[8,32]{1,0:T(8,128)}) custom-call(bf16[1280,128]{1,0:T(8,128)(2,1)S(1)} %bitcast.36), custom_call_target="tpu_custom_call" | custom-call | flops 1048576 | bytes 4194304 | tf_op jit(solution)/shard_map/pallas_call | solution.py:21
  85.1 0.8 shard_map.155
  (55 shorter events, 1.1 us)
Async XLA Ops:
  0.6 8.1 %copy-start.2 = (bf16[256,384]{1,0:T(8,128)(2,1)S(1)}, bf16[256,384]{1,0:T(8,128)(2,1)}, u32[]{:S(2)}) copy-start(bf16[256,384]{1,0:T(8,128)(2,1)} %constant.10.clone.pool_ref) | copy-start | bytes 589828
  0.6 8.1 %copy-start.7 = (bf16[8,32]{1,0:T(8,128)(2,1)S(1)}, bf16[8,32]{1,0:T(8,128)(2,1)}, u32[]{:S(2)}) copy-start(bf16[8,32]{1,0:T(8,128)(2,1)} %head_ref.1) | copy-start | bytes 1540
  0.7 8.1 %copy-start.1 = (bf16[1,8,4,24,128]{4,3,2,1,0:T(8,128)(2,1)S(1)}, bf16[1,8,4,24,128]{4,3,2,1,0:T(8,128)(2,1)}, u32[]{:S(2)}) copy-start(bf16[1,8,4,24,128]{4,3,2,1,0:T(8,128)(2,1)} %param.15) | copy-start | bytes 589828
  0.7 8.1 %copy-start = (bf16[1,32,4,24,128]{4,3,2,1,0:T(8,128)(2,1)S(1)}, bf16[1,32,4,24,128]{4,3,2,1,0:T(8,128)(2,1)}, u32[]{:S(2)}) copy-start(bf16[1,32,4,24,128]{4,3,2,1,0:T(8,128)(2,1)} %param.14) | copy-start | bytes 2359300
  0.7 8.1 %copy-start.3 = (bf16[1,32,4,24,128]{4,3,2,1,0:T(8,128)(2,1)S(1)}, bf16[1,32,4,24,128]{4,3,2,1,0:T(8,128)(2,1)}, u32[]{:S(2)}) copy-start(bf16[1,32,4,24,128]{4,3,2,1,0:T(8,128)(2,1)} %param.12) | copy-start | bytes 2359300
  0.7 8.1 %copy-start.4 = (bf16[1,8,4,24,128]{4,3,2,1,0:T(8,128)(2,1)S(1)}, bf16[1,8,4,24,128]{4,3,2,1,0:T(8,128)(2,1)}, u32[]{:S(2)}) copy-start(bf16[1,8,4,24,128]{4,3,2,1,0:T(8,128)(2,1)} %param.11) | copy-start | bytes 589828
  3.2 7.9 %collective-permute-start = (bf16[24,32,128]{2,1,0:T(8,128)(2,1)}, bf16[24,32,128]{2,1,0:T(8,128)(2,1)S(1)}, u32[]{:S(2)}, u32[]{:S(2)}) collective-permute-start(bf16[24,32,128]{2,1,0:T(8,128)(2,1)} %get-tuple-element.55.face1_ref), channel_id=1, source_target_pairs={{0,8},{16,24},{32,40},{48,56},{8,0},{24,16},{40,32},{56,48},{1,9},... | collective-permute-start | bytes 589832 | tf_op jit(solution)/shard_map/ppermute | solution.py:594
  5.7 5.5 %collective-permute-start.1 = (bf16[24,32,128]{2,1,0:T(8,128)(2,1)}, bf16[24,32,128]{2,1,0:T(8,128)(2,1)S(1)}, u32[]{:S(2)}, u32[]{:S(2)}) collective-permute-start(bf16[24,32,128]{2,1,0:T(8,128)(2,1)} %get-tuple-element.57.face2_ref), channel_id=1, source_target_pairs={{8,16},{24,32},{40,48},{16,8},{32,24},{48,40},{9,17},{25,33},{41,4... | collective-permute-start | bytes 589832 | tf_op jit(solution)/shard_map/ppermute | solution.py:594
  8.7 8.5 %copy-start.5 = (bf16[24,32,128]{2,1,0:T(8,128)(2,1)S(1)}, bf16[24,32,128]{2,1,0:T(8,128)(2,1)}, u32[]{:S(2)}) copy-start(bf16[24,32,128]{2,1,0:T(8,128)(2,1)} %get-tuple-element.55.face1_ref) | copy-start | bytes 589828
  8.8 8.5 %copy-start.6 = (bf16[24,32,128]{2,1,0:T(8,128)(2,1)S(1)}, bf16[24,32,128]{2,1,0:T(8,128)(2,1)}, u32[]{:S(2)}) copy-start(bf16[24,32,128]{2,1,0:T(8,128)(2,1)} %get-tuple-element.57.face2_ref) | copy-start | bytes 589828
  8.8 8.5 %copy-start.8 = (bf16[32,96,3,3,3]{1,0,4,3,2:T(8,128)(2,1)S(1)}, bf16[32,96,3,3,3]{1,0,4,3,2:T(8,128)(2,1)}, u32[]{:S(2)}) copy-start(bf16[32,96,3,3,3]{1,0,4,3,2:T(8,128)(2,1)} %param.18) | copy-start | bytes 497668
  8.8 8.5 %copy-start.9 = (bf16[64,32,3,3,3]{0,1,4,3,2:T(8,128)(2,1)S(1)}, bf16[64,32,3,3,3]{0,1,4,3,2:T(8,128)(2,1)}, u32[]{:S(2)}) copy-start(bf16[64,32,3,3,3]{0,1,4,3,2:T(8,128)(2,1)} %param.17) | copy-start | bytes 331780
  11.4 10.7 %collective-permute-start.3 = (bf16[672,128]{1,0:T(8,128)(2,1)S(1)}, bf16[672,128]{1,0:T(8,128)(2,1)S(1)}, u32[]{:S(2)}, u32[]{:S(2)}) collective-permute-start(bf16[672,128]{1,0:T(8,128)(2,1)S(1)} %get-tuple-element.109), channel_id=1, source_target_pairs={{1,2},{3,4},{5,6},{2,1},{4,3},{6,5},{9,10},{11,12},{13,14},{10,9},... | collective-permute-start | bytes 516104 | tf_op jit(solution)/shard_map/ppermute | solution.py:594
  12.0 10.0 %collective-permute-start.2 = (bf16[672,128]{1,0:T(8,128)(2,1)S(1)}, bf16[672,128]{1,0:T(8,128)(2,1)S(1)}, u32[]{:S(2)}, u32[]{:S(2)}) collective-permute-start(bf16[672,128]{1,0:T(8,128)(2,1)S(1)} %get-tuple-element.110), channel_id=1, source_target_pairs={{0,1},{2,3},{4,5},{6,7},{1,0},{3,2},{5,4},{7,6},{8,9},{10,11},{12,... | collective-permute-start | bytes 516104 | tf_op jit(solution)/shard_map/ppermute | solution.py:594
  24.0 12.4 %collective-permute-start.4 = (bf16[592,128]{1,0:T(8,128)(2,1)S(1)}, bf16[592,128]{1,0:T(8,128)(2,1)S(1)}, u32[]{:S(2)}, u32[]{:S(2)}) collective-permute-start(bf16[592,128]{1,0:T(8,128)(2,1)S(1)} %get-tuple-element.80), channel_id=1, source_target_pairs={{0,8},{16,24},{32,40},{48,56},{8,0},{24,16},{40,32},{56,48},{1,9},... | collective-permute-start | bytes 454664 | tf_op jit(solution)/shard_map/ppermute | solution.py:594
  30.9 5.4 %collective-permute-start.5 = (bf16[592,128]{1,0:T(8,128)(2,1)S(1)}, bf16[592,128]{1,0:T(8,128)(2,1)S(1)}, u32[]{:S(2)}, u32[]{:S(2)}) collective-permute-start(bf16[592,128]{1,0:T(8,128)(2,1)S(1)} %get-tuple-element.81), channel_id=1, source_target_pairs={{8,16},{24,32},{40,48},{16,8},{32,24},{48,40},{9,17},{25,33},{41,4... | collective-permute-start | bytes 454664 | tf_op jit(solution)/shard_map/ppermute | solution.py:594
  31.8 4.6 %copy-start.10 = (bf16[32,8,3,3,3]{0,1,4,3,2:T(8,128)(2,1)S(1)}, bf16[32,8,3,3,3]{0,1,4,3,2:T(8,128)(2,1)}, u32[]{:S(2)}) copy-start(bf16[32,8,3,3,3]{0,1,4,3,2:T(8,128)(2,1)} %param.16) | copy-start | bytes 41476
  31.8 4.6 %copy-start.11 = (bf16[256,256]{1,0:T(8,128)(2,1)S(1)}, bf16[256,256]{1,0:T(8,128)(2,1)}, u32[]{:S(2)}) copy-start(bf16[256,256]{1,0:T(8,128)(2,1)} %constant.11.clone.up_ref) | copy-start | bytes 393220
  39.1 26.6 %all-to-all-start = ((bf16[128,5,2,128]{3,2,1,0:T(2,128)(2,1)}), bf16[128,5,2,128]{3,2,1,0:T(2,128)(2,1)S(1)}, u32[]{:S(2)}, u32[]{:S(2)}) async-start(bf16[128,5,2,128]{3,2,1,0:T(2,128)(2,1)} %bitcast.21), calls=%async_computation | async-start | bytes 655360 | tf_op jit(solution)/shard_map/all_to_all | solution.py:729
  53.7 13.1 %collective-permute-start.6 = (bf16[208,128]{1,0:T(8,128)(2,1)S(1)}, bf16[208,128]{1,0:T(8,128)(2,1)S(1)}, u32[]{:S(2)}, u32[]{:S(2)}) collective-permute-start(bf16[208,128]{1,0:T(8,128)(2,1)S(1)} %get-tuple-element.89), channel_id=1, source_target_pairs={{0,8},{16,24},{32,40},{48,56},{8,0},{24,16},{40,32},{56,48},{1,9},... | collective-permute-start | bytes 159752 | tf_op jit(solution)/shard_map/ppermute | solution.py:594
  55.3 11.5 %collective-permute-start.7 = (bf16[208,128]{1,0:T(8,128)(2,1)S(1)}, bf16[208,128]{1,0:T(8,128)(2,1)S(1)}, u32[]{:S(2)}, u32[]{:S(2)}) collective-permute-start(bf16[208,128]{1,0:T(8,128)(2,1)S(1)} %get-tuple-element.90), channel_id=1, source_target_pairs={{8,16},{24,32},{40,48},{16,8},{32,24},{48,40},{9,17},{25,33},{41,4... | collective-permute-start | bytes 159752 | tf_op jit(solution)/shard_map/ppermute | solution.py:594
  66.8 17.1 %all-to-all-start.1 = ((bf16[128,5,2,128]{3,2,1,0:T(2,128)(2,1)}), bf16[128,5,2,128]{3,2,1,0:T(2,128)(2,1)S(1)}, u32[]{:S(2)}, u32[]{:S(2)}) async-start(bf16[128,5,2,128]{3,2,1,0:T(2,128)(2,1)} %bitcast.23), calls=%async_computation.1 | async-start | bytes 655360 | tf_op jit(solution)/shard_map/all_to_all | solution.py:734
  72.0 13.2 %collective-permute-start.8 = (bf16[32,128]{1,0:T(8,128)(2,1)S(1)}, bf16[32,128]{1,0:T(8,128)(2,1)S(1)}, u32[]{:S(2)}, u32[]{:S(2)}) collective-permute-start(bf16[32,128]{1,0:T(8,128)(2,1)S(1)} %get-tuple-element.97), channel_id=1, source_target_pairs={{0,1},{2,3},{4,5},{6,7},{1,0},{3,2},{5,4},{7,6},{8,9},{10,11},{12,... | collective-permute-start | bytes 24584 | tf_op jit(solution)/shard_map/ppermute | solution.py:594
  75.3 9.8 %collective-permute-start.9 = (bf16[32,128]{1,0:T(8,128)(2,1)S(1)}, bf16[32,128]{1,0:T(8,128)(2,1)S(1)}, u32[]{:S(2)}, u32[]{:S(2)}) collective-permute-start(bf16[32,128]{1,0:T(8,128)(2,1)S(1)} %get-tuple-element.98), channel_id=1, source_target_pairs={{1,2},{3,4},{5,6},{2,1},{4,3},{6,5},{9,10},{11,12},{13,14},{10,9},... | collective-permute-start | bytes 24584 | tf_op jit(solution)/shard_map/ppermute | solution.py:594

commit v6 on v5

--- a/solution.py
+++ b/solution.py
@@ -219,7 +219,7 @@
                 acc_ref[x, y + r] += sum(parts[1:], parts[0])
         return carry
 
-    lax.fori_loop(0, 6, step, 0)
+    lax.fori_loop(0, 6, step, 0, unroll=2)
     for m in range(1, 5):
 
         def rows_of(x, j):
@@ -375,7 +375,7 @@
         skip_ref[...] += dot_nt(rows, hidden_rows(hpad_ref, [y + j for j in range(4)]))
         return carry
 
-    lax.fori_loop(0, 6, step, 0)
+    lax.fori_loop(0, 6, step, 0, unroll=2)
     rows_ref[0:288, :] = jnp.concatenate([skip_ref[...], jnp.zeros((288, 32), F32)], axis=1).astype(BF16)
 
     def side(bx, m):
@@ -540,18 +540,14 @@
     out_ref[...] = dot_tn(pick, total).astype(BF16)
 
 
-def unpack_body(scale, rows_ref, enc_ref, mid_ref, dec_ref, head_ref):
+def unpack_body(
+    scale, rows_ref, enc_far, mid_far, dec_far, head_far, enc_ref, mid_ref, dec_ref, head_ref, sems
+):
     def rows(at, count):
         return rows_ref[at : at + count, :].astype(F32) * scale
 
-    skip = [rows(i * 32, 32) for i in range(9)]
-    head_ref[...] = rows(720, 16)[:8, :32]
-    mid_rest = [rows(1024 + i * 48, 48) for i in range(3)]
-    mid_rest = jnp.concatenate(mid_rest, axis=0)
+    mid_rest = rows(1024, 144)
     mid_rest = jnp.concatenate([mid_rest[:, :64], mid_rest[:, 64:]], axis=0)
-    enc = rows(1168, 80)
-    lift = rows(288, 432)
-    lift = jnp.concatenate([lift[:, :64], lift[:, 64:]], axis=0)
     for a in range(3):
         for b in range(3):
             tap = a * 3 + b
@@ -559,12 +555,26 @@
             mid_ref[a, b, 0] = pair[:, :64]
             mid_ref[a, b, 1] = pair[:, 64:]
             mid_ref[a, b, 2] = mid_rest[tap * 32 : tap * 32 + 32]
+    writes = fetch([(mid_ref, mid_far)], sems.at[0])
+    lift = rows(288, 432)
+    lift = jnp.concatenate([lift[:, :64], lift[:, 64:]], axis=0)
+    for a in range(3):
+        skip = [rows((a * 3 + c) * 32, 32) for c in range(3)]
+        for b in range(3):
             for c in range(3):
+                at = ((a * 3 + b) * 3 + c) * 32
+                dec_ref[a, b, c] = jnp.concatenate([lift[at : at + 32], skip[c][:, b * 32 : b * 32 + 32]], axis=1)
+        writes += fetch([(dec_ref.at[a], dec_far.at[a])], sems.at[1 + a])
+    enc = rows(1168, 80)
+    for a in range(3):
+        for b in range(3):
+            for c in range(3):
+                tap = a * 3 + b
                 enc_ref[a, b, c] = enc[tap * 8 : tap * 8 + 8, c * 32 : c * 32 + 32]
-                at = (tap * 3 + c) * 32
-                dec_ref[a, b, c] = jnp.concatenate(
-                    [lift[at : at + 32], skip[a * 3 + c][:, b * 32 : b * 32 + 32]], axis=1
-                )
+    head_ref[...] = rows(720, 16)[:8, :32]
+    writes += fetch([(enc_ref, enc_far), (head_ref, head_far)], sems.at[4])
+    for wait in writes:
+        wait()
 
 
 def pool_matrix():
@@ -739,9 +749,15 @@
     genc, gmid, gdec, ghead = call(
         functools.partial(unpack_body, grad_scale),
         [sds((3, 3, 3, 8, 32), F32), sds((3, 3, 3, 32, 64), F32), sds((3, 3, 3, 32, 96), F32), sds((8, 32), F32)],
-        [],
+        [
+            pltpu.VMEM((3, 3, 3, 8, 32), F32),
+            pltpu.VMEM((3, 3, 3, 32, 64), F32),
+            pltpu.VMEM((3, 3, 3, 32, 96), F32),
+            pltpu.VMEM((8, 32), F32),
+            pltpu.SemaphoreType.DMA((5, 2)),
+        ],
         (rows,),
-        1 << 20, 12,
+        1 << 20, 12, far_outs=4,
     )
     genc, end1, end2 = lax.optimization_barrier((genc, end1, end2))
     (state_grad,) = call(

time: 86.4 us -> 86.3 us (level)
  Pallas kernels: 21.8 us -> 20.9 us
  starting transfers between devices: 42.9 us -> 43.8 us
    pallas_call x10, Pallas kernels: 21.8 us -> 20.9 us  [call(): pl.pallas_call(body, out_shape=outs, in_specs=[HBM] * far + [VMEM] * (len...]
  transfers between devices with their start and end apart: 12 -> 12, of which waited for: 2 -> 2; matrix products, arithmetic and copies ran while one was open for 3% -> 3% of each run, Pallas kernels for 16% -> 15%
where the time goes in v6:
time: 86.3 us; the launch traced here: 85.9 us
  starting transfers between devices  43.8 us (51%)
  Pallas kernels  20.9 us (24%)
  waiting for transfers between devices  17.7 us (21%)
  local copies, waits for them, and re-layouts  2.49 us (3%)
  between operations  1.08 us (1%)
    ppermute x10, starting transfers between devices, swaps(): lax.ppermute(v, axis, ahead + [(b, a) for a, b in ahead])  23.6 us
    pallas_call x10, Pallas kernels, call(): pl.pallas_call(body, out_shape=outs, in_specs=[HBM] * far + [VMEM] * (len...  20.9 us
    all_to_all x1, starting transfers between devices, on_device(): pieces = lax.all_to_all(rows.reshape(shape), axes, 0, 0).reshape(1280, 128)  15.1 us
    all_to_all x1, waiting for transfers between devices, on_device(): pieces = lax.all_to_all(rows.reshape(shape), axes, 0, 0).reshape(1280, 128)  9.71 us
    all_to_all x1, waiting for transfers between devices, on_device(): rows = lax.all_to_all(shares.reshape(shape), axes, 0, 0).reshape(1280, 128)  7.92 us
    all_to_all x1, starting transfers between devices, on_device(): rows = lax.all_to_all(shares.reshape(shape), axes, 0, 0).reshape(1280, 128)  5.11 us
  transfers between devices with their start and end apart: 12, of which 2 were waited for; matrix products, arithmetic and copies ran while one was open for 3% of the time, Pallas kernels for 15%

profile of v6, /device:TPU:1, one launch (start us, length us, event | category | flops | bytes accessed | tf_op | source)
XLA Modules:
  0.0 85.9 jit_solution(13702350539147345991)
XLA Ops:
  0.7 2.5 %shard_map.146 = (bf16[24,32,128]{2,1,0:T(8,128)(2,1)}, bf16[24,32,128]{2,1,0:T(8,128)(2,1)}) custom-call(bf16[32,4,24,128]{3,2,1,0:T(8,128)(2,1)} %bitcast.31, bf16[8,4,24,128]{3,2,1,0:T(8,128)(2,1)} %bitcast.33, bf16[8,32]{1,0:T(8,128)(2,1)} %head_ref.1), custom_call_target="tpu_custom_call" | custom-call | flops 209715200 | bytes 4194304 | tf_op jit(solution)/shard_map/pallas_call | solution.py:21
  3.2 2.5 %collective-permute-start = (bf16[24,32,128]{2,1,0:T(8,128)(2,1)}, bf16[24,32,128]{2,1,0:T(8,128)(2,1)S(1)}, u32[]{:S(2)}, u32[]{:S(2)}) collective-permute-start(bf16[24,32,128]{2,1,0:T(8,128)(2,1)} %get-tuple-element.55.face1_ref), channel_id=1, source_target_pairs={{0,8},{16,24},{32,40},{48,56},{8,0},{24,16},{40,32},{56,48},{1,9},... | collective-permute-start | bytes 589832 | tf_op jit(solution)/shard_map/ppermute | solution.py:604
  5.7 0.7 collective-permute-start.1
  6.4 0.8 fusion.2
  7.2 1.3 %copy.18 = bf16[64,2,6,2,64]{4,3,0,2,1:T(2,128)(2,1)S(1)} copy(bf16[64,2,6,2,64]{4,1,3,2,0:T(2,128)(2,1)} %bitcast.44) | data formatting | bytes 393216 | tf_op jit(solution)/shard_map/reshape;squeeze | solution.py:637
  8.8 2.3 %shard_map.147 = (bf16[2,24,32,128]{3,2,1,0:T(8,128)(2,1)S(1)}, f32[8,32]{1,0:T(8,128)S(1)}, bf16[4,24,32,128]{3,2,1,0:T(8,128)(2,1)S(1)}, f32[4,24,32,128]{3,2,...) custom-call(bf16[32,4,24,128]{3,2,1,0:T(8,128)(2,1)S(1)} %bitcast.32, ...), custom_call_target="tpu_custom_call" | custom-call | flops 629145600 | bytes 4194304 | tf_op jit(solution)/shard_map/pallas_call | solution.py:21
  11.4 0.7 collective-permute-start.3
  12.0 5.2 %collective-permute-start.2 = (bf16[672,128]{1,0:T(8,128)(2,1)S(1)}, bf16[672,128]{1,0:T(8,128)(2,1)S(1)}, u32[]{:S(2)}, u32[]{:S(2)}) collective-permute-start(bf16[672,128]{1,0:T(8,128)(2,1)S(1)} %get-tuple-element.110), channel_id=1, source_target_pairs={{0,1},{2,3},{4,5},{6,7},{1,0},{3,2},{5,4},{7,6},{8,9},{10,11},{12,... | collective-permute-start | bytes 516104 | tf_op jit(solution)/shard_map/ppermute | solution.py:604
  17.3 4.4 %shard_map.148 = (f32[4,26,32,128]{3,2,1,0:T(8,128)S(1)}, bf16[6,24,96,128]{3,2,1,0:T(8,128)(2,1)S(1)}, bf16[864,1024]{1,0:T(8,128)(2,1)S(1)}, f32[64,1024]{1,0:...) custom-call(bf16[24,32,128]{2,1,0:T(8,128)(2,1)S(1)} %collective-permute-done.g, ...), custom_call_target="tpu_custom_call" | custom-call | flops 3221225472 | bytes 4194304 | tf_op jit(solution)/shard_map/pallas_call | solution.py:21
  21.7 1.9 %shard_map.149 = (f32[4,2,32,128]{3,2,1,0:T(8,128)S(1)}, bf16[6,2,96,128]{3,2,1,0:T(8,128)(2,1)S(1)}, bf16[864,768]{1,0:T(8,128)(2,1)S(1)}, bf16[192,1792]{1,0:T...) custom-call(bf16[672,128]{1,0:T(8,128)(2,1)S(1)} %collective-permute-don, ...), custom_call_target="tpu_custom_call" | custom-call | flops 1073741824 | bytes 4194304 | tf_op jit(solution)/shard_map/pallas_call | solution.py:21
  23.6 7.4 %collective-permute-start.4 = (bf16[592,128]{1,0:T(8,128)(2,1)S(1)}, bf16[592,128]{1,0:T(8,128)(2,1)S(1)}, u32[]{:S(2)}, u32[]{:S(2)}) collective-permute-start(bf16[592,128]{1,0:T(8,128)(2,1)S(1)} %get-tuple-element.80), channel_id=1, source_target_pairs={{0,8},{16,24},{32,40},{48,56},{8,0},{24,16},{40,32},{56,48},{1,9},... | collective-permute-start | bytes 454664 | tf_op jit(solution)/shard_map/ppermute | solution.py:604
  30.9 0.8 collective-permute-start.5
  31.8 4.1 %shard_map.150 = (bf16[736,128]{1,0:T(8,128)(2,1)S(1)}, f32[288,192]{1,0:T(8,128)S(1)}) custom-call(bf16[6,24,96,128]{3,2,1,0:T(8,128)(2,1)S(1)} %get-tuple-element.61.wide_ref, bf16[6,2,96,128]{3,2,1,0:T(8,128)(2,1)S(1)} %get-tuple-element.71.rim_ref, bf16[4,24,32,128]{3,2,1,0:T(8,128)(2,1)S(1)} %get-tuple-element.72.hid_ref, ...), custom_call_target="tpu_custom_call" | custom-call | flops 3221225472 | bytes 4194304 | tf_op jit(solution)/shard_map/pallas_call | solution.py:21
  35.9 2.7 %shard_map.151 = (bf16[1280,128]{1,0:T(8,128)(2,1)}, f32[4,24,8,128]{3,2,1,0:T(8,128)S(1)}, bf16[208,128]{1,0:T(8,128)(2,1)S(1)}, bf16[208,128]{1,0:T(8,128)(2,1...) custom-call(f32[4,26,32,128]{3,2,1,0:T(8,128)S(1)} %get-tuple-element.58.acc_ref, ...), custom_call_target="tpu_custom_call" | custom-call | flops 2147483648 | bytes 4194304 | tf_op jit(solution)/shard_map/pallas_call | solution.py:21
  38.6 15.1 %all-to-all-start = ((bf16[128,5,2,128]{3,2,1,0:T(2,128)(2,1)}), bf16[128,5,2,128]{3,2,1,0:T(2,128)(2,1)S(1)}, u32[]{:S(2)}, u32[]{:S(2)}) async-start(bf16[128,5,2,128]{3,2,1,0:T(2,128)(2,1)} %bitcast.21), calls=%async_computation | async-start | bytes 655360 | tf_op jit(solution)/shard_map/all_to_all | solution.py:739
  53.7 1.6 %collective-permute-start.6 = (bf16[208,128]{1,0:T(8,128)(2,1)S(1)}, bf16[208,128]{1,0:T(8,128)(2,1)S(1)}, u32[]{:S(2)}, u32[]{:S(2)}) collective-permute-start(bf16[208,128]{1,0:T(8,128)(2,1)S(1)} %get-tuple-element.89), channel_id=1, source_target_pairs={{0,8},{16,24},{32,40},{48,56},{8,0},{24,16},{40,32},{56,48},{1,9},... | collective-permute-start | bytes 159752 | tf_op jit(solution)/shard_map/ppermute | solution.py:604
  55.3 0.7 collective-permute-start.7
  56.0 9.7 %all-to-all-done = bf16[128,5,2,128]{3,2,1,0:T(2,128)(2,1)S(1)} async-done(((bf16[128,5,2,128]{3,2,1,0:T(2,128)(2,1)}), bf16[128,5,2,128]{3,2,1,0:T(2,128)(2,1)S(1)}, u32[]{:S(2)}, u32[]{:S(2)}) %all-to-all-start) | async-done | bytes 327712 | tf_op jit(solution)/shard_map/all_to_all | solution.py:739
  65.7 1.1 %shard_map.152 = bf16[1280,128]{1,0:T(8,128)(2,1)} custom-call(bf16[1280,128]{1,0:T(8,128)(2,1)S(1)} %bitcast.37), custom_call_target="tpu_custom_call" | custom-call | flops 1048576 | bytes 4194304 | tf_op jit(solution)/shard_map/pallas_call | solution.py:21
  66.8 5.1 %all-to-all-start.1 = ((bf16[128,5,2,128]{3,2,1,0:T(2,128)(2,1)}), bf16[128,5,2,128]{3,2,1,0:T(2,128)(2,1)S(1)}, u32[]{:S(2)}, u32[]{:S(2)}) async-start(bf16[128,5,2,128]{3,2,1,0:T(2,128)(2,1)} %bitcast.23), calls=%async_computation.1 | async-start | bytes 655360 | tf_op jit(solution)/shard_map/all_to_all | solution.py:744
  72.0 3.4 %collective-permute-start.8 = (bf16[32,128]{1,0:T(8,128)(2,1)S(1)}, bf16[32,128]{1,0:T(8,128)(2,1)S(1)}, u32[]{:S(2)}, u32[]{:S(2)}) collective-permute-start(bf16[32,128]{1,0:T(8,128)(2,1)S(1)} %get-tuple-element.97), channel_id=1, source_target_pairs={{0,1},{2,3},{4,5},{6,7},{1,0},{3,2},{5,4},{7,6},{8,9},{10,11},{12,... | collective-permute-start | bytes 24584 | tf_op jit(solution)/shard_map/ppermute | solution.py:604
  76.0 7.9 %all-to-all-done.1 = bf16[128,5,2,128]{3,2,1,0:T(2,128)(2,1)S(1)} async-done(((bf16[128,5,2,128]{3,2,1,0:T(2,128)(2,1)}), bf16[128,5,2,128]{3,2,1,0:T(2,128)(2,1)S(1)}, u32[]{:S(2)}, u32[]{:S(2)}) %all-to-all-start.1) | async-done | bytes 327712 | tf_op jit(solution)/shard_map/all_to_all | solution.py:744
  83.9 1.2 %shard_map.153 = (f32[3,3,3,8,32]{4,3,2,1,0:T(8,128)}, f32[3,3,3,32,64]{4,3,2,1,0:T(8,128)}, f32[3,3,3,32,96]{4,3,2,1,0:T(8,128)}, f32[8,32]{1,0:T(8,128)}) custom-call(bf16[1280,128]{1,0:T(8,128)(2,1)S(1)} %bitcast.36), custom_call_target="tpu_custom_call" | custom-call | flops 1048576 | bytes 4194304 | tf_op jit(solution)/shard_map/pallas_call | solution.py:21
  85.1 0.8 shard_map.155
  (55 shorter events, 1.1 us)
Async XLA Ops:
  0.6 8.1 %copy-start.2 = (bf16[256,384]{1,0:T(8,128)(2,1)S(1)}, bf16[256,384]{1,0:T(8,128)(2,1)}, u32[]{:S(2)}) copy-start(bf16[256,384]{1,0:T(8,128)(2,1)} %constant.10.clone.pool_ref) | copy-start | bytes 589828
  0.6 8.1 %copy-start.7 = (bf16[8,32]{1,0:T(8,128)(2,1)S(1)}, bf16[8,32]{1,0:T(8,128)(2,1)}, u32[]{:S(2)}) copy-start(bf16[8,32]{1,0:T(8,128)(2,1)} %head_ref.1) | copy-start | bytes 1540
  0.7 8.1 %copy-start.1 = (bf16[1,8,4,24,128]{4,3,2,1,0:T(8,128)(2,1)S(1)}, bf16[1,8,4,24,128]{4,3,2,1,0:T(8,128)(2,1)}, u32[]{:S(2)}) copy-start(bf16[1,8,4,24,128]{4,3,2,1,0:T(8,128)(2,1)} %param.15) | copy-start | bytes 589828
  0.7 8.1 %copy-start = (bf16[1,32,4,24,128]{4,3,2,1,0:T(8,128)(2,1)S(1)}, bf16[1,32,4,24,128]{4,3,2,1,0:T(8,128)(2,1)}, u32[]{:S(2)}) copy-start(bf16[1,32,4,24,128]{4,3,2,1,0:T(8,128)(2,1)} %param.14) | copy-start | bytes 2359300
  0.7 8.1 %copy-start.3 = (bf16[1,32,4,24,128]{4,3,2,1,0:T(8,128)(2,1)S(1)}, bf16[1,32,4,24,128]{4,3,2,1,0:T(8,128)(2,1)}, u32[]{:S(2)}) copy-start(bf16[1,32,4,24,128]{4,3,2,1,0:T(8,128)(2,1)} %param.12) | copy-start | bytes 2359300
  0.7 8.1 %copy-start.4 = (bf16[1,8,4,24,128]{4,3,2,1,0:T(8,128)(2,1)S(1)}, bf16[1,8,4,24,128]{4,3,2,1,0:T(8,128)(2,1)}, u32[]{:S(2)}) copy-start(bf16[1,8,4,24,128]{4,3,2,1,0:T(8,128)(2,1)} %param.11) | copy-start | bytes 589828
  3.2 7.9 %collective-permute-start = (bf16[24,32,128]{2,1,0:T(8,128)(2,1)}, bf16[24,32,128]{2,1,0:T(8,128)(2,1)S(1)}, u32[]{:S(2)}, u32[]{:S(2)}) collective-permute-start(bf16[24,32,128]{2,1,0:T(8,128)(2,1)} %get-tuple-element.55.face1_ref), channel_id=1, source_target_pairs={{0,8},{16,24},{32,40},{48,56},{8,0},{24,16},{40,32},{56,48},{1,9},... | collective-permute-start | bytes 589832 | tf_op jit(solution)/shard_map/ppermute | solution.py:604
  5.7 5.5 %collective-permute-start.1 = (bf16[24,32,128]{2,1,0:T(8,128)(2,1)}, bf16[24,32,128]{2,1,0:T(8,128)(2,1)S(1)}, u32[]{:S(2)}, u32[]{:S(2)}) collective-permute-start(bf16[24,32,128]{2,1,0:T(8,128)(2,1)} %get-tuple-element.57.face2_ref), channel_id=1, source_target_pairs={{8,16},{24,32},{40,48},{16,8},{32,24},{48,40},{9,17},{25,33},{41,4... | collective-permute-start | bytes 589832 | tf_op jit(solution)/shard_map/ppermute | solution.py:604
  8.7 8.5 %copy-start.5 = (bf16[24,32,128]{2,1,0:T(8,128)(2,1)S(1)}, bf16[24,32,128]{2,1,0:T(8,128)(2,1)}, u32[]{:S(2)}) copy-start(bf16[24,32,128]{2,1,0:T(8,128)(2,1)} %get-tuple-element.55.face1_ref) | copy-start | bytes 589828
  8.8 8.5 %copy-start.6 = (bf16[24,32,128]{2,1,0:T(8,128)(2,1)S(1)}, bf16[24,32,128]{2,1,0:T(8,128)(2,1)}, u32[]{:S(2)}) copy-start(bf16[24,32,128]{2,1,0:T(8,128)(2,1)} %get-tuple-element.57.face2_ref) | copy-start | bytes 589828
  8.8 8.5 %copy-start.8 = (bf16[32,96,3,3,3]{1,0,4,3,2:T(8,128)(2,1)S(1)}, bf16[32,96,3,3,3]{1,0,4,3,2:T(8,128)(2,1)}, u32[]{:S(2)}) copy-start(bf16[32,96,3,3,3]{1,0,4,3,2:T(8,128)(2,1)} %param.18) | copy-start | bytes 497668
  8.8 8.5 %copy-start.9 = (bf16[64,32,3,3,3]{0,1,4,3,2:T(8,128)(2,1)S(1)}, bf16[64,32,3,3,3]{0,1,4,3,2:T(8,128)(2,1)}, u32[]{:S(2)}) copy-start(bf16[64,32,3,3,3]{0,1,4,3,2:T(8,128)(2,1)} %param.17) | copy-start | bytes 331780
  11.4 10.3 %collective-permute-start.3 = (bf16[672,128]{1,0:T(8,128)(2,1)S(1)}, bf16[672,128]{1,0:T(8,128)(2,1)S(1)}, u32[]{:S(2)}, u32[]{:S(2)}) collective-permute-start(bf16[672,128]{1,0:T(8,128)(2,1)S(1)} %get-tuple-element.109), channel_id=1, source_target_pairs={{1,2},{3,4},{5,6},{2,1},{4,3},{6,5},{9,10},{11,12},{13,14},{10,9},... | collective-permute-start | bytes 516104 | tf_op jit(solution)/shard_map/ppermute | solution.py:604
  12.0 9.6 %collective-permute-start.2 = (bf16[672,128]{1,0:T(8,128)(2,1)S(1)}, bf16[672,128]{1,0:T(8,128)(2,1)S(1)}, u32[]{:S(2)}, u32[]{:S(2)}) collective-permute-start(bf16[672,128]{1,0:T(8,128)(2,1)S(1)} %get-tuple-element.110), channel_id=1, source_target_pairs={{0,1},{2,3},{4,5},{6,7},{1,0},{3,2},{5,4},{7,6},{8,9},{10,11},{12,... | collective-permute-start | bytes 516104 | tf_op jit(solution)/shard_map/ppermute | solution.py:604
  23.6 12.3 %collective-permute-start.4 = (bf16[592,128]{1,0:T(8,128)(2,1)S(1)}, bf16[592,128]{1,0:T(8,128)(2,1)S(1)}, u32[]{:S(2)}, u32[]{:S(2)}) collective-permute-start(bf16[592,128]{1,0:T(8,128)(2,1)S(1)} %get-tuple-element.80), channel_id=1, source_target_pairs={{0,8},{16,24},{32,40},{48,56},{8,0},{24,16},{40,32},{56,48},{1,9},... | collective-permute-start | bytes 454664 | tf_op jit(solution)/shard_map/ppermute | solution.py:604
  30.9 4.9 %collective-permute-start.5 = (bf16[592,128]{1,0:T(8,128)(2,1)S(1)}, bf16[592,128]{1,0:T(8,128)(2,1)S(1)}, u32[]{:S(2)}, u32[]{:S(2)}) collective-permute-start(bf16[592,128]{1,0:T(8,128)(2,1)S(1)} %get-tuple-element.81), channel_id=1, source_target_pairs={{8,16},{24,32},{40,48},{16,8},{32,24},{48,40},{9,17},{25,33},{41,4... | collective-permute-start | bytes 454664 | tf_op jit(solution)/shard_map/ppermute | solution.py:604
  31.8 4.1 %copy-start.10 = (bf16[32,8,3,3,3]{0,1,4,3,2:T(8,128)(2,1)S(1)}, bf16[32,8,3,3,3]{0,1,4,3,2:T(8,128)(2,1)}, u32[]{:S(2)}) copy-start(bf16[32,8,3,3,3]{0,1,4,3,2:T(8,128)(2,1)} %param.16) | copy-start | bytes 41476
  31.8 4.1 %copy-start.11 = (bf16[256,256]{1,0:T(8,128)(2,1)S(1)}, bf16[256,256]{1,0:T(8,128)(2,1)}, u32[]{:S(2)}) copy-start(bf16[256,256]{1,0:T(8,128)(2,1)} %constant.11.clone.up_ref) | copy-start | bytes 393220
  38.6 27.1 %all-to-all-start = ((bf16[128,5,2,128]{3,2,1,0:T(2,128)(2,1)}), bf16[128,5,2,128]{3,2,1,0:T(2,128)(2,1)S(1)}, u32[]{:S(2)}, u32[]{:S(2)}) async-start(bf16[128,5,2,128]{3,2,1,0:T(2,128)(2,1)} %bitcast.21), calls=%async_computation | async-start | bytes 655360 | tf_op jit(solution)/shard_map/all_to_all | solution.py:739
  53.7 13.1 %collective-permute-start.6 = (bf16[208,128]{1,0:T(8,128)(2,1)S(1)}, bf16[208,128]{1,0:T(8,128)(2,1)S(1)}, u32[]{:S(2)}, u32[]{:S(2)}) collective-permute-start(bf16[208,128]{1,0:T(8,128)(2,1)S(1)} %get-tuple-element.89), channel_id=1, source_target_pairs={{0,8},{16,24},{32,40},{48,56},{8,0},{24,16},{40,32},{56,48},{1,9},... | collective-permute-start | bytes 159752 | tf_op jit(solution)/shard_map/ppermute | solution.py:604
  55.3 11.5 %collective-permute-start.7 = (bf16[208,128]{1,0:T(8,128)(2,1)S(1)}, bf16[208,128]{1,0:T(8,128)(2,1)S(1)}, u32[]{:S(2)}, u32[]{:S(2)}) collective-permute-start(bf16[208,128]{1,0:T(8,128)(2,1)S(1)} %get-tuple-element.90), channel_id=1, source_target_pairs={{8,16},{24,32},{40,48},{16,8},{32,24},{48,40},{9,17},{25,33},{41,4... | collective-permute-start | bytes 159752 | tf_op jit(solution)/shard_map/ppermute | solution.py:604
  66.8 17.1 %all-to-all-start.1 = ((bf16[128,5,2,128]{3,2,1,0:T(2,128)(2,1)}), bf16[128,5,2,128]{3,2,1,0:T(2,128)(2,1)S(1)}, u32[]{:S(2)}, u32[]{:S(2)}) async-start(bf16[128,5,2,128]{3,2,1,0:T(2,128)(2,1)} %bitcast.23), calls=%async_computation.1 | async-start | bytes 655360 | tf_op jit(solution)/shard_map/all_to_all | solution.py:744
  72.0 13.1 %collective-permute-start.8 = (bf16[32,128]{1,0:T(8,128)(2,1)S(1)}, bf16[32,128]{1,0:T(8,128)(2,1)S(1)}, u32[]{:S(2)}, u32[]{:S(2)}) collective-permute-start(bf16[32,128]{1,0:T(8,128)(2,1)S(1)} %get-tuple-element.97), channel_id=1, source_target_pairs={{0,1},{2,3},{4,5},{6,7},{1,0},{3,2},{5,4},{7,6},{8,9},{10,11},{12,... | collective-permute-start | bytes 24584 | tf_op jit(solution)/shard_map/ppermute | solution.py:604
  75.3 9.7 %collective-permute-start.9 = (bf16[32,128]{1,0:T(8,128)(2,1)S(1)}, bf16[32,128]{1,0:T(8,128)(2,1)S(1)}, u32[]{:S(2)}, u32[]{:S(2)}) collective-permute-start(bf16[32,128]{1,0:T(8,128)(2,1)S(1)} %get-tuple-element.98), channel_id=1, source_target_pairs={{1,2},{3,4},{5,6},{2,1},{4,3},{6,5},{9,10},{11,12},{13,14},{10,9},... | collective-permute-start | bytes 24584 | tf_op jit(solution)/shard_map/ppermute | solution.py:604

commit v7 on v6

--- a/solution.py
+++ b/solution.py
@@ -242,11 +242,10 @@
 
 
 def outer_body(
-    got1_ref, got2_ref, wide_ref, up_ref, mslope_ref, st_ref, pooled_ref, pool_ref, wup_ref, wskip_ref, wm_ref,
-    edge_ref, rim_ref, win_ref, mid_ref, back_ref, face1_ref, face2_ref,
+    got1_ref, got2_ref, wide_ref, up_ref, mslope_ref, st_ref, pooled_ref, pool_ref, wup_ref, wm_ref,
+    win_ref, mid_ref, back_ref, face1_ref, face2_ref,
     total_ref, got_ref,
 ):
-    wskip = wskip_ref[...]
     odd_x, odd_y = parity("gx"), parity("gy")
     got_ref[1 - odd_y] = got1_ref[...]
     got_ref[odd_y] = got2_ref[...]
@@ -257,17 +256,6 @@
         slot = x + (1 - odd_x) * (5, 3, 0, 0, -3, -5)[x]
         at = (slot * 3 + (y + 3 if y < 0 else y - 24)) * 32
         return got_ref[0 if y < 0 else 1, pl.ds(pl.multiple_of(at, 32), 32), :]
-
-    for x in range(6):
-        v = jnp.concatenate([row(x, -1), row(x, 24)], axis=0).astype(F32)
-        parts = shifts(v, 128)
-        for a in range(3):
-            rim_ref[x, :, a * 32 : a * 32 + 32, :] = parts[a].astype(BF16).reshape(2, 32, 128)
-    outs = [dot(wskip, stack_of(lambda x, r=r: rim_ref[x, r])) for r in range(2)]
-    for x in range(4):
-        at = slice(x * 128, x * 128 + 128)
-        edge_ref[x, 0] = outs[0][64:96, at]
-        edge_ref[x, 1] = outs[1][0:32, at]
 
     for i, (left, right) in enumerate(((-1, 1), (19, 21), (23, -3))):
 
@@ -358,9 +346,29 @@
 
 
 def dec_grad_body(
-    wide_ref, rim_ref, hid_ref, win_ref, rim_win_ref, hmid_ref, head_ref, pooled_ref, mid_ref,
-    rows_ref, gmid_ref, hpad_ref, skip_ref,
+    got1_ref, got2_ref, wskip_ref, wide_ref, hid_ref, win_ref, rim_win_ref, hmid_ref, head_ref, pooled_ref, mid_ref,
+    edge_ref, rows_ref, gmid_ref, hpad_ref, skip_ref, rim_ref, got_ref,
 ):
+    odd_x, odd_y = parity("gx"), parity("gy")
+    got_ref[1 - odd_y] = got1_ref[...]
+    got_ref[odd_y] = got2_ref[...]
+
+    def row(x, y):
+        slot = x + (1 - odd_x) * (5, 3, 0, 0, -3, -5)[x]
+        at = (slot * 3 + (2 if y < 0 else 0)) * 32
+        return got_ref[0 if y < 0 else 1, pl.ds(pl.multiple_of(at, 32), 32), :]
+
+    for x in range(6):
+        v = jnp.concatenate([row(x, -1), row(x, 24)], axis=0).astype(F32)
+        parts = shifts(v, 128)
+        for a in range(3):
+            rim_ref[x, :, a * 32 : a * 32 + 32, :] = parts[a].astype(BF16).reshape(2, 32, 128)
+    outs = [dot(wskip_ref[...], stack_of(lambda x, r=r: rim_ref[x, r])) for r in range(2)]
+    for x in range(4):
+        at = slice(x * 128, x * 128 + 128)
+        edge_ref[x, 0] = outs[0][64:96, at]
+        edge_ref[x, 1] = outs[1][0:32, at]
+
     blank = jnp.zeros((2, 32, 128), BF16)
     for x in range(4):
         hpad_ref[x, 0:2] = blank
@@ -679,11 +687,9 @@
         (got1, face1, delta, face2, got2, pool, dec_w, mid_w),
         3 << 30, 24,
     )
-    edge, rim_wide, rim_win, mid_wide, back, face1, face2 = call(
+    rim_win, mid_wide, back, face1, face2 = call(
         outer_body,
         [
-            sds((4, 2, 32, 128), F32),
-            sds((6, 2, 96, 128), BF16),
             sds((864, 768), BF16),
             sds((192, 1792), BF16),
             sds((2, 6, 32, 128), F32),
@@ -691,15 +697,20 @@
             sds((592, 128), BF16),
         ],
         [pltpu.VMEM((4, 6, 32, 128), F32), pltpu.VMEM((2, 672, 128), BF16)],
-        (rim1, rim2, wide, up, mid_slope, state, pooled, pool, wup, wskip, wmid),
+        (rim1, rim2, wide, up, mid_slope, state, pooled, pool, wup, wmid),
         1 << 30, 24,
     )
     got1, got2 = swaps(face1, face2, "gx")
-    dec_rows, mid_grad = call(
+    edge, dec_rows, mid_grad = call(
         dec_grad_body,
-        [sds((736, 128), BF16), sds((288, 192), F32)],
-        [pltpu.VMEM((4, 28, 32, 128), BF16), pltpu.VMEM((288, 96), F32)],
-        (wide, rim_wide, hidden, win, rim_win, hidden_mid, head_grad, pooled, mid_wide),
+        [sds((4, 2, 32, 128), F32), sds((736, 128), BF16), sds((288, 192), F32)],
+        [
+            pltpu.VMEM((4, 28, 32, 128), BF16),
+            pltpu.VMEM((288, 96), F32),
+            pltpu.VMEM((6, 2, 96, 128), BF16),
+            pltpu.VMEM((2, 672, 128), BF16),
+        ],
+        (rim1, rim2, wskip, wide, hidden, win, rim_win, hidden_mid, head_grad, pooled, mid_wide),
         3 << 30, 20,
     )
     dec_rows, mid_grad, got1, got2 = lax.optimization_barrier((dec_rows, mid_grad, got1, got2))

time: 86.3 us -> 86.1 us (level)
  no operation moved by 1% of the time
where the time goes in v7:
time: 86.1 us; the launch traced here: 85.7 us
  starting transfers between devices  43.6 us (51%)
  Pallas kernels  20.8 us (24%)
  waiting for transfers between devices  17.7 us (21%)
  local copies, waits for them, and re-layouts  2.49 us (3%)
  between operations  1.08 us (1%)
    ppermute x10, starting transfers between devices, swaps(): lax.ppermute(v, axis, ahead + [(b, a) for a, b in ahead])  23.6 us
    pallas_call x10, Pallas kernels, call(): pl.pallas_call(body, out_shape=outs, in_specs=[HBM] * far + [VMEM] * (len...  20.8 us
    all_to_all x1, starting transfers between devices, on_device(): pieces = lax.all_to_all(rows.reshape(shape), axes, 0, 0).reshape(1280, 128)  14.9 us
    all_to_all x1, waiting for transfers between devices, on_device(): pieces = lax.all_to_all(rows.reshape(shape), axes, 0, 0).reshape(1280, 128)  9.71 us
    all_to_all x1, waiting for transfers between devices, on_device(): rows = lax.all_to_all(shares.reshape(shape), axes, 0, 0).reshape(1280, 128)  7.92 us
    all_to_all x1, starting transfers between devices, on_device(): rows = lax.all_to_all(shares.reshape(shape), axes, 0, 0).reshape(1280, 128)  5.1 us
  transfers between devices with their start and end apart: 12, of which 2 were waited for; matrix products, arithmetic and copies ran while one was open for 3% of the time, Pallas kernels for 15%

profile of v7, /device:TPU:1, one launch (start us, length us, event | category | flops | bytes accessed | tf_op | source)
XLA Modules:
  0.0 85.7 jit_solution(11589350526061935205)
XLA Ops:
  0.7 2.5 %shard_map.146 = (bf16[24,32,128]{2,1,0:T(8,128)(2,1)}, bf16[24,32,128]{2,1,0:T(8,128)(2,1)}) custom-call(bf16[32,4,24,128]{3,2,1,0:T(8,128)(2,1)} %bitcast.31, bf16[8,4,24,128]{3,2,1,0:T(8,128)(2,1)} %bitcast.33, bf16[8,32]{1,0:T(8,128)(2,1)} %head_ref.1), custom_call_target="tpu_custom_call" | custom-call | flops 209715200 | bytes 4194304 | tf_op jit(solution)/shard_map/pallas_call | solution.py:21
  3.2 2.5 %collective-permute-start = (bf16[24,32,128]{2,1,0:T(8,128)(2,1)}, bf16[24,32,128]{2,1,0:T(8,128)(2,1)S(1)}, u32[]{:S(2)}, u32[]{:S(2)}) collective-permute-start(bf16[24,32,128]{2,1,0:T(8,128)(2,1)} %get-tuple-element.54.face1_ref), channel_id=1, source_target_pairs={{0,8},{16,24},{32,40},{48,56},{8,0},{24,16},{40,32},{56,48},{1,9},... | collective-permute-start | bytes 589832 | tf_op jit(solution)/shard_map/ppermute | solution.py:612
  5.7 0.7 collective-permute-start.1
  6.4 0.8 fusion.2
  7.2 1.3 %copy.18 = bf16[64,2,6,2,64]{4,3,0,2,1:T(2,128)(2,1)S(1)} copy(bf16[64,2,6,2,64]{4,1,3,2,0:T(2,128)(2,1)} %bitcast.44) | data formatting | bytes 393216 | tf_op jit(solution)/shard_map/reshape;squeeze | solution.py:645
  8.8 2.3 %shard_map.147 = (bf16[2,24,32,128]{3,2,1,0:T(8,128)(2,1)S(1)}, f32[8,32]{1,0:T(8,128)S(1)}, bf16[4,24,32,128]{3,2,1,0:T(8,128)(2,1)S(1)}, f32[4,24,32,128]{3,2,...) custom-call(bf16[32,4,24,128]{3,2,1,0:T(8,128)(2,1)S(1)} %bitcast.32, ...), custom_call_target="tpu_custom_call" | custom-call | flops 629145600 | bytes 4194304 | tf_op jit(solution)/shard_map/pallas_call | solution.py:21
  11.4 0.7 collective-permute-start.3
  12.0 5.2 %collective-permute-start.2 = (bf16[672,128]{1,0:T(8,128)(2,1)S(1)}, bf16[672,128]{1,0:T(8,128)(2,1)S(1)}, u32[]{:S(2)}, u32[]{:S(2)}) collective-permute-start(bf16[672,128]{1,0:T(8,128)(2,1)S(1)} %get-tuple-element.108), channel_id=1, source_target_pairs={{0,1},{2,3},{4,5},{6,7},{1,0},{3,2},{5,4},{7,6},{8,9},{10,11},{12,... | collective-permute-start | bytes 516104 | tf_op jit(solution)/shard_map/ppermute | solution.py:612
  17.3 4.4 %shard_map.148 = (f32[4,26,32,128]{3,2,1,0:T(8,128)S(1)}, bf16[6,24,96,128]{3,2,1,0:T(8,128)(2,1)S(1)}, bf16[864,1024]{1,0:T(8,128)(2,1)S(1)}, f32[64,1024]{1,0:...) custom-call(bf16[24,32,128]{2,1,0:T(8,128)(2,1)S(1)} %collective-permute-done.g, ...), custom_call_target="tpu_custom_call" | custom-call | flops 3221225472 | bytes 4194304 | tf_op jit(solution)/shard_map/pallas_call | solution.py:21
  21.7 1.7 %shard_map.149 = (bf16[864,768]{1,0:T(8,128)(2,1)S(1)}, bf16[192,1792]{1,0:T(8,128)(2,1)S(1)}, f32[2,6,32,128]{3,2,1,0:T(8,128)S(1)}, bf16[592,128]{1,0:T(8,128)(2,1)S(1)}, bf16[592,128]{1,0:T(8,128)(2,1)S(1)}) custom-call(bf16[672,128]{1,0:T(8,128)(2,1)S(1)} %collective-permute-done.2.got1_ref.rim1_ref, ...), custom_call_target="tpu_custom_call" | custom-call | flops 1073741824 | bytes 4194304 | tf_op jit(solution)/shard_map/pallas_call | solution.py:21
  23.3 7.4 %collective-permute-start.4 = (bf16[592,128]{1,0:T(8,128)(2,1)S(1)}, bf16[592,128]{1,0:T(8,128)(2,1)S(1)}, u32[]{:S(2)}, u32[]{:S(2)}) collective-permute-start(bf16[592,128]{1,0:T(8,128)(2,1)S(1)} %get-tuple-element.78), channel_id=1, source_target_pairs={{0,8},{16,24},{32,40},{48,56},{8,0},{24,16},{40,32},{56,48},{1,9},... | collective-permute-start | bytes 454664 | tf_op jit(solution)/shard_map/ppermute | solution.py:612
  30.7 0.8 collective-permute-start.5
  31.6 4.2 %shard_map.150 = (f32[4,2,32,128]{3,2,1,0:T(8,128)S(1)}, bf16[736,128]{1,0:T(8,128)(2,1)S(1)}, f32[288,192]{1,0:T(8,128)S(1)}) custom-call(bf16[672,128]{1,0:T(8,128)(2,1)S(1)} %collective-permute-done.2.got1_ref.rim1_ref, bf16[672,128]{1,0:T(8,128)(2,1)S(1)} %collective-permute-done.3.got2_ref.rim2_ref, bf16[96,288]{1,0:T(8,128)(2,1)S(1)} %get-tuple-element.60.wskip_ref, ...), custom_call_target="tpu_custom_call" | custom-call | flops 3221225472 | bytes 4194304 | tf_op jit(solution)/shard_map/pallas_call | solution.py:21
  35.9 2.7 %shard_map.151 = (bf16[1280,128]{1,0:T(8,128)(2,1)}, f32[4,24,8,128]{3,2,1,0:T(8,128)S(1)}, bf16[208,128]{1,0:T(8,128)(2,1)S(1)}, bf16[208,128]{1,0:T(8,128)(2,1...) custom-call(f32[4,26,32,128]{3,2,1,0:T(8,128)S(1)} %get-tuple-element.57.acc_ref, ...), custom_call_target="tpu_custom_call" | custom-call | flops 2147483648 | bytes 4194304 | tf_op jit(solution)/shard_map/pallas_call | solution.py:21
  38.6 14.9 %all-to-all-start = ((bf16[128,5,2,128]{3,2,1,0:T(2,128)(2,1)}), bf16[128,5,2,128]{3,2,1,0:T(2,128)(2,1)S(1)}, u32[]{:S(2)}, u32[]{:S(2)}) async-start(bf16[128,5,2,128]{3,2,1,0:T(2,128)(2,1)} %bitcast.21), calls=%async_computation | async-start | bytes 655360 | tf_op jit(solution)/shard_map/all_to_all | solution.py:750
  53.5 1.6 %collective-permute-start.6 = (bf16[208,128]{1,0:T(8,128)(2,1)S(1)}, bf16[208,128]{1,0:T(8,128)(2,1)S(1)}, u32[]{:S(2)}, u32[]{:S(2)}) collective-permute-start(bf16[208,128]{1,0:T(8,128)(2,1)S(1)} %get-tuple-element.87), channel_id=1, source_target_pairs={{0,8},{16,24},{32,40},{48,56},{8,0},{24,16},{40,32},{56,48},{1,9},... | collective-permute-start | bytes 159752 | tf_op jit(solution)/shard_map/ppermute | solution.py:612
  55.1 0.7 collective-permute-start.7
  55.8 9.7 %all-to-all-done = bf16[128,5,2,128]{3,2,1,0:T(2,128)(2,1)S(1)} async-done(((bf16[128,5,2,128]{3,2,1,0:T(2,128)(2,1)}), bf16[128,5,2,128]{3,2,1,0:T(2,128)(2,1)S(1)}, u32[]{:S(2)}, u32[]{:S(2)}) %all-to-all-start) | async-done | bytes 327712 | tf_op jit(solution)/shard_map/all_to_all | solution.py:750
  65.5 1.1 %shard_map.152 = bf16[1280,128]{1,0:T(8,128)(2,1)} custom-call(bf16[1280,128]{1,0:T(8,128)(2,1)S(1)} %bitcast.37), custom_call_target="tpu_custom_call" | custom-call | flops 1048576 | bytes 4194304 | tf_op jit(solution)/shard_map/pallas_call | solution.py:21
  66.6 5.1 %all-to-all-start.1 = ((bf16[128,5,2,128]{3,2,1,0:T(2,128)(2,1)}), bf16[128,5,2,128]{3,2,1,0:T(2,128)(2,1)S(1)}, u32[]{:S(2)}, u32[]{:S(2)}) async-start(bf16[128,5,2,128]{3,2,1,0:T(2,128)(2,1)} %bitcast.23), calls=%async_computation.1 | async-start | bytes 655360 | tf_op jit(solution)/shard_map/all_to_all | solution.py:755
  71.7 3.4 %collective-permute-start.8 = (bf16[32,128]{1,0:T(8,128)(2,1)S(1)}, bf16[32,128]{1,0:T(8,128)(2,1)S(1)}, u32[]{:S(2)}, u32[]{:S(2)}) collective-permute-start(bf16[32,128]{1,0:T(8,128)(2,1)S(1)} %get-tuple-element.95), channel_id=1, source_target_pairs={{0,1},{2,3},{4,5},{6,7},{1,0},{3,2},{5,4},{7,6},{8,9},{10,11},{12,... | collective-permute-start | bytes 24584 | tf_op jit(solution)/shard_map/ppermute | solution.py:612
  75.8 7.9 %all-to-all-done.1 = bf16[128,5,2,128]{3,2,1,0:T(2,128)(2,1)S(1)} async-done(((bf16[128,5,2,128]{3,2,1,0:T(2,128)(2,1)}), bf16[128,5,2,128]{3,2,1,0:T(2,128)(2,1)S(1)}, u32[]{:S(2)}, u32[]{:S(2)}) %all-to-all-start.1) | async-done | bytes 327712 | tf_op jit(solution)/shard_map/all_to_all | solution.py:755
  83.7 1.2 %shard_map.153 = (f32[3,3,3,8,32]{4,3,2,1,0:T(8,128)}, f32[3,3,3,32,64]{4,3,2,1,0:T(8,128)}, f32[3,3,3,32,96]{4,3,2,1,0:T(8,128)}, f32[8,32]{1,0:T(8,128)}) custom-call(bf16[1280,128]{1,0:T(8,128)(2,1)S(1)} %bitcast.36), custom_call_target="tpu_custom_call" | custom-call | flops 1048576 | bytes 4194304 | tf_op jit(solution)/shard_map/pallas_call | solution.py:21
  84.9 0.8 shard_map.155
  (55 shorter events, 1.1 us)
Async XLA Ops:
  0.6 8.1 %copy-start.3 = (bf16[256,384]{1,0:T(8,128)(2,1)S(1)}, bf16[256,384]{1,0:T(8,128)(2,1)}, u32[]{:S(2)}) copy-start(bf16[256,384]{1,0:T(8,128)(2,1)} %constant.10.clone.pool_ref) | copy-start | bytes 589828
  0.6 8.1 %copy-start.7 = (bf16[8,32]{1,0:T(8,128)(2,1)S(1)}, bf16[8,32]{1,0:T(8,128)(2,1)}, u32[]{:S(2)}) copy-start(bf16[8,32]{1,0:T(8,128)(2,1)} %head_ref.1) | copy-start | bytes 1540
  0.7 8.1 %copy-start.1 = (bf16[1,8,4,24,128]{4,3,2,1,0:T(8,128)(2,1)S(1)}, bf16[1,8,4,24,128]{4,3,2,1,0:T(8,128)(2,1)}, u32[]{:S(2)}) copy-start(bf16[1,8,4,24,128]{4,3,2,1,0:T(8,128)(2,1)} %param.15) | copy-start | bytes 589828
  0.7 8.1 %copy-start = (bf16[1,32,4,24,128]{4,3,2,1,0:T(8,128)(2,1)S(1)}, bf16[1,32,4,24,128]{4,3,2,1,0:T(8,128)(2,1)}, u32[]{:S(2)}) copy-start(bf16[1,32,4,24,128]{4,3,2,1,0:T(8,128)(2,1)} %param.14) | copy-start | bytes 2359300
  0.7 8.1 %copy-start.2 = (bf16[1,32,4,24,128]{4,3,2,1,0:T(8,128)(2,1)S(1)}, bf16[1,32,4,24,128]{4,3,2,1,0:T(8,128)(2,1)}, u32[]{:S(2)}) copy-start(bf16[1,32,4,24,128]{4,3,2,1,0:T(8,128)(2,1)} %param.12) | copy-start | bytes 2359300
  0.7 8.1 %copy-start.4 = (bf16[1,8,4,24,128]{4,3,2,1,0:T(8,128)(2,1)S(1)}, bf16[1,8,4,24,128]{4,3,2,1,0:T(8,128)(2,1)}, u32[]{:S(2)}) copy-start(bf16[1,8,4,24,128]{4,3,2,1,0:T(8,128)(2,1)} %param.11) | copy-start | bytes 589828
  3.2 7.9 %collective-permute-start = (bf16[24,32,128]{2,1,0:T(8,128)(2,1)}, bf16[24,32,128]{2,1,0:T(8,128)(2,1)S(1)}, u32[]{:S(2)}, u32[]{:S(2)}) collective-permute-start(bf16[24,32,128]{2,1,0:T(8,128)(2,1)} %get-tuple-element.54.face1_ref), channel_id=1, source_target_pairs={{0,8},{16,24},{32,40},{48,56},{8,0},{24,16},{40,32},{56,48},{1,9},... | collective-permute-start | bytes 589832 | tf_op jit(solution)/shard_map/ppermute | solution.py:612
  5.7 5.5 %collective-permute-start.1 = (bf16[24,32,128]{2,1,0:T(8,128)(2,1)}, bf16[24,32,128]{2,1,0:T(8,128)(2,1)S(1)}, u32[]{:S(2)}, u32[]{:S(2)}) collective-permute-start(bf16[24,32,128]{2,1,0:T(8,128)(2,1)} %get-tuple-element.56.face2_ref), channel_id=1, source_target_pairs={{8,16},{24,32},{40,48},{16,8},{32,24},{48,40},{9,17},{25,33},{41,4... | collective-permute-start | bytes 589832 | tf_op jit(solution)/shard_map/ppermute | solution.py:612
  8.7 8.5 %copy-start.5 = (bf16[24,32,128]{2,1,0:T(8,128)(2,1)S(1)}, bf16[24,32,128]{2,1,0:T(8,128)(2,1)}, u32[]{:S(2)}) copy-start(bf16[24,32,128]{2,1,0:T(8,128)(2,1)} %get-tuple-element.54.face1_ref) | copy-start | bytes 589828
  8.8 8.5 %copy-start.6 = (bf16[24,32,128]{2,1,0:T(8,128)(2,1)S(1)}, bf16[24,32,128]{2,1,0:T(8,128)(2,1)}, u32[]{:S(2)}) copy-start(bf16[24,32,128]{2,1,0:T(8,128)(2,1)} %get-tuple-element.56.face2_ref) | copy-start | bytes 589828
  8.8 8.5 %copy-start.8 = (bf16[32,96,3,3,3]{1,0,4,3,2:T(8,128)(2,1)S(1)}, bf16[32,96,3,3,3]{1,0,4,3,2:T(8,128)(2,1)}, u32[]{:S(2)}) copy-start(bf16[32,96,3,3,3]{1,0,4,3,2:T(8,128)(2,1)} %param.18) | copy-start | bytes 497668
  8.8 8.5 %copy-start.9 = (bf16[64,32,3,3,3]{0,1,4,3,2:T(8,128)(2,1)S(1)}, bf16[64,32,3,3,3]{0,1,4,3,2:T(8,128)(2,1)}, u32[]{:S(2)}) copy-start(bf16[64,32,3,3,3]{0,1,4,3,2:T(8,128)(2,1)} %param.17) | copy-start | bytes 331780
  11.4 10.3 %collective-permute-start.3 = (bf16[672,128]{1,0:T(8,128)(2,1)S(1)}, bf16[672,128]{1,0:T(8,128)(2,1)S(1)}, u32[]{:S(2)}, u32[]{:S(2)}) collective-permute-start(bf16[672,128]{1,0:T(8,128)(2,1)S(1)} %get-tuple-element.107), channel_id=1, source_target_pairs={{1,2},{3,4},{5,6},{2,1},{4,3},{6,5},{9,10},{11,12},{13,14},{10,9},... | collective-permute-start | bytes 516104 | tf_op jit(solution)/shard_map/ppermute | solution.py:612
  12.0 9.6 %collective-permute-start.2 = (bf16[672,128]{1,0:T(8,128)(2,1)S(1)}, bf16[672,128]{1,0:T(8,128)(2,1)S(1)}, u32[]{:S(2)}, u32[]{:S(2)}) collective-permute-start(bf16[672,128]{1,0:T(8,128)(2,1)S(1)} %get-tuple-element.108), channel_id=1, source_target_pairs={{0,1},{2,3},{4,5},{6,7},{1,0},{3,2},{5,4},{7,6},{8,9},{10,11},{12,... | collective-permute-start | bytes 516104 | tf_op jit(solution)/shard_map/ppermute | solution.py:612
  23.3 12.5 %collective-permute-start.4 = (bf16[592,128]{1,0:T(8,128)(2,1)S(1)}, bf16[592,128]{1,0:T(8,128)(2,1)S(1)}, u32[]{:S(2)}, u32[]{:S(2)}) collective-permute-start(bf16[592,128]{1,0:T(8,128)(2,1)S(1)} %get-tuple-element.78), channel_id=1, source_target_pairs={{0,8},{16,24},{32,40},{48,56},{8,0},{24,16},{40,32},{56,48},{1,9},... | collective-permute-start | bytes 454664 | tf_op jit(solution)/shard_map/ppermute | solution.py:612
  30.7 5.1 %collective-permute-start.5 = (bf16[592,128]{1,0:T(8,128)(2,1)S(1)}, bf16[592,128]{1,0:T(8,128)(2,1)S(1)}, u32[]{:S(2)}, u32[]{:S(2)}) collective-permute-start(bf16[592,128]{1,0:T(8,128)(2,1)S(1)} %get-tuple-element.79), channel_id=1, source_target_pairs={{8,16},{24,32},{40,48},{16,8},{32,24},{48,40},{9,17},{25,33},{41,4... | collective-permute-start | bytes 454664 | tf_op jit(solution)/shard_map/ppermute | solution.py:612
  31.6 4.3 %copy-start.10 = (bf16[32,8,3,3,3]{0,1,4,3,2:T(8,128)(2,1)S(1)}, bf16[32,8,3,3,3]{0,1,4,3,2:T(8,128)(2,1)}, u32[]{:S(2)}) copy-start(bf16[32,8,3,3,3]{0,1,4,3,2:T(8,128)(2,1)} %param.16) | copy-start | bytes 41476
  31.6 4.3 %copy-start.11 = (bf16[256,256]{1,0:T(8,128)(2,1)S(1)}, bf16[256,256]{1,0:T(8,128)(2,1)}, u32[]{:S(2)}) copy-start(bf16[256,256]{1,0:T(8,128)(2,1)} %constant.11.clone.up_ref) | copy-start | bytes 393220
  38.6 26.9 %all-to-all-start = ((bf16[128,5,2,128]{3,2,1,0:T(2,128)(2,1)}), bf16[128,5,2,128]{3,2,1,0:T(2,128)(2,1)S(1)}, u32[]{:S(2)}, u32[]{:S(2)}) async-start(bf16[128,5,2,128]{3,2,1,0:T(2,128)(2,1)} %bitcast.21), calls=%async_computation | async-start | bytes 655360 | tf_op jit(solution)/shard_map/all_to_all | solution.py:750
  53.5 13.1 %collective-permute-start.6 = (bf16[208,128]{1,0:T(8,128)(2,1)S(1)}, bf16[208,128]{1,0:T(8,128)(2,1)S(1)}, u32[]{:S(2)}, u32[]{:S(2)}) collective-permute-start(bf16[208,128]{1,0:T(8,128)(2,1)S(1)} %get-tuple-element.87), channel_id=1, source_target_pairs={{0,8},{16,24},{32,40},{48,56},{8,0},{24,16},{40,32},{56,48},{1,9},... | collective-permute-start | bytes 159752 | tf_op jit(solution)/shard_map/ppermute | solution.py:612
  55.1 11.5 %collective-permute-start.7 = (bf16[208,128]{1,0:T(8,128)(2,1)S(1)}, bf16[208,128]{1,0:T(8,128)(2,1)S(1)}, u32[]{:S(2)}, u32[]{:S(2)}) collective-permute-start(bf16[208,128]{1,0:T(8,128)(2,1)S(1)} %get-tuple-element.88), channel_id=1, source_target_pairs={{8,16},{24,32},{40,48},{16,8},{32,24},{48,40},{9,17},{25,33},{41,4... | collective-permute-start | bytes 159752 | tf_op jit(solution)/shard_map/ppermute | solution.py:612
  66.6 17.1 %all-to-all-start.1 = ((bf16[128,5,2,128]{3,2,1,0:T(2,128)(2,1)}), bf16[128,5,2,128]{3,2,1,0:T(2,128)(2,1)S(1)}, u32[]{:S(2)}, u32[]{:S(2)}) async-start(bf16[128,5,2,128]{3,2,1,0:T(2,128)(2,1)} %bitcast.23), calls=%async_computation.1 | async-start | bytes 655360 | tf_op jit(solution)/shard_map/all_to_all | solution.py:755
  71.7 13.1 %collective-permute-start.8 = (bf16[32,128]{1,0:T(8,128)(2,1)S(1)}, bf16[32,128]{1,0:T(8,128)(2,1)S(1)}, u32[]{:S(2)}, u32[]{:S(2)}) collective-permute-start(bf16[32,128]{1,0:T(8,128)(2,1)S(1)} %get-tuple-element.95), channel_id=1, source_target_pairs={{0,1},{2,3},{4,5},{6,7},{1,0},{3,2},{5,4},{7,6},{8,9},{10,11},{12,... | collective-permute-start | bytes 24584 | tf_op jit(solution)/shard_map/ppermute | solution.py:612
  75.1 9.7 %collective-permute-start.9 = (bf16[32,128]{1,0:T(8,128)(2,1)S(1)}, bf16[32,128]{1,0:T(8,128)(2,1)S(1)}, u32[]{:S(2)}, u32[]{:S(2)}) collective-permute-start(bf16[32,128]{1,0:T(8,128)(2,1)S(1)} %get-tuple-element.96), channel_id=1, source_target_pairs={{1,2},{3,4},{5,6},{2,1},{4,3},{6,5},{9,10},{11,12},{13,14},{10,9},... | collective-permute-start | bytes 24584 | tf_op jit(solution)/shard_map/ppermute | solution.py:612
